TPU v7x, 256 devices: a whole 4x4x8 slice. The times are simulated.
256 devices in a mesh: seq: 4 (over z_lo), row: 8 (over x, core), col: 8 (over y, z_hi).
Axes of the slice: x: 4, y: 4, z: 8 (z_hi: 2, z_lo: 4; z = z_hi * 4 + z_lo), core: 2. Of those that a mesh axis runs over, the one named last changes fastest.
Arguments:
- layernormed_alignment: bfloat16 [128, 1536, 64], P('seq', 'row'), may hold values from -6 to 6
- average_cotangent: bfloat16 [128, 1536, 64], P('seq', 'row'), may hold values from -6 to 6
- sequence_validity: int32 [128, 1536], P('seq', 'row'), may hold values 0 or 1
- residue_validity: int32 [1536], replicated, may hold values 0 or 1
- pair_scores: float32 [8, 1536, 1536], P(None, 'row', 'col'), may hold values from -12 to 280
- payload_projection: bfloat16 [64, 256], replicated, may hold values from -0.75 to 0.75
- sigmoid_projection: bfloat16 [64, 256], replicated, may hold values from -0.75 to 0.75
- final_projection: bfloat16 [256, 64], replicated, may hold values from -0.375 to 0.375
Outputs:
- alignment_cotangent: float32 [128, 1536, 64], P('seq', ('row', 'col'))
- score_cotangent: float32 [8, 1536, 1536], P('seq', 'row', 'col')
All inputs are finite; a program needn't handle non-finite values. No bound on the sum of `sequence_validity` on one device may be relied on, other than what follows from the above.
Results may differ from a plain program's by a relative error of at most 0.0041.
Values may be sent and summed in bfloat16 or wider, within the bound.
No kernel may reach another device: no remote copies, remote signals or barrier semaphores. Data moves between devices by JAX's collectives and lax.ppermute only.
A program may use at most 128 MiB of HBM per device.

v0:
```python
import jax
import jax.numpy as jnp
from jax import lax
from jax.sharding import PartitionSpec as P


def body(
    layernormed_alignment,
    average_cotangent,
    sequence_validity,
    residue_validity,
    pair_scores,
    payload_projection,
    sigmoid_projection,
    final_projection,
):
    row_count = lax.axis_size("row")
    seq_count = lax.axis_size("seq")
    row_pos = lax.axis_index("row")
    column_position = lax.axis_index("col")
    seq_pos = lax.axis_index("seq")
    shard_sequences = layernormed_alignment.shape[0]
    sequence_stretch = layernormed_alignment.shape[1]
    feature_extent = layernormed_alignment.shape[2]
    heads = pair_scores.shape[0]
    block_columns = pair_scores.shape[2]
    head_dim = payload_projection.shape[1] // heads
    residues_complete = lax.all_gather(layernormed_alignment, "row", axis=1, tiled=True)
    residue_alignment_part = lax.dynamic_slice_in_dim(
        residues_complete, column_position * block_columns, block_columns, 1
    )
    values_per_column = jnp.dot(
        residue_alignment_part.reshape(-1, feature_extent),
        payload_projection,
        preferred_element_type=jnp.float32,
    )
    values_per_column = values_per_column.astype(jnp.bfloat16).reshape(
        shard_sequences, block_columns, heads, head_dim
    )
    sequence_merged = layernormed_alignment.reshape(-1, feature_extent)
    gate_act = jax.nn.sigmoid(
        jnp.dot(sequence_merged, sigmoid_projection, preferred_element_type=jnp.float32)
    )
    projection_cotangent = jnp.dot(
        average_cotangent.reshape(-1, feature_extent),
        final_projection.T,
        preferred_element_type=jnp.float32,
    )
    kept_sequences = sequence_validity.reshape(-1, 1).astype(jnp.float32)
    d_att = (
        (projection_cotangent * gate_act * kept_sequences)
        .astype(jnp.bfloat16)
        .reshape(shard_sequences, sequence_stretch, heads, head_dim)
    )
    gate_term = (projection_cotangent * kept_sequences * gate_act * (1.0 - gate_act)).reshape(
        shard_sequences, sequence_stretch, heads, head_dim
    )
    keep_cols = (
        lax.dynamic_slice_in_dim(
            residue_validity, column_position * block_columns, block_columns, 0
        )
        > 0
    )
    masked = jnp.where(keep_cols[None, None, :], pair_scores, jnp.float32(-1000000000.0))
    peak = lax.pmax(jnp.max(masked, axis=2), "col")
    expon = jnp.exp(masked - peak[:, :, None])
    denom = lax.psum(jnp.sum(expon, axis=2), "col")
    weights = expon / denom[:, :, None]
    weights_b = weights.astype(jnp.bfloat16)
    average = jnp.einsum(
        "hij,sjhc->sihc", weights_b, values_per_column, preferred_element_type=jnp.float32
    )
    payload_cotangent = jnp.einsum(
        "hij,sihc->sjhc", weights_b, d_att, preferred_element_type=jnp.float32
    )
    heads_mine = heads // seq_count
    d_weights = jnp.einsum(
        "sihc,sjhc->hij", d_att, values_per_column, preferred_element_type=jnp.float32
    )
    totals = lax.psum(d_weights, "seq")
    mine = lax.dynamic_slice_in_dim(totals, seq_pos * heads_mine, heads_mine, 0)
    weights_mine = lax.dynamic_slice_in_dim(weights, seq_pos * heads_mine, heads_mine, 0)
    inner = lax.psum(jnp.sum(weights_mine * mine, axis=2), "col")
    score_cotangent = weights_mine * (mine - inner[:, :, None])
    gate_flat = (gate_term * average).reshape(-1, heads * head_dim)
    row_term = jnp.dot(
        gate_flat, sigmoid_projection.astype(jnp.float32).T, precision=lax.Precision.HIGHEST
    )
    row_term = row_term.reshape(shard_sequences, sequence_stretch, feature_extent)
    col_term = jnp.dot(
        payload_cotangent.reshape(-1, heads * head_dim),
        payload_projection.astype(jnp.float32).T,
        precision=lax.Precision.HIGHEST,
    )
    col_term = col_term.reshape(shard_sequences, block_columns, feature_extent)
    split_attenders = jnp.zeros(
        (shard_sequences, sequence_stretch * row_count, feature_extent), jnp.float32
    )
    split_attenders = lax.dynamic_update_slice_in_dim(
        split_attenders, row_term, row_pos * sequence_stretch, 1
    )
    split_attenders = split_attenders + lax.dynamic_update_slice_in_dim(
        jnp.zeros_like(split_attenders), col_term, column_position * block_columns, 1
    )
    alignment_cotangent = lax.psum_scatter(
        split_attenders, ("row", "col"), scatter_dimension=1, tiled=True
    )
    return (alignment_cotangent, score_cotangent)


def solution(mesh):
    return jax.shard_map(
        body,
        mesh=mesh,
        in_specs=(
            P("seq", "row", None),
            P("seq", "row", None),
            P("seq", "row"),
            P(),
            P(None, "row", "col"),
            P(),
            P(),
            P(),
        ),
        out_specs=(P("seq", ("row", "col"), None), P("seq", "row", "col")),
        check_vma=False,
    )
```

profile of v0, /device:TPU:2, one launch (start us, length us, event | category | flops | bytes accessed | tf_op | source)
XLA Modules:
  0.0 552.6 jit_solution(10936830736147795902)
XLA Ops:
  7.2 0.0 copy-start
  7.2 0.0 all-gather.2.cloned.1.call-start
  7.3 3.3 copy.33
  10.5 0.0 all-gather.2.cloned.1.call-update
  10.6 0.0 all-reduce.2.cloned.1.call-start
  10.6 0.6 copy.31
  11.3 0.1 convert_element_type.23
  11.3 0.6 copy.30
  11.9 2.1 reshape.43
  14.0 1.1 reshape.44
  15.1 1.8 fusion.2
  17.0 4.3 multiply_convert_fusion
  21.3 3.1 copy.40
  24.4 8.3 %reshape.48 = bf16[32,192,8,32]{1,0,3,2:T(8,128)(2,1)} reshape(bf16[6144,256]{0,1:T(8,128)(2,1)} %copy.40) | data formatting | bytes 6291456 | tf_op jit(solution)/shard_map/reshape | solution.py:53
  32.7 0.8 dynamic-slice_compare_fusion
  33.5 0.3 select_reduce_fusion
  33.8 33.8 %pmax.7 = f32[8,192]{1,0:T(8,128)S(1)} all-reduce(f32[8,192]{1,0:T(8,128)S(1)} %select_reduce_fusion), channel_id=1, replica_groups=mesh['seq'=4,'row'=8,'col'=8] {'col'}, use_global_device_ids=true, to_apply=%region_1.2 | all-reduce | flops 1536 | bytes 12288 | tf_op jit(solution)/shard_map/pmax | solution.py:65
  67.7 0.7 fusion.13
  68.4 24.7 %psum.21 = f32[8,192]{1,0:T(8,128)S(1)} all-reduce(f32[8,192]{1,0:T(8,128)S(1)} %fusion.13), channel_id=1, replica_groups=mesh['seq'=4,'row'=8,'col'=8] {'col'}, use_global_device_ids=true, to_apply=%region_3.4 | all-reduce | flops 1536 | bytes 12288 | tf_op jit(solution)/shard_map/psum | solution.py:67
  93.1 0.5 fusion.12
  93.6 5.1 fusion.9
  98.7 4.1 copy.42
  102.8 6.6 %copy.32 = f32[6144,256]{0,1:T(8,128)} copy(f32[6144,256]{1,0:T(8,128)} %get-tuple-element.9) | data formatting | bytes 12582912 | tf_op jit(solution)/shard_map/mul | solution.py:55
  109.3 9.2 %reshape.45 = f32[32,192,8,32]{1,0,3,2:T(8,128)} reshape(f32[6144,256]{0,1:T(8,128)} %copy.32) | data formatting | bytes 12582912 | tf_op jit(solution)/shard_map/reshape | solution.py:55
  118.6 1.7 constant_dynamic-slice_fusion
  120.3 3.2 copy.34
  123.5 2.2 reshape.46
  125.7 2.7 convolution_convert_fusion
  128.3 4.7 copy.35
  133.0 8.0 %reshape.47 = bf16[32,192,8,32]{1,0,3,2:T(8,128)(2,1)} reshape(bf16[6144,256]{0,1:T(8,128)(2,1)} %copy.35) | data formatting | bytes 6291456 | tf_op jit(solution)/shard_map/reshape | solution.py:37
  141.1 5.9 %convolution_bitcast_fusion = f32[8,192,192]{2,1,0:T(8,128)} fusion(bf16[32,192,8,32]{1,0,3,2:T(8,128)(2,1)} %reshape.48, bf16[32,192,8,32]{1,0,3,2:T(8,128)(2,1)} %reshape.47), kind=kOutput, calls=%fused_computation.15 | convolution fusion | flops 603979776 | bytes 7471104 | tf_op jit(solution)/shard_map/sihc,sjhc->hij/dot_general | solution.py:77
  147.0 0.0 all-reduce.2.cloned.1.call-update
  147.0 0.2 reduce-scatter.2.cloned.1.call-start
  147.2 13.7 %bitcast_multiply_fusion = f32[32,192,8,32]{1,3,0,2:T(8,128)S(1)} fusion(f32[32,192,8,32]{1,0,3,2:T(8,128)} %reshape.45, bf16[32,192,8,32]{1,0,3,2:T(8,128)(2,1)} %reshape.47, f32[8,192,192]{2,1,0:T(8,128)S(1)} %fusion.12), kind=kOutput, calls=%fused_computation | convolution fusion | flops 605847552 | bytes 16908288 | tf_op jit(solution)/shard_map/hij,sjhc->sihc/dot_general | solution.py:70
  160.9 1.7 copy.38
  162.6 5.1 fusion.19
  167.7 6.2 %broadcast.10 = f32[32,1536,64]{1,2,0:T(8,128)} broadcast(f32[]{:T(128)} %constant.12.clone.1), dimensions={} | broadcast | bytes 12582916 | tf_op jit(solution)/shard_map/broadcast.2
  173.9 11.1 %dynamic_update_slice.8 = f32[32,1536,64]{1,2,0:T(8,128)} dynamic-update-slice(f32[32,1536,64]{1,2,0:T(8,128)} %broadcast.10, f32[32,192,64]{1,2,0:T(8,128)} %fusion.19, s32[]{:T(128)} %constant.14.clone.1, s32[]{:T(128)S(6)} %select_n.18, s32[]{:T(128)} %constant.14.clone.1) | dynamic-update-slice | bytes 3145732 | tf_op jit(solution)/shard_map/dynamic_update_slice | solution.py:99
  184.9 9.0 %dynamic-slice_add_fusion = f32[32,192,64]{1,2,0:T(8,128)} fusion(f32[32,1536,64]{1,2,0:T(8,128)} %dynamic_update_slice.8, s32[]{:T(128)S(6)} %select_n.16, f32[32,192,256]{1,2,0:T(8,128)} %bitcast.45, bf16[64,256]{1,0:T(8,128)(2,1)S(1)} %copy-done.6), kind=kOutput, calls=%fused_computation.13 | convolution fusion | flops 1208352768 | bytes 9469956 | tf_op jit(solution)/shard_map/dot_general | solution.py:90
  194.0 11.1 %add.30 = f32[32,1536,64]{1,2,0:T(8,128)} dynamic-update-slice(f32[32,1536,64]{1,2,0:T(8,128)} %dynamic_update_slice.8, f32[32,192,64]{1,2,0:T(8,128)} %dynamic-slice_add_fusion, s32[]{:T(128)} %constant.14.clone.1, s32[]{:T(128)S(6)} %select_n.16, s32[]{:T(128)} %constant.14.clone.1) | dynamic-update-slice | bytes 3145732 | tf_op jit(solution)/shard_map/add | solution.py:102
  205.0 23.4 %copy.44 = f32[32,1536,64]{2,0,1:T(8,128)} copy(f32[32,1536,64]{1,2,0:T(8,128)} %add.30) | data formatting | bytes 25165824 | tf_op jit(solution)/shard_map/add | solution.py:102
  228.4 0.0 reduce-scatter.2.cloned.1.call-update
  228.4 0.0 all-reduce.2.cloned.1.call-done
  228.4 1.2 multiply_reduce_fusion
  229.6 32.5 %psum.23 = f32[2,192]{1,0:T(2,128)S(1)} all-reduce(f32[2,192]{1,0:T(2,128)S(1)} %multiply_reduce_fusion), channel_id=1, replica_groups=mesh['seq'=4,'row'=8,'col'=8] {'col'}, use_global_device_ids=true, to_apply=%region_7.8 | all-reduce | flops 384 | bytes 3072 | tf_op jit(solution)/shard_map/psum | solution.py:83
  262.1 1.9 subtract_multiply_fusion.1
  264.0 279.9 %reduce-scatter.2.cloned.1.call-done = f32[32,24,64]{2,0,1:T(8,128)} async-done(((f32[32,1536,64]{2,0,1:T(8,128)}), f32[32,24,64]{2,0,1:T(8,128)}) %reduce-scatter.2.cloned.1.call-update) | async-done | bytes 196624 | tf_op jit(solution)/shard_map/reduce_scatter | solution.py:105
  543.8 2.0 copy.45
  (19 shorter events, 0.0 us)
Async XLA Ops:
  7.2 9.8 %copy-start = (bf16[256,64]{0,1:T(8,128)(2,1)S(1)}, bf16[256,64]{0,1:T(8,128)(2,1)}, u32[]{:S(2)}) copy-start(bf16[256,64]{0,1:T(8,128)(2,1)} %param.15) | copy-start | bytes 98308
  7.2 3.5 copy-start.3
  7.2 4.0 copy-start.8
  7.2 4.1 copy-start.5
  7.2 111.4 %all-gather.2.cloned.1.call-start = ((), (), s32[]{:S(2)}) async-start(), calls=%async_computation.1 | async-start | bytes 14155776 | tf_op jit(solution)/shard_map/all_gather | solution.py:28
  10.6 4.6 copy-start.7
  10.6 217.9 %all-reduce.2.cloned.1.call-start = ((), (), s32[]{:S(2)}) async-start(), calls=%async_computation.3 | async-start | bytes 3145728 | tf_op jit(solution)/shard_map/psum | solution.py:80
  15.1 1.9 copy-start.4
  24.4 9.1 %copy-start.2 = (f32[8,192,192]{2,1,0:T(8,128)S(1)}, f32[8,192,192]{2,1,0:T(8,128)}, u32[]{:S(2)}) copy-start(f32[8,192,192]{2,1,0:T(8,128)} %param.12) | copy-start | bytes 3538948
  118.6 7.1 %copy-start.6 = (bf16[64,256]{1,0:T(8,128)(2,1)S(1)}, bf16[64,256]{1,0:T(8,128)(2,1)}, u32[]{:S(2)}) copy-start(bf16[64,256]{1,0:T(8,128)(2,1)} %param.13) | copy-start | bytes 98308
  147.0 396.8 %reduce-scatter.2.cloned.1.call-start = ((), (), s32[]{:S(2)}) async-start(), calls=%async_computation.2 | async-start | bytes 25559040 | tf_op jit(solution)/shard_map/reduce_scatter | solution.py:105
  228.4 317.4 %copy-start.1 = (bf16[256,64]{0,1:T(8,128)(2,1)S(1)}, bf16[256,64]{0,1:T(8,128)(2,1)}, u32[]{:S(2)}) copy-start(bf16[256,64]{0,1:T(8,128)(2,1)} %param.15) | copy-start | bytes 98308
Sparse Core Ops, SparseCore 0:
  10.7 72.2 all-gather.1
  147.1 79.6 all-reduce.1
  233.3 310.5 reduce-scatter.1
where the time goes:
time: 562 us; the launch traced here: 553 us
  waiting for transfers between devices  280 us (50%)
  local copies, waits for them, and re-layouts  114 us (20%)
  blocking collectives  91 us (16%)
  matrix products  47.7 us (8%)
  between operations  14.2 us (3%)
    reduce_scatter x1, waiting for transfers between devices, body(): lax.psum_scatter(split_attenders, ('row', 'col'), scatter_dimension=1, ti...  280 us
    add x2, local copies, waits for them, and re-layouts, body(): split_attenders + lax.dynamic_update_slice_in_dim(jnp.zeros_like(split_at...  34.4 us
    pmax x1, blocking collectives, body(): peak = lax.pmax(jnp.max(masked, axis=2), 'col')  33.8 us
    psum x1, blocking collectives, body(): inner = lax.psum(jnp.sum(weights_mine * mine, axis=2), 'col')  32.5 us
    psum x1, blocking collectives, body(): denom = lax.psum(jnp.sum(expon, axis=2), 'col')  24.7 us
    dot_general x1, matrix products, body(): jnp.einsum('hij,sjhc->sihc', weights_b, values_per_column, preferred_elem...  13.7 us
  transfers between devices with their start and end apart: 3, of which 1 were waited for; matrix products, arithmetic and copies ran while one was open for 24% of the time, Pallas kernels for 0%

commit v1 on v0

v1 whole, which is shorter than its diff:
```python
import jax
import jax.numpy as jnp
from jax import lax
from jax.experimental import pallas as pl
from jax.experimental.pallas import tpu as pltpu
from jax.sharding import PartitionSpec as P

F32 = jnp.float32
BF16 = jnp.bfloat16
MASKED = -1000000000.0
VMEM_BYTES = 24 * 1024 * 1024
STEPS = 4


def call(kernel, outs, inputs, in_specs=None, out_specs=None, grid=None, scratch=(), scalars=None, flops=0, moved=0):
    local = lambda: pl.BlockSpec(memory_space=pltpu.VMEM)
    several = isinstance(outs, list)
    operands = [] if scalars is None else [scalars]
    if in_specs is None:
        in_specs = [local() for _ in inputs]
    if out_specs is None:
        out_specs = [local() for _ in outs] if several else local()
    extra = {} if grid is None else {"grid": grid}
    return pl.pallas_call(
        kernel,
        out_shape=outs,
        in_specs=[pl.BlockSpec(memory_space=pltpu.SMEM)] * len(operands) + in_specs,
        out_specs=out_specs,
        scratch_shapes=list(scratch),
        compiler_params=pltpu.CompilerParams(vmem_limit_bytes=VMEM_BYTES),
        cost_estimate=pl.CostEstimate(flops=flops, bytes_accessed=moved, transcendentals=0),
        **extra,
    )(*operands, *inputs)


def whole(shape):
    return pl.BlockSpec(shape, lambda i: (0,) * len(shape))


def by_step(*dims):
    return pl.BlockSpec(dims, lambda i: (i,) + (0,) * (len(dims) - 1))


def far(a):
    return pltpu.with_memory_space_constraint(a, pltpu.HBM)


def dot(a, b):
    return jnp.dot(a, b, preferred_element_type=F32)


def turned(a):
    return a.astype(F32).T.astype(a.dtype)


def open_kernel(x_ref, scores_ref, keep_ref, out_ref, stats_ref):
    sequences = x_ref.shape[0]
    half = sequences // 2
    out_ref[0:sequences] = x_ref[:, :, 0:128]
    out_ref[sequences:] = jnp.concatenate([x_ref[0:half, :, 128:192], x_ref[half:, :, 128:192]], axis=-1)
    heads, rows, _ = scores_ref.shape
    keep = keep_ref[...] > 0
    lane = lax.broadcasted_iota(jnp.int32, (rows, 128), 1)
    table = jnp.zeros((rows, 128), F32)
    for h in range(heads):
        masked = jnp.where(keep, scores_ref[h], MASKED)
        peak = jnp.max(masked, axis=1, keepdims=True)
        total = jnp.sum(jnp.exp(masked - peak), axis=1, keepdims=True)
        table = jnp.where(lane == h, peak, table)
        table = jnp.where(lane == heads + h, total, table)
    packed = table.T[0 : 2 * heads]
    for k in range(stats_ref.shape[0]):
        stats_ref[k] = packed


def gate_kernel(x_ref, cot_ref, mask_ref, gate_w_ref, final_w_ref, att_ref, term_ref, att_rows_ref, wt):
    @pl.when(pl.program_id(0) == 0)
    def _():
        wt[0] = turned(gate_w_ref[...])
        wt[1] = turned(final_w_ref[...])

    sequences, _, rows = x_ref.shape
    heads = att_rows_ref.shape[0]
    dim = wt.shape[1] // heads
    mask = mask_ref[...].astype(F32)
    for s in range(sequences):
        gate = 1.0 / (1.0 + jnp.exp(-dot(wt[0], x_ref[s])))
        cot = dot(wt[1], cot_ref[s]) * mask[s : s + 1]
        att = cot * gate
        att_ref[s] = att.astype(BF16)
        term_ref[s] = att * (1.0 - gate)
    for h in range(heads):
        block = att_ref[:, h * dim : (h + 1) * dim, :].reshape(sequences * dim, rows)
        att_rows_ref[h] = turned(block)


def project_rows(weight, hi, lo, out_ref, first=None):
    sequences = hi.shape[0]
    chunks, stretch, _ = out_ref.shape
    features = weight.shape[0]
    for s in range(0, sequences, 2):
        pair = [dot(weight, hi[s + k]) + dot(weight, lo[s + k]) for k in (0, 1)]
        wide = jnp.concatenate(pair, axis=0).T.reshape(chunks, stretch, 2 * features).astype(out_ref.dtype)
        if first is None:
            out_ref[:, :, s * features : (s + 2) * features] = wide
        else:
            out_ref[:, :, pl.ds(pl.multiple_of((first + s) * features, 128), 2 * features)] = wide


def split(grad, hi, lo, h, dim):
    top = grad.astype(BF16)
    hi[:, h * dim : (h + 1) * dim, :] = top
    lo[:, h * dim : (h + 1) * dim, :] = (grad - top.astype(F32)).astype(BF16)


def column_kernel(
    scores_ref, keep_ref, stats_ref, att_ref, payload_ref, weights_ref, turned_ref, out_ref, wb, hi, lo
):
    heads, rows, columns = scores_ref.shape
    sequences, width, _ = att_ref.shape
    dim = width // heads

    @pl.when(pl.program_id(0) == 0)
    def _():
        peaks = stats_ref[:, 0:heads]
        peak = jnp.max(peaks, axis=0)
        total = jnp.sum(stats_ref[:, heads : 2 * heads] * jnp.exp(peaks - peak[None]), axis=0)
        table = jnp.concatenate([peak, 1.0 / total, jnp.zeros((128 - 2 * heads, rows), F32)], axis=0).T
        keep = keep_ref[...] > 0
        for h in range(heads):
            masked = jnp.where(keep, scores_ref[h], MASKED)
            weights = jnp.exp(masked - table[:, h : h + 1]) * table[:, heads + h : heads + h + 1]
            weights_ref[h] = weights
            wb[h] = weights.astype(BF16)
            turned_ref[h] = weights.T.astype(BF16)

    for h in range(heads):
        block = att_ref[:, h * dim : (h + 1) * dim, :].reshape(sequences * dim, rows)
        split(dot(block, wb[h]).reshape(sequences, dim, columns), hi, lo, h, dim)
    project_rows(payload_ref[...], hi, lo, out_ref)


def row_kernel(
    place_ref,
    mine_ref,
    other_ref,
    payload_ref,
    gate_w_ref,
    turned_ref,
    weights_ref,
    term_ref,
    att_rows_ref,
    inner_ref,
    row0_ref,
    row1_ref,
    row2_ref,
    row3_ref,
    pair0_ref,
    pair1_ref,
    pair2_ref,
    pair3_ref,
    wt,
    values,
    hi,
    lo,
    row_out,
    pair_sum,
    pair_out,
):
    step = pl.program_id(0)
    group, width, rows = term_ref.shape
    heads, columns, _ = turned_ref.shape
    dim = width // heads
    sequences = mine_ref.shape[0] * 2 // 3
    half = sequences // 2

    @pl.when(step == 0)
    def _():
        wt[...] = turned(payload_ref[...])
        pair_sum[...] = jnp.zeros(pair_sum.shape, F32)

    first = pl.multiple_of(step * group, group)
    late = first >= half
    shared = sequences + first - jnp.where(late, half, 0)
    own = place_ref[0] == place_ref[1]
    main = jnp.where(own, mine_ref[pl.ds(first, group)], other_ref[pl.ds(first, group)])
    tail = jnp.where(own, mine_ref[pl.ds(shared, group)], other_ref[pl.ds(shared, group)])
    tail = jnp.where(late, tail[:, :, 64:128], tail[:, :, 0:64])
    for k in range(group):
        tokens = jnp.concatenate([main[k], tail[k]], axis=-1)
        values[k] = dot(wt[...], tokens).astype(BF16)
    for h in range(heads):
        block = values[:, h * dim : (h + 1) * dim, :].reshape(group * dim, columns)
        average = dot(block, turned_ref[h]).reshape(group, dim, rows)
        split(average * term_ref[:, h * dim : (h + 1) * dim, :], hi, lo, h, dim)
        pair_sum[h] += dot(att_rows_ref[h], block)
    project_rows(gate_w_ref[...], hi, lo, row_out, first)

    @pl.when(step == pl.num_programs(0) - 1)
    def _():
        for k, out_ref in enumerate((row0_ref, row1_ref, row2_ref, row3_ref)):
            out_ref[...] = row_out[pl.ds(2 * (place_ref[2] ^ k), 2)]
        lane = lax.broadcasted_iota(jnp.int32, (rows, 128), 1)
        table = jnp.zeros((rows, 128), F32)
        owners = pair_out.shape[0]
        own_heads = heads // owners
        for k in range(owners):
            tails = []
            for g in range(own_heads):
                h = k * own_heads + g
                grad = pair_sum[h].astype(BF16)
                pair_out[k, g] = grad[:, 0:128]
                tails.append(grad[:, 128:192])
                inner = jnp.sum(weights_ref[h] * grad.astype(F32), axis=1, keepdims=True)
                table = jnp.where(lane == h, inner, table)
            pair_out[k, own_heads] = jnp.concatenate(tails, axis=-1)
        inner_ref[...] = table.T[0:heads]
        for k, out_ref in enumerate((pair0_ref, pair1_ref, pair2_ref, pair3_ref)):
            out_ref[...] = pair_out[place_ref[3] ^ k]


def score_kernel(
    place_ref,
    part0_ref,
    part1_ref,
    part2_ref,
    part3_ref,
    inner0_ref,
    inner1_ref,
    inner2_ref,
    inner3_ref,
    weights_ref,
    out_ref,
):
    heads, rows, _ = out_ref.shape
    total = part0_ref[...].astype(F32)
    for part in (part1_ref, part2_ref, part3_ref):
        total = total + part[...].astype(F32)
    inner = (inner0_ref[...] + inner1_ref[...]) + (inner2_ref[...] + inner3_ref[...])
    table = jnp.concatenate([inner, jnp.zeros((128 - inner.shape[0], rows), F32)], axis=0).T
    lane = lax.broadcasted_iota(jnp.int32, table.shape, 1)
    for h in range(heads):
        mine = place_ref[3] * heads + h
        grad = jnp.concatenate([total[h], total[heads][:, 64 * h : 64 * h + 64]], axis=-1)
        own = jnp.sum(jnp.where(lane == mine, table, 0.0), axis=1, keepdims=True)
        out_ref[h] = weights_ref[mine] * (grad - own)


def fold_kernel(place_ref, part0_ref, part1_ref, part2_ref, part3_ref, cols_ref, keep_ref, send_ref):
    total = part0_ref[...].astype(F32)
    for part in (part1_ref, part2_ref, part3_ref):
        total = total + part[...].astype(F32)
    high = place_ref[1] == 1
    keep_ref[...] = jnp.where(high, total[1], total[0]) + cols_ref[...].astype(F32)
    send_ref[...] = jnp.where(high, total[0], total[1]).astype(BF16)


def join_kernel(keep_ref, rows_ref, out_ref):
    sequences, _, features = out_ref.shape
    total = keep_ref[...] + rows_ref[...].astype(F32)
    for s in range(sequences):
        out_ref[s] = total[:, s * features : (s + 1) * features]


def body(
    layernormed_alignment,
    average_cotangent,
    sequence_validity,
    residue_validity,
    pair_scores,
    payload_projection,
    sigmoid_projection,
    final_projection,
):
    row_count = lax.axis_size("row")
    col_count = lax.axis_size("col")
    seq_count = lax.axis_size("seq")
    row_pos = lax.axis_index("row")
    col_pos = lax.axis_index("col")
    seq_pos = lax.axis_index("seq")
    sequences, rows, features = layernormed_alignment.shape
    heads, _, columns = pair_scores.shape
    width = payload_projection.shape[1]
    dim = width // heads
    stretch = rows // col_count
    wide = sequences * features
    own = heads // seq_count
    group = sequences // STEPS
    side = row_count // 2
    core, plane, across = row_pos % 2, col_pos % 2, col_pos // 2
    place = jnp.stack([core, plane, across, seq_pos]).astype(jnp.int32)

    tokens = far(jnp.swapaxes(layernormed_alignment, 1, 2))
    cotangent = far(jnp.swapaxes(average_cotangent, 1, 2))
    scores = far(pair_scores)
    payload_w = far(payload_projection)
    gate_w = far(sigmoid_projection)
    final_w = far(final_projection.T)
    keep = lax.dynamic_slice_in_dim(residue_validity, col_pos * columns, columns, 0).reshape(1, columns)

    packed, stats = call(
        open_kernel,
        [
            jax.ShapeDtypeStruct((sequences * 3 // 2, features, 128), BF16),
            jax.ShapeDtypeStruct((col_count, 2 * heads, rows), F32),
        ],
        [tokens, scores, keep],
        moved=4 << 20,
    )
    stats = lax.all_to_all(stats, "col", 0, 0, tiled=True)

    at = lambda x, core, y, z: (x * 2 + core) * col_count + y * 2 + z
    routes = [
        (at(a, z, b, z), at((b + 2 * a) % side, z, a, z))
        for a in range(side)
        for b in range(side)
        for z in range(2)
    ]
    mine = lax.ppermute(packed, ("row", "col"), routes)

    d_att, gate_term, att_rows = call(
        gate_kernel,
        [
            pltpu.HBM((sequences, width, rows), BF16),
            pltpu.HBM((sequences, width, rows), F32),
            pltpu.HBM((heads, rows, sequences * dim), BF16),
        ],
        [tokens, cotangent, far(sequence_validity), gate_w, final_w],
        [
            by_step(group, features, rows),
            by_step(group, features, rows),
            by_step(group, rows),
            whole((features, width)),
            whole((features, width)),
        ],
        [
            by_step(group, width, rows),
            by_step(group, width, rows),
            pl.BlockSpec((heads, rows, group * dim), lambda i: (0, 0, i)),
        ],
        grid=(STEPS,),
        scratch=[pltpu.VMEM((2, width, features), BF16)],
        flops=1 << 30,
        moved=14 << 20,
    )
    mine, stats, d_att = lax.optimization_barrier((mine, stats, d_att))
    other = lax.ppermute(mine, "row", [(i, i ^ 1) for i in range(row_count)])

    pieces = [pltpu.VMEM((group, width, rows), BF16)] * 2
    weights, weights_turned, col_term = call(
        column_kernel,
        [
            pltpu.HBM((heads, rows, columns), F32),
            pltpu.HBM((heads, columns, rows), BF16),
            jax.ShapeDtypeStruct((row_count, stretch, wide), BF16),
        ],
        [scores, keep, stats, far(d_att), payload_w],
        [
            whole(pair_scores.shape),
            whole((1, columns)),
            whole((col_count, 2 * heads, rows)),
            by_step(group, width, rows),
            whole((features, width)),
        ],
        [
            whole((heads, rows, columns)),
            whole((heads, columns, rows)),
            pl.BlockSpec((row_count, stretch, group * features), lambda i: (0, 0, i)),
        ],
        grid=(STEPS,),
        scratch=[pltpu.VMEM((heads, rows, columns), BF16)] + pieces,
        flops=1 << 30,
        moved=14 << 20,
    )
    weights, weights_turned = far(weights), far(weights_turned)
    col_term = lax.all_to_all(col_term, "row", 0, 0, tiled=True)
    col_term = jnp.sum(col_term.astype(F32), axis=0).astype(BF16)
    col_term = lax.ppermute(
        col_term,
        ("row", "col"),
        [(r * col_count + c, c * col_count + r) for r in range(row_count) for c in range(col_count)],
    )

    packed_shape = (sequences * 3 // 2, features, 128)
    inner, *sent = call(
        row_kernel,
        [jax.ShapeDtypeStruct((heads, rows), F32)]
        + [jax.ShapeDtypeStruct((2, stretch, wide), BF16)] * side
        + [jax.ShapeDtypeStruct((own + 1, rows, 128), BF16)] * seq_count,
        [mine, other, payload_w, gate_w, weights_turned, weights, far(gate_term), far(att_rows)],
        [
            whole(packed_shape),
            whole(packed_shape),
            whole((features, width)),
            whole((features, width)),
            whole((heads, columns, rows)),
            whole((heads, rows, columns)),
            by_step(group, width, rows),
            pl.BlockSpec((heads, rows, group * dim), lambda i: (0, 0, i)),
        ],
        [whole((heads, rows))]
        + [whole((2, stretch, wide)) for _ in range(side)]
        + [whole((own + 1, rows, 128)) for _ in range(seq_count)],
        grid=(STEPS,),
        scratch=[pltpu.VMEM((width, features), BF16), pltpu.VMEM((group, width, columns), BF16)]
        + pieces
        + [
            pltpu.VMEM((col_count, stretch, wide), BF16),
            pltpu.VMEM((heads, rows, columns), F32),
            pltpu.VMEM((seq_count, own + 1, rows, 128), BF16),
        ],
        scalars=place,
        flops=1 << 30,
        moved=18 << 20,
    )
    row_term, d_weights = sent[:side], sent[side:]

    def swapped(a, axis, bits):
        return lax.ppermute(a, axis, [(i, i ^ bits) for i in range(lax.axis_size(axis))])

    inner = inner + sum(swapped(inner, "col", 2 * k) for k in range(1, side))
    row_term = row_term[:1] + [swapped(row_term[k], "col", 2 * k) for k in range(1, side)]
    d_weights = d_weights[:1] + [swapped(d_weights[k], "seq", k) for k in range(1, seq_count)]
    row_keep, row_send = call(
        fold_kernel,
        [jax.ShapeDtypeStruct((stretch, wide), F32), jax.ShapeDtypeStruct((stretch, wide), BF16)],
        row_term + [col_term],
        scalars=place,
        moved=2 << 20,
    )
    inner = inner + swapped(inner, "col", 1)
    row_send = swapped(row_send, "col", 1)
    inner, *d_weights = lax.optimization_barrier((inner, *d_weights))
    inners = [inner] + [swapped(inner, "seq", k) for k in range(1, seq_count)]
    score_cotangent = call(
        score_kernel,
        jax.ShapeDtypeStruct((own, rows, columns), F32),
        d_weights + inners + [weights],
        scalars=place,
        moved=2 << 20,
    )

    alignment_cotangent = call(
        join_kernel,
        jax.ShapeDtypeStruct((sequences, stretch, features), F32),
        [row_keep, row_send],
        moved=2 << 20,
    )
    return (alignment_cotangent, score_cotangent)


def solution(mesh):
    return jax.shard_map(
        body,
        mesh=mesh,
        in_specs=(
            P("seq", "row", None),
            P("seq", "row", None),
            P("seq", "row"),
            P(),
            P(None, "row", "col"),
            P(),
            P(),
            P(),
        ),
        out_specs=(P("seq", ("row", "col"), None), P("seq", "row", "col")),
        check_vma=False,
    )
```

time: 562 us -> 105 us (0.19); the launches traced: 553 us -> 104 us
  waiting for transfers between devices: 280 us -> 14.3 us
  local copies, waits for them, and re-layouts: 114 us -> 0.78 us
  blocking collectives: 91 us -> 0 us
  starting transfers between devices: 0.29 us -> 53.4 us
  matrix products: 47.7 us -> 0 us
  Pallas kernels: 0 us -> 33.6 us
  between operations: 14.2 us -> 0.71 us
    reduce_scatter x1 -> x0, waiting for transfers between devices: 280 us -> none  [body(): lax.psum_scatter(split_attenders, ('row', 'col'), scatter_dimension=1, ti...]
    psum x2 -> x0, blocking collectives: 57.2 us -> none  [the longest x1 32.5 us: body(): inner = lax.psum(jnp.sum(weights_mine * mine, axis=2), 'col')]
    dot_general x8 -> x0, matrix products: 47.7 us -> none  [the longest x1 13.7 us: body(): jnp.einsum('hij,sjhc->sihc', weights_b, values_per_column, preferred_elem...]
    ppermute x0 -> x17, starting transfers between devices: none -> 39.8 us  [the longest x14 33.2 us: swapped(): lax.ppermute(a, axis, [(i, i ^ bits) for i in range(lax.axis_size(axis))])]
    add x2 -> x0, local copies, waits for them, and re-layouts: 34.4 us -> none  [body(): split_attenders + lax.dynamic_update_slice_in_dim(jnp.zeros_like(split_at...]
    pmax x1 -> x0, blocking collectives: 33.8 us -> none  [body(): peak = lax.pmax(jnp.max(masked, axis=2), 'col')]
    pallas_call x0 -> x7, Pallas kernels: none -> 33.6 us  [call(): pl.pallas_call(kernel, out_shape=outs, in_specs=[pl.BlockSpec(memory_spac...]
    reshape x6 -> x0, local copies, waits for them, and re-layouts: 30.9 us -> none  [the longest x1 9.24 us: body(): (projection_cotangent * kept_sequences * gate_act * (1.0 - gate_act)).res...]
  transfers between devices with their start and end apart: 3 -> 19, of which waited for: 1 -> 5; matrix products, arithmetic and copies ran while one was open for 24% -> 1% of each run, Pallas kernels for 0% -> 28%
where the time goes in v1:
time: 105 us; the launch traced here: 104 us
  starting transfers between devices  53.4 us (51%)
  Pallas kernels  33.6 us (32%)
  waiting for transfers between devices  14.3 us (14%)
  other arithmetic  1.33 us (1%)
    pallas_call x7, Pallas kernels, call(): pl.pallas_call(kernel, out_shape=outs, in_specs=[pl.BlockSpec(memory_spac...  33.6 us
    ppermute x14, starting transfers between devices, swapped(): lax.ppermute(a, axis, [(i, i ^ bits) for i in range(lax.axis_size(axis))])  33.2 us
    ppermute x14, waiting for transfers between devices, swapped(): lax.ppermute(a, axis, [(i, i ^ bits) for i in range(lax.axis_size(axis))])  9.76 us
    all_to_all x1, starting transfers between devices, body(): stats = lax.all_to_all(stats, 'col', 0, 0, tiled=True)  7.41 us
    all_to_all x1, starting transfers between devices, body(): col_term = lax.all_to_all(col_term, 'row', 0, 0, tiled=True)  6.16 us
    ppermute x1, starting transfers between devices, body(): mine = lax.ppermute(packed, ('row', 'col'), routes)  4.4 us
    all_to_all x1, waiting for transfers between devices, body(): stats = lax.all_to_all(stats, 'col', 0, 0, tiled=True)  2.69 us
  transfers between devices with their start and end apart: 19, of which 5 were waited for; matrix products, arithmetic and copies ran while one was open for 1% of the time, Pallas kernels for 28%

profile of v1, /device:TPU:2, one launch (start us, length us, event | category | flops | bytes accessed | tf_op | source)
XLA Modules:
  0.0 104.1 jit_solution(7118269805939409962)
XLA Ops:
  0.6 0.8 dynamic_slice.3
  1.4 3.5 %shard_map.95 = (bf16[48,64,128]{2,1,0:T(8,128)(2,1)S(1)}, f32[8,16,192]{2,1,0:T(8,128)}) custom-call(bf16[32,64,192]{2,1,0:T(8,128)(2,1)} %bitcast.10, f32[8,192,192]{2,1,0:T(8,128)} %scores_ref.3, s32[1,192]{1,0:T(1,128)S(1)} %bitcast.8), custom_call_target="tpu_custom_call" | custom-call | bytes 4194304 | tf_op jit(solution)/shard_map/pallas_call | solution.py:24
  4.9 4.4 %collective-permute-start = (bf16[48,64,128]{2,1,0:T(8,128)(2,1)S(1)}, bf16[48,64,128]{2,1,0:T(8,128)(2,1)S(1)}, u32[]{:S(2)}, u32[]{:S(2)}) collective-permute-start(bf16[48,64,128]{2,1,0:T(8,128)(2,1)S(1)} %get-tuple-element.29), channel_id=1, source_target_pairs={{0,0},{9,9},{2,16},{11,25},{4,32},{13,41},{6,48},{15,57},{16,34},{... | collective-permute-start | bytes 2359304 | tf_op jit(solution)/shard_map/ppermute | solution.py:319
  9.3 7.4 %all-to-all-start = ((f32[8,16,192]{2,1,0:T(8,128)}), f32[8,16,192]{2,1,0:T(8,128)S(1)}, u32[]{:S(2)}, u32[]{:S(2)}) async-start(f32[8,16,192]{2,1,0:T(8,128)} %get-tuple-element.30), calls=%async_computation | async-start | bytes 262144 | tf_op jit(solution)/shard_map/all_to_all | solution.py:310
  16.7 8.2 %shard_map.96 = (bf16[32,256,192]{2,1,0:T(8,128)(2,1)}, f32[32,256,192]{2,1,0:T(8,128)}, bf16[8,192,1024]{2,1,0:T(8,128)(2,1)}) custom-call(bf16[32,64,192]{2,1,0:T(8,128)(2,1)} %bitcast.11, bf16[32,64,192]{2,1,0:T(8,128)(2,1)} %bitcast.12, s32[32,192]{1,0:T(8,128)} %mask_ref.1, bf16[64,256]{1,0:T(8,128)(2,1)} %gate_w_ref.3, bf16[64,256]{1,0:T(8,128)(2,1)} %bitcast.13), custom_call_target="tpu_custom_call" | custom-call | flops 1073741824 | bytes 14680064 | tf_op jit(solution)/shard_map/pallas_call | solution.py:24
  24.9 2.7 %all-to-all-done.stats_ref = f32[8,16,192]{2,1,0:T(8,128)S(1)} async-done(((f32[8,16,192]{2,1,0:T(8,128)}), f32[8,16,192]{2,1,0:T(8,128)S(1)}, u32[]{:S(2)}, u32[]{:S(2)}) %all-to-all-start) | async-done | bytes 98336 | tf_op jit(solution)/shard_map/all_to_all | solution.py:310
  27.6 0.0 collective-permute-done.mine_ref
  27.6 0.3 collective-permute-start.1
  27.9 7.7 %shard_map.97 = (f32[8,192,192]{2,1,0:T(8,128)}, bf16[8,192,192]{2,1,0:T(8,128)(2,1)}, bf16[8,24,2048]{2,1,0:T(8,128)(2,1)}) custom-call(f32[8,192,192]{2,1,0:T(8,128)} %scores_ref.3, s32[1,192]{1,0:T(1,128)S(1)} %bitcast.9, f32[8,16,192]{2,1,0:T(8,128)S(1)} %all-to-all-done.stats_ref, bf16[32,256,192]{2,1,0:T(8,128)(2,1)} %get-tuple-element.34.att_ref, ...), custom_call_target="tpu_custom_call" | custom-call | flops 1073741824 | bytes 14680064 | tf_op jit(solution)/shard_map/pallas_call | solution.py:24
  35.6 6.2 %all-to-all-start.1 = ((bf16[8,24,2048]{2,1,0:T(8,128)(2,1)}), bf16[8,24,2048]{2,1,0:T(8,128)(2,1)}, u32[]{:S(2)}, u32[]{:S(2)}) async-start(bf16[8,24,2048]{2,1,0:T(8,128)(2,1)} %get-tuple-element.43), calls=%async_computation.1 | async-start | bytes 1572864 | tf_op jit(solution)/shard_map/all_to_all | solution.py:376
  41.7 0.1 pad_add_fusion.place_ref
  41.8 0.0 collective-permute-done.1.other_ref
  41.8 10.2 %shard_map.98 = (f32[8,192]{1,0:T(8,128)S(1)}, bf16[2,24,2048]{2,1,0:T(8,128)(2,1)S(1)}, bf16[2,24,2048]{2,1,0:T(8,128)(2,1)S(1)}, bf16[2,24,2048]{2,1,0:T(8,128...) custom-call(s32[4]{0:T(128)S(1)} %pad_add_fusion.place_ref, ...), custom_call_target="tpu_custom_call" | custom-call | flops 1073741824 | bytes 18874368 | tf_op jit(solution)/shard_map/pallas_call | solution.py:24
  52.1 0.7 collective-permute-start.2
  52.7 2.7 %collective-permute-start.3 = (bf16[2,24,2048]{2,1,0:T(8,128)(2,1)S(1)}, bf16[2,24,2048]{2,1,0:T(8,128)(2,1)S(1)}, u32[]{:S(2)}, u32[]{:S(2)}) collective-permute-start(bf16[2,24,2048]{2,1,0:T(8,128)(2,1)S(1)} %get-tuple-element.41), channel_id=1, source_target_pairs={{0,4},{1,5},{2,6},{3,7},{4,0},{5,1},{6,2},{7,3},{8,12},{9,13},{10,... | collective-permute-start | bytes 589832 | tf_op jit(solution)/shard_map/ppermute | solution.py:419
  55.4 1.4 %collective-permute-start.4 = (bf16[2,24,2048]{2,1,0:T(8,128)(2,1)S(1)}, bf16[2,24,2048]{2,1,0:T(8,128)(2,1)S(1)}, u32[]{:S(2)}, u32[]{:S(2)}) collective-permute-start(bf16[2,24,2048]{2,1,0:T(8,128)(2,1)S(1)} %get-tuple-element.42), channel_id=1, source_target_pairs={{0,6},{1,7},{2,4},{3,5},{4,2},{5,3},{6,0},{7,1},{8,14},{9,15},{10,... | collective-permute-start | bytes 589832 | tf_op jit(solution)/shard_map/ppermute | solution.py:419
  56.9 0.0 all-to-all-done.1
  56.9 1.2 %reduce_sum.12 = bf16[24,2048]{1,0:T(8,128)(2,1)S(1)} reduce(bf16[8,24,2048]{2,1,0:T(8,128)(2,1)} %all-to-all-done.1, bf16[]{:T(256)} %constant.47.clone.1), dimensions={0}, to_apply=%region_0.1 | reduce | flops 344064 | bytes 884738 | tf_op jit(solution)/shard_map/reduce_sum | solution.py:377
  58.1 1.9 %collective-permute-start.5 = (bf16[24,2048]{1,0:T(8,128)(2,1)S(1)}, bf16[24,2048]{1,0:T(8,128)(2,1)S(1)}, u32[]{:S(2)}, u32[]{:S(2)}) collective-permute-start(bf16[24,2048]{1,0:T(8,128)(2,1)S(1)} %reduce_sum.12), channel_id=1, source_target_pairs={{0,0},{1,8},{2,16},{3,24},{4,32},{5,40},{6,48},{7,56},{8,1},{9,9},... | collective-permute-start | bytes 294920 | tf_op jit(solution)/shard_map/ppermute | solution.py:378
  60.0 3.7 %collective-permute-start.9 = (f32[8,192]{1,0:T(8,128)S(1)}, f32[8,192]{1,0:T(8,128)S(1)}, u32[]{:S(2)}, u32[]{:S(2)}) collective-permute-start(f32[8,192]{1,0:T(8,128)S(1)} %get-tuple-element.46), channel_id=1, source_target_pairs={{0,6},{1,7},{2,4},{3,5},{4,2},{5,3},{6,0},{7,1},{8,14},{9,15},{10,... | collective-permute-start | bytes 18440 | tf_op jit(solution)/shard_map/ppermute | solution.py:419
  63.7 1.8 %collective-permute-done.5.cols_ref = bf16[24,2048]{1,0:T(8,128)(2,1)S(1)} collective-permute-done((bf16[24,2048]{1,0:T(8,128)(2,1)S(1)}, bf16[24,2048]{1,0:T(8,128)(2,1)S(1)}, u32[]{:S(2)}, u32[]{:S(2)}) %collective-permute-start.5) | collective-permute-done | bytes 98336 | tf_op jit(solution)/shard_map/ppermute | solution.py:378
  65.5 1.1 %collective-permute-start.8 = (f32[8,192]{1,0:T(8,128)S(1)}, f32[8,192]{1,0:T(8,128)S(1)}, u32[]{:S(2)}, u32[]{:S(2)}) collective-permute-start(f32[8,192]{1,0:T(8,128)S(1)} %get-tuple-element.46), channel_id=1, source_target_pairs={{0,4},{1,5},{2,6},{3,7},{4,0},{5,1},{6,2},{7,3},{8,12},{9,13},{10,... | collective-permute-start | bytes 18440 | tf_op jit(solution)/shard_map/ppermute | solution.py:419
  66.6 0.0 collective-permute-done.2.part1_ref
  66.6 5.2 %collective-permute-start.7 = (f32[8,192]{1,0:T(8,128)S(1)}, f32[8,192]{1,0:T(8,128)S(1)}, u32[]{:S(2)}, u32[]{:S(2)}) collective-permute-start(f32[8,192]{1,0:T(8,128)S(1)} %get-tuple-element.46), channel_id=1, source_target_pairs={{0,2},{1,3},{2,0},{3,1},{4,6},{5,7},{6,4},{7,5},{8,10},{9,11},{10,... | collective-permute-start | bytes 18440 | tf_op jit(solution)/shard_map/ppermute | solution.py:419
  71.8 0.0 collective-permute-done.3.part2_ref
  71.8 1.1 %collective-permute-start.11 = (bf16[3,192,128]{2,1,0:T(8,128)(2,1)S(1)}, bf16[3,192,128]{2,1,0:T(8,128)(2,1)S(1)}, u32[]{:S(2)}, u32[]{:S(2)}) collective-permute-start(bf16[3,192,128]{2,1,0:T(8,128)(2,1)S(1)} %get-tuple-element.48), channel_id=1, source_target_pairs={{0,64},{64,0},{128,192},{192,128},{1,65},{65,1},{129,193},{193,129... | collective-permute-start | bytes 442376 | tf_op jit(solution)/shard_map/ppermute | solution.py:419
  72.8 0.0 collective-permute-done.4.part3_ref
  72.8 1.4 %collective-permute-start.12 = (bf16[3,192,128]{2,1,0:T(8,128)(2,1)S(1)}, bf16[3,192,128]{2,1,0:T(8,128)(2,1)S(1)}, u32[]{:S(2)}, u32[]{:S(2)}) collective-permute-start(bf16[3,192,128]{2,1,0:T(8,128)(2,1)S(1)} %get-tuple-element.49), channel_id=1, source_target_pairs={{0,128},{64,192},{128,0},{192,64},{1,129},{65,193},{129,1},{193,65... | collective-permute-start | bytes 442376 | tf_op jit(solution)/shard_map/ppermute | solution.py:419
  74.3 0.7 shard_map.99
  75.0 0.0 collective-permute-done.9
  75.0 2.2 %collective-permute-start.13 = (bf16[3,192,128]{2,1,0:T(8,128)(2,1)S(1)}, bf16[3,192,128]{2,1,0:T(8,128)(2,1)S(1)}, u32[]{:S(2)}, u32[]{:S(2)}) collective-permute-start(bf16[3,192,128]{2,1,0:T(8,128)(2,1)S(1)} %get-tuple-element.50), channel_id=1, source_target_pairs={{0,192},{64,128},{128,64},{192,0},{1,193},{65,129},{129,65},{193,1... | collective-permute-start | bytes 442376 | tf_op jit(solution)/shard_map/ppermute | solution.py:419
  77.1 0.0 collective-permute-done.8
  77.1 9.2 %collective-permute-start.6 = (bf16[24,2048]{1,0:T(8,128)(2,1)S(1)}, bf16[24,2048]{1,0:T(8,128)(2,1)S(1)}, u32[]{:S(2)}, u32[]{:S(2)}) collective-permute-start(bf16[24,2048]{1,0:T(8,128)(2,1)S(1)} %get-tuple-element.45), channel_id=1, source_target_pairs={{0,1},{1,0},{2,3},{3,2},{4,5},{5,4},{6,7},{7,6},{8,9},{9,8},{10,11... | collective-permute-start | bytes 294920 | tf_op jit(solution)/shard_map/ppermute | solution.py:419
  86.4 0.0 collective-permute-done.7
  86.4 0.1 collective-permute-start.10
  86.5 7.7 %collective-permute-done.10 = f32[8,192]{1,0:T(8,128)S(1)} collective-permute-done((f32[8,192]{1,0:T(8,128)S(1)}, f32[8,192]{1,0:T(8,128)S(1)}, u32[]{:S(2)}, u32[]{:S(2)}) %collective-permute-start.10) | collective-permute-done | bytes 6176 | tf_op jit(solution)/shard_map/ppermute | solution.py:419
  94.2 0.0 collective-permute-done.11.part1_ref
  94.2 0.0 collective-permute-done.12.part2_ref
  94.2 0.0 collective-permute-done.13.part3_ref
  94.2 2.0 %collective-permute-start.16 = (f32[8,192]{1,0:T(8,128)S(1)}, f32[8,192]{1,0:T(8,128)S(1)}, u32[]{:S(2)}, u32[]{:S(2)}) collective-permute-start(f32[8,192]{1,0:T(8,128)S(1)} %add.29.inner0_ref), channel_id=1, source_target_pairs={{0,192},{64,128},{128,64},{192,0},{1,193},{65,129},{129,65},{193,1... | collective-permute-start | bytes 18440 | tf_op jit(solution)/shard_map/ppermute | solution.py:419
  96.2 0.5 collective-permute-start.15
  96.7 2.0 %collective-permute-start.14 = (f32[8,192]{1,0:T(8,128)S(1)}, f32[8,192]{1,0:T(8,128)S(1)}, u32[]{:S(2)}, u32[]{:S(2)}) collective-permute-start(f32[8,192]{1,0:T(8,128)S(1)} %add.29.inner0_ref), channel_id=1, source_target_pairs={{0,64},{64,0},{128,192},{192,128},{1,65},{65,1},{129,193},{193,129... | collective-permute-start | bytes 18440 | tf_op jit(solution)/shard_map/ppermute | solution.py:419
  98.7 1.1 %collective-permute-done.16.inner3_ref = f32[8,192]{1,0:T(8,128)S(1)} collective-permute-done((f32[8,192]{1,0:T(8,128)S(1)}, f32[8,192]{1,0:T(8,128)S(1)}, u32[]{:S(2)}, u32[]{:S(2)}) %collective-permute-start.16) | collective-permute-done | bytes 6176 | tf_op jit(solution)/shard_map/ppermute | solution.py:419
  99.7 1.0 collective-permute-done.15.inner2_ref
  100.7 0.0 collective-permute-done.14.inner1_ref
  100.7 2.5 %shard_map.101 = f32[2,192,192]{2,1,0:T(8,128)} custom-call(s32[4]{0:T(128)S(1)} %pad_add_fusion.place_ref, bf16[3,192,128]{2,1,0:T(8,128)(2,1)S(1)} %get-tuple-element.51.part0_ref, bf16[3,192,128]{2,1,0:T(8,128)(2,1)S(1)} %collective-permute-done.11.part1_ref, bf16[3,192,128]{2,1,0:T(8,128)(2,1)S(1)} %collective-permute-done.12.part2_ref, ...), custom_call_target="tpu_custom_call" | custom-call | bytes 2097152 | tf_op jit(solution)/shard_map/pallas_call | solution.py:24
  103.2 0.0 collective-permute-done.6.rows_ref
  103.2 0.9 shard_map.100
  (2 shorter events, 0.0 us)
Async XLA Ops:
  4.9 22.7 %collective-permute-start = (bf16[48,64,128]{2,1,0:T(8,128)(2,1)S(1)}, bf16[48,64,128]{2,1,0:T(8,128)(2,1)S(1)}, u32[]{:S(2)}, u32[]{:S(2)}) collective-permute-start(bf16[48,64,128]{2,1,0:T(8,128)(2,1)S(1)} %get-tuple-element.29), channel_id=1, source_target_pairs={{0,0},{9,9},{2,16},{11,25},{4,32},{13,41},{6,48},{15,57},{16,34},{... | collective-permute-start | bytes 2359304 | tf_op jit(solution)/shard_map/ppermute | solution.py:319
  9.3 18.3 %all-to-all-start = ((f32[8,16,192]{2,1,0:T(8,128)}), f32[8,16,192]{2,1,0:T(8,128)S(1)}, u32[]{:S(2)}, u32[]{:S(2)}) async-start(f32[8,16,192]{2,1,0:T(8,128)} %get-tuple-element.30), calls=%async_computation | async-start | bytes 262144 | tf_op jit(solution)/shard_map/all_to_all | solution.py:310
  27.6 14.2 %collective-permute-start.1 = (bf16[48,64,128]{2,1,0:T(8,128)(2,1)S(1)}, bf16[48,64,128]{2,1,0:T(8,128)(2,1)S(1)}, u32[]{:S(2)}, u32[]{:S(2)}) collective-permute-start(bf16[48,64,128]{2,1,0:T(8,128)(2,1)S(1)} %collective-permute-done.mine_ref), channel_id=1, source_target_pairs={{0,8},{8,0},{16,24},{24,16},{32,40},{40,32},{48,56},{56,48},{1,9},... | collective-permute-start | bytes 2359304 | tf_op jit(solution)/shard_map/ppermute | solution.py:347
  35.6 21.3 %all-to-all-start.1 = ((bf16[8,24,2048]{2,1,0:T(8,128)(2,1)}), bf16[8,24,2048]{2,1,0:T(8,128)(2,1)}, u32[]{:S(2)}, u32[]{:S(2)}) async-start(bf16[8,24,2048]{2,1,0:T(8,128)(2,1)} %get-tuple-element.43), calls=%async_computation.1 | async-start | bytes 1572864 | tf_op jit(solution)/shard_map/all_to_all | solution.py:376
  52.1 14.5 %collective-permute-start.2 = (bf16[2,24,2048]{2,1,0:T(8,128)(2,1)S(1)}, bf16[2,24,2048]{2,1,0:T(8,128)(2,1)S(1)}, u32[]{:S(2)}, u32[]{:S(2)}) collective-permute-start(bf16[2,24,2048]{2,1,0:T(8,128)(2,1)S(1)} %get-tuple-element.40), channel_id=1, source_target_pairs={{0,2},{1,3},{2,0},{3,1},{4,6},{5,7},{6,4},{7,5},{8,10},{9,11},{10,... | collective-permute-start | bytes 589832 | tf_op jit(solution)/shard_map/ppermute | solution.py:419
  52.7 19.0 %collective-permute-start.3 = (bf16[2,24,2048]{2,1,0:T(8,128)(2,1)S(1)}, bf16[2,24,2048]{2,1,0:T(8,128)(2,1)S(1)}, u32[]{:S(2)}, u32[]{:S(2)}) collective-permute-start(bf16[2,24,2048]{2,1,0:T(8,128)(2,1)S(1)} %get-tuple-element.41), channel_id=1, source_target_pairs={{0,4},{1,5},{2,6},{3,7},{4,0},{5,1},{6,2},{7,3},{8,12},{9,13},{10,... | collective-permute-start | bytes 589832 | tf_op jit(solution)/shard_map/ppermute | solution.py:419
  55.4 17.4 %collective-permute-start.4 = (bf16[2,24,2048]{2,1,0:T(8,128)(2,1)S(1)}, bf16[2,24,2048]{2,1,0:T(8,128)(2,1)S(1)}, u32[]{:S(2)}, u32[]{:S(2)}) collective-permute-start(bf16[2,24,2048]{2,1,0:T(8,128)(2,1)S(1)} %get-tuple-element.42), channel_id=1, source_target_pairs={{0,6},{1,7},{2,4},{3,5},{4,2},{5,3},{6,0},{7,1},{8,14},{9,15},{10,... | collective-permute-start | bytes 589832 | tf_op jit(solution)/shard_map/ppermute | solution.py:419
  58.1 7.4 %collective-permute-start.5 = (bf16[24,2048]{1,0:T(8,128)(2,1)S(1)}, bf16[24,2048]{1,0:T(8,128)(2,1)S(1)}, u32[]{:S(2)}, u32[]{:S(2)}) collective-permute-start(bf16[24,2048]{1,0:T(8,128)(2,1)S(1)} %reduce_sum.12), channel_id=1, source_target_pairs={{0,0},{1,8},{2,16},{3,24},{4,32},{5,40},{6,48},{7,56},{8,1},{9,9},... | collective-permute-start | bytes 294920 | tf_op jit(solution)/shard_map/ppermute | solution.py:378
  60.0 14.9 %collective-permute-start.9 = (f32[8,192]{1,0:T(8,128)S(1)}, f32[8,192]{1,0:T(8,128)S(1)}, u32[]{:S(2)}, u32[]{:S(2)}) collective-permute-start(f32[8,192]{1,0:T(8,128)S(1)} %get-tuple-element.46), channel_id=1, source_target_pairs={{0,6},{1,7},{2,4},{3,5},{4,2},{5,3},{6,0},{7,1},{8,14},{9,15},{10,... | collective-permute-start | bytes 18440 | tf_op jit(solution)/shard_map/ppermute | solution.py:419
  65.5 11.6 %collective-permute-start.8 = (f32[8,192]{1,0:T(8,128)S(1)}, f32[8,192]{1,0:T(8,128)S(1)}, u32[]{:S(2)}, u32[]{:S(2)}) collective-permute-start(f32[8,192]{1,0:T(8,128)S(1)} %get-tuple-element.46), channel_id=1, source_target_pairs={{0,4},{1,5},{2,6},{3,7},{4,0},{5,1},{6,2},{7,3},{8,12},{9,13},{10,... | collective-permute-start | bytes 18440 | tf_op jit(solution)/shard_map/ppermute | solution.py:419
  66.6 19.8 %collective-permute-start.7 = (f32[8,192]{1,0:T(8,128)S(1)}, f32[8,192]{1,0:T(8,128)S(1)}, u32[]{:S(2)}, u32[]{:S(2)}) collective-permute-start(f32[8,192]{1,0:T(8,128)S(1)} %get-tuple-element.46), channel_id=1, source_target_pairs={{0,2},{1,3},{2,0},{3,1},{4,6},{5,7},{6,4},{7,5},{8,10},{9,11},{10,... | collective-permute-start | bytes 18440 | tf_op jit(solution)/shard_map/ppermute | solution.py:419
  71.8 22.4 %collective-permute-start.11 = (bf16[3,192,128]{2,1,0:T(8,128)(2,1)S(1)}, bf16[3,192,128]{2,1,0:T(8,128)(2,1)S(1)}, u32[]{:S(2)}, u32[]{:S(2)}) collective-permute-start(bf16[3,192,128]{2,1,0:T(8,128)(2,1)S(1)} %get-tuple-element.48), channel_id=1, source_target_pairs={{0,64},{64,0},{128,192},{192,128},{1,65},{65,1},{129,193},{193,129... | collective-permute-start | bytes 442376 | tf_op jit(solution)/shard_map/ppermute | solution.py:419
  72.8 21.3 %collective-permute-start.12 = (bf16[3,192,128]{2,1,0:T(8,128)(2,1)S(1)}, bf16[3,192,128]{2,1,0:T(8,128)(2,1)S(1)}, u32[]{:S(2)}, u32[]{:S(2)}) collective-permute-start(bf16[3,192,128]{2,1,0:T(8,128)(2,1)S(1)} %get-tuple-element.49), channel_id=1, source_target_pairs={{0,128},{64,192},{128,0},{192,64},{1,129},{65,193},{129,1},{193,65... | collective-permute-start | bytes 442376 | tf_op jit(solution)/shard_map/ppermute | solution.py:419
  75.0 19.2 %collective-permute-start.13 = (bf16[3,192,128]{2,1,0:T(8,128)(2,1)S(1)}, bf16[3,192,128]{2,1,0:T(8,128)(2,1)S(1)}, u32[]{:S(2)}, u32[]{:S(2)}) collective-permute-start(bf16[3,192,128]{2,1,0:T(8,128)(2,1)S(1)} %get-tuple-element.50), channel_id=1, source_target_pairs={{0,192},{64,128},{128,64},{192,0},{1,193},{65,129},{129,65},{193,1... | collective-permute-start | bytes 442376 | tf_op jit(solution)/shard_map/ppermute | solution.py:419
  77.1 26.1 %collective-permute-start.6 = (bf16[24,2048]{1,0:T(8,128)(2,1)S(1)}, bf16[24,2048]{1,0:T(8,128)(2,1)S(1)}, u32[]{:S(2)}, u32[]{:S(2)}) collective-permute-start(bf16[24,2048]{1,0:T(8,128)(2,1)S(1)} %get-tuple-element.45), channel_id=1, source_target_pairs={{0,1},{1,0},{2,3},{3,2},{4,5},{5,4},{6,7},{7,6},{8,9},{9,8},{10,11... | collective-permute-start | bytes 294920 | tf_op jit(solution)/shard_map/ppermute | solution.py:419
  86.4 7.8 %collective-permute-start.10 = (f32[8,192]{1,0:T(8,128)S(1)}, f32[8,192]{1,0:T(8,128)S(1)}, u32[]{:S(2)}, u32[]{:S(2)}) collective-permute-start(f32[8,192]{1,0:T(8,128)S(1)} %add_add_fusion), channel_id=1, source_target_pairs={{0,1},{1,0},{2,3},{3,2},{4,5},{5,4},{6,7},{7,6},{8,9},{9,8},{10,11... | collective-permute-start | bytes 18440 | tf_op jit(solution)/shard_map/ppermute | solution.py:419
  94.2 5.5 %collective-permute-start.16 = (f32[8,192]{1,0:T(8,128)S(1)}, f32[8,192]{1,0:T(8,128)S(1)}, u32[]{:S(2)}, u32[]{:S(2)}) collective-permute-start(f32[8,192]{1,0:T(8,128)S(1)} %add.29.inner0_ref), channel_id=1, source_target_pairs={{0,192},{64,128},{128,64},{192,0},{1,193},{65,129},{129,65},{193,1... | collective-permute-start | bytes 18440 | tf_op jit(solution)/shard_map/ppermute | solution.py:419
  96.2 4.5 %collective-permute-start.15 = (f32[8,192]{1,0:T(8,128)S(1)}, f32[8,192]{1,0:T(8,128)S(1)}, u32[]{:S(2)}, u32[]{:S(2)}) collective-permute-start(f32[8,192]{1,0:T(8,128)S(1)} %add.29.inner0_ref), channel_id=1, source_target_pairs={{0,128},{64,192},{128,0},{192,64},{1,129},{65,193},{129,1},{193,65... | collective-permute-start | bytes 18440 | tf_op jit(solution)/shard_map/ppermute | solution.py:419
  96.7 4.1 %collective-permute-start.14 = (f32[8,192]{1,0:T(8,128)S(1)}, f32[8,192]{1,0:T(8,128)S(1)}, u32[]{:S(2)}, u32[]{:S(2)}) collective-permute-start(f32[8,192]{1,0:T(8,128)S(1)} %add.29.inner0_ref), channel_id=1, source_target_pairs={{0,64},{64,0},{128,192},{192,128},{1,65},{65,1},{129,193},{193,129... | collective-permute-start | bytes 18440 | tf_op jit(solution)/shard_map/ppermute | solution.py:419

commit v2 on v1

v2 whole, which is shorter than its diff:
```python
import jax
import jax.numpy as jnp
from jax import lax
from jax.experimental import pallas as pl
from jax.experimental.pallas import tpu as pltpu
from jax.sharding import PartitionSpec as P

F32 = jnp.float32
BF16 = jnp.bfloat16
MASKED = -1000000000.0
VMEM_BYTES = 24 * 1024 * 1024
STEPS = 4


def call(kernel, outs, inputs, in_specs=None, out_specs=None, grid=None, scratch=(), scalars=None, flops=0, moved=0):
    local = lambda: pl.BlockSpec(memory_space=pltpu.VMEM)
    several = isinstance(outs, list)
    operands = [] if scalars is None else [scalars]
    if in_specs is None:
        in_specs = [local() for _ in inputs]
    if out_specs is None:
        out_specs = [local() for _ in outs] if several else local()
    extra = {} if grid is None else {"grid": grid}
    return pl.pallas_call(
        kernel,
        out_shape=outs,
        in_specs=[pl.BlockSpec(memory_space=pltpu.SMEM)] * len(operands) + in_specs,
        out_specs=out_specs,
        scratch_shapes=list(scratch),
        compiler_params=pltpu.CompilerParams(vmem_limit_bytes=VMEM_BYTES),
        cost_estimate=pl.CostEstimate(flops=flops, bytes_accessed=moved, transcendentals=0),
        **extra,
    )(*operands, *inputs)


def whole(shape):
    return pl.BlockSpec(shape, lambda i: (0,) * len(shape))


def by_step(*dims):
    return pl.BlockSpec(dims, lambda i: (i,) + (0,) * (len(dims) - 1))


def far(a):
    return pltpu.with_memory_space_constraint(a, pltpu.HBM)


def dot(a, b):
    return jnp.dot(a, b, preferred_element_type=F32)


def turned(a):
    return a.astype(F32).T.astype(a.dtype)


def stats_kernel(scores_ref, keep_ref, stats_ref):
    heads, rows, _ = scores_ref.shape
    keep = keep_ref[...] > 0
    lane = lax.broadcasted_iota(jnp.int32, (rows, 128), 1)
    table = jnp.zeros((rows, 128), F32)
    for h in range(heads):
        masked = jnp.where(keep, scores_ref[h], MASKED)
        peak = jnp.max(masked, axis=1, keepdims=True)
        total = jnp.sum(jnp.exp(masked - peak), axis=1, keepdims=True)
        table = jnp.where(lane == h, peak, table)
        table = jnp.where(lane == heads + h, total, table)
    packed = table.T[0 : 2 * heads]
    for k in range(stats_ref.shape[0]):
        stats_ref[k] = packed


def gate_kernel(x_ref, cot_ref, mask_ref, gate_w_ref, final_w_ref, att_ref, term_ref, att_rows_ref, wt):
    @pl.when(pl.program_id(0) == 0)
    def _():
        wt[0] = turned(gate_w_ref[...])
        wt[1] = turned(final_w_ref[...])

    sequences, _, rows = x_ref.shape
    heads = att_rows_ref.shape[0]
    dim = wt.shape[1] // heads
    mask = mask_ref[...].astype(F32)
    for s in range(sequences):
        gate = 1.0 / (1.0 + jnp.exp(-dot(wt[0], x_ref[s])))
        cot = dot(wt[1], cot_ref[s]) * mask[s : s + 1]
        att = cot * gate
        att_ref[s] = att.astype(BF16)
        term_ref[s] = (att * (1.0 - gate)).astype(BF16)
    for h in range(heads):
        block = att_ref[:, h * dim : (h + 1) * dim, :].reshape(sequences * dim, rows)
        att_rows_ref[h] = turned(block)


def project_rows(weight, hi, lo, out_ref, first):
    sequences = hi.shape[0]
    chunks, stretch, _ = out_ref.shape
    features = weight.shape[0]
    for s in range(0, sequences, 2):
        pair = [dot(weight, hi[s + k]) + dot(weight, lo[s + k]) for k in (0, 1)]
        rows = jnp.concatenate(pair, axis=0).T.reshape(chunks, stretch, 2 * features)
        lanes = pl.ds(pl.multiple_of((first + s) * features, 128), 2 * features)
        out_ref[:, :, lanes] = rows.astype(out_ref.dtype)


def split(grad, hi, lo, h, dim):
    top = grad.astype(BF16)
    hi[:, h * dim : (h + 1) * dim, :] = top
    lo[:, h * dim : (h + 1) * dim, :] = (grad - top.astype(F32)).astype(BF16)


def thirds(table):
    first = table.astype(BF16)
    rest = table - first.astype(F32)
    second = rest.astype(BF16)
    third = (rest - second.astype(F32)).astype(BF16)
    return jnp.concatenate([t.astype(F32) for t in (first, second, third)], axis=0).astype(BF16)


def joined(table):
    count = table.shape[0] // 3
    table = table.astype(F32)
    return table[0:count] + table[count : 2 * count] + table[2 * count : 3 * count]


def main_kernel(
    place_ref,
    scores_ref,
    keep_ref,
    stats_ref,
    att_ref,
    term_ref,
    att_rows_ref,
    mine_ref,
    other_ref,
    payload_ref,
    gate_w_ref,
    weights_ref,
    col_ref,
    row0_ref,
    row1_ref,
    row2_ref,
    row3_ref,
    pair0_ref,
    pair1_ref,
    pair2_ref,
    pair3_ref,
    wt,
    weights,
    wb,
    turned_wb,
    values,
    hi,
    lo,
    row_out,
    pair_sum,
    pair_out,
):
    step = pl.program_id(0)
    heads, rows, columns = scores_ref.shape
    group, width, _ = att_ref.shape
    dim = width // heads
    wide = col_ref.shape[2]

    @pl.when(step == 0)
    def _():
        wt[...] = turned(payload_ref[...])
        pair_sum[...] = jnp.zeros(pair_sum.shape, F32)
        peaks = stats_ref[:, 0:heads]
        peak = jnp.max(peaks, axis=0)
        total = jnp.sum(stats_ref[:, heads : 2 * heads] * jnp.exp(peaks - peak[None]), axis=0)
        table = jnp.concatenate([peak, 1.0 / total, jnp.zeros((128 - 2 * heads, rows), F32)], axis=0).T
        keep = keep_ref[...] > 0
        for h in range(heads):
            masked = jnp.where(keep, scores_ref[h], MASKED)
            exact = jnp.exp(masked - table[:, h : h + 1]) * table[:, heads + h : heads + h + 1]
            weights[h] = exact
            wb[h] = exact.astype(BF16)
            turned_wb[h] = exact.T.astype(BF16)

    first = pl.multiple_of(step * group, group)
    for h in range(heads):
        block = att_ref[:, h * dim : (h + 1) * dim, :].reshape(group * dim, rows)
        split(dot(block, wb[h]).reshape(group, dim, columns), hi, lo, h, dim)
    project_rows(payload_ref[...], hi, lo, col_ref, first)

    own = place_ref[0] == place_ref[1]
    tokens = jnp.where(own, mine_ref[pl.ds(first, group)], other_ref[pl.ds(first, group)])
    for k in range(group):
        values[k] = dot(wt[...], tokens[k]).astype(BF16)
    for h in range(heads):
        block = values[:, h * dim : (h + 1) * dim, :].reshape(group * dim, columns)
        average = dot(block, turned_wb[h]).reshape(group, dim, rows)
        split(average * term_ref[:, h * dim : (h + 1) * dim, :].astype(F32), hi, lo, h, dim)
        pair_sum[h] += dot(att_rows_ref[h], block)
    project_rows(gate_w_ref[...], hi, lo, row_out, first)

    @pl.when(step == pl.num_programs(0) - 1)
    def _():
        lane = lax.broadcasted_iota(jnp.int32, (rows, 128), 1)
        table = jnp.zeros((rows, 128), F32)
        owners = pair_out.shape[0]
        own_heads = heads // owners
        for k in range(owners):
            tails = []
            for g in range(own_heads):
                h = k * own_heads + g
                grad = pair_sum[h].astype(BF16)
                pair_out[k, g] = grad[:, 0:128]
                tails.append(grad[:, 128:192])
                inner = jnp.sum(weights[h] * grad.astype(F32), axis=1, keepdims=True)
                table = jnp.where(lane == h, inner, table)
            pair_out[k, own_heads] = jnp.concatenate(tails, axis=-1)
        inner = thirds(jnp.concatenate([table.T[0:heads], jnp.zeros((heads, 256 - rows), F32)], axis=-1))
        for k, out_ref in enumerate((row0_ref, row1_ref, row2_ref, row3_ref)):
            out_ref[:, :, 0:wide] = row_out[pl.ds(2 * (place_ref[2] ^ k), 2)]
            for z in range(2):
                out_ref[z, :, wide:] = inner
        for k, out_ref in enumerate((pair0_ref, pair1_ref, pair2_ref, pair3_ref)):
            out_ref[...] = pair_out[place_ref[3] ^ k]
        weights_ref[...] = weights[pl.ds(place_ref[3] * own_heads, own_heads)]


def score_kernel(
    place_ref,
    part0_ref,
    part1_ref,
    part2_ref,
    part3_ref,
    inner0_ref,
    inner1_ref,
    inner2_ref,
    inner3_ref,
    weights_ref,
    out_ref,
):
    heads, rows, _ = out_ref.shape
    total = part0_ref[...].astype(F32)
    for part in (part1_ref, part2_ref, part3_ref):
        total = total + part[...].astype(F32)
    inner = ((inner0_ref[...] + inner1_ref[...]) + (inner2_ref[...] + inner3_ref[...]))[:, 0:rows]
    table = jnp.concatenate([inner, jnp.zeros((128 - inner.shape[0], rows), F32)], axis=0).T
    lane = lax.broadcasted_iota(jnp.int32, table.shape, 1)
    for h in range(heads):
        mine = place_ref[3] * heads + h
        grad = jnp.concatenate([total[h], total[heads][:, 64 * h : 64 * h + 64]], axis=-1)
        own = jnp.sum(jnp.where(lane == mine, table, 0.0), axis=1, keepdims=True)
        out_ref[h] = weights_ref[h] * (grad - own)


def fold_kernel(place_ref, part0_ref, part1_ref, part2_ref, part3_ref, keep_ref, inner_ref, send_ref):
    wide = keep_ref.shape[1]
    parts = (part0_ref, part1_ref, part2_ref, part3_ref)
    total = sum(part[:, :, 0:wide].astype(F32) for part in parts)
    high = place_ref[1] == 1
    keep_ref[...] = jnp.where(high, total[1], total[0])
    send_ref[:, 0:wide] = jnp.where(high, total[0], total[1]).astype(BF16)
    inner = sum(joined(part[0, :, wide:]) for part in parts)
    inner_ref[...] = inner
    send_ref[:, wide:] = thirds(inner)


def inner_kernel(inner_ref, rows_ref, out_ref):
    out_ref[...] = inner_ref[...] + joined(rows_ref[:, rows_ref.shape[1] - 256 :])


def join_kernel(keep_ref, rows_ref, cols_ref, out_ref):
    sequences, _, features = out_ref.shape
    total = keep_ref[...] + rows_ref[:, 0 : keep_ref.shape[1]].astype(F32) + cols_ref[...].astype(F32)
    for s in range(sequences):
        out_ref[s] = total[:, s * features : (s + 1) * features]


def body(
    layernormed_alignment,
    average_cotangent,
    sequence_validity,
    residue_validity,
    pair_scores,
    payload_projection,
    sigmoid_projection,
    final_projection,
):
    row_count = lax.axis_size("row")
    col_count = lax.axis_size("col")
    seq_count = lax.axis_size("seq")
    row_pos = lax.axis_index("row")
    col_pos = lax.axis_index("col")
    seq_pos = lax.axis_index("seq")
    sequences, rows, features = layernormed_alignment.shape
    heads, _, columns = pair_scores.shape
    width = payload_projection.shape[1]
    dim = width // heads
    stretch = rows // col_count
    wide = sequences * features
    own = heads // seq_count
    group = sequences // STEPS
    side = row_count // 2
    core, plane, across = row_pos % 2, col_pos % 2, col_pos // 2
    place = jnp.stack([core, plane, across, seq_pos]).astype(jnp.int32)

    tokens = far(jnp.swapaxes(layernormed_alignment, 1, 2))
    cotangent = far(jnp.swapaxes(average_cotangent, 1, 2))
    scores = far(pair_scores)
    payload_w = far(payload_projection)
    gate_w = far(sigmoid_projection)
    final_w = far(final_projection.T)
    keep = lax.dynamic_slice_in_dim(residue_validity, col_pos * columns, columns, 0).reshape(1, columns)

    at = lambda x, core, y, z: (x * 2 + core) * col_count + y * 2 + z
    routes = [
        (at(a, z, b, z), at((b + 2 * a) % side, z, a, z))
        for a in range(side)
        for b in range(side)
        for z in range(2)
    ]
    mine = lax.ppermute(jnp.swapaxes(layernormed_alignment, 1, 2), ("row", "col"), routes)

    stats = call(
        stats_kernel,
        jax.ShapeDtypeStruct((col_count, 2 * heads, rows), F32),
        [scores, keep],
        moved=4 << 20,
    )
    stats = lax.all_to_all(stats, "col", 0, 0, tiled=True)

    by_lanes = pl.BlockSpec((heads, rows, group * dim), lambda i: (0, 0, i))
    d_att, gate_term, att_rows = call(
        gate_kernel,
        [
            pltpu.HBM((sequences, width, rows), BF16),
            pltpu.HBM((sequences, width, rows), BF16),
            pltpu.HBM((heads, rows, sequences * dim), BF16),
        ],
        [tokens, cotangent, far(sequence_validity), gate_w, final_w],
        [
            by_step(group, features, rows),
            by_step(group, features, rows),
            by_step(group, rows),
            whole((features, width)),
            whole((features, width)),
        ],
        [by_step(group, width, rows), by_step(group, width, rows), by_lanes],
        grid=(STEPS,),
        scratch=[pltpu.VMEM((2, width, features), BF16)],
        flops=1 << 30,
        moved=14 << 20,
    )
    mine, stats, d_att = lax.optimization_barrier((mine, stats, d_att))
    other = lax.ppermute(mine, "row", [(i, i ^ 1) for i in range(row_count)])

    message = wide + 256
    pieces = pltpu.VMEM((group, width, rows), BF16)
    square = pltpu.VMEM((heads, rows, columns), F32)
    weights, col_term, *sent = call(
        main_kernel,
        [jax.ShapeDtypeStruct((own, rows, columns), F32), jax.ShapeDtypeStruct((row_count, stretch, wide), BF16)]
        + [jax.ShapeDtypeStruct((2, stretch, message), BF16)] * side
        + [jax.ShapeDtypeStruct((own + 1, rows, 128), BF16)] * seq_count,
        [scores, keep, stats, far(d_att), far(gate_term), far(att_rows), mine, other, payload_w, gate_w],
        [
            whole((heads, rows, columns)),
            whole((1, columns)),
            whole((col_count, 2 * heads, rows)),
            by_step(group, width, rows),
            by_step(group, width, rows),
            by_lanes,
            whole((sequences, features, rows)),
            whole((sequences, features, rows)),
            whole((features, width)),
            whole((features, width)),
        ],
        [whole((own, rows, columns)), whole((row_count, stretch, wide))]
        + [whole((2, stretch, message)) for _ in range(side)]
        + [whole((own + 1, rows, 128)) for _ in range(seq_count)],
        grid=(STEPS,),
        scratch=[
            pltpu.VMEM((width, features), BF16),
            square,
            pltpu.VMEM((heads, rows, columns), BF16),
            pltpu.VMEM((heads, columns, rows), BF16),
            pieces,
            pieces,
            pieces,
            pltpu.VMEM((col_count, stretch, wide), BF16),
            square,
            pltpu.VMEM((seq_count, own + 1, rows, 128), BF16),
        ],
        scalars=place,
        flops=1 << 30,
        moved=18 << 20,
    )
    row_term, d_weights = sent[:side], sent[side:]

    def swapped(a, axis, bits):
        return lax.ppermute(a, axis, [(i, i ^ bits) for i in range(lax.axis_size(axis))])

    row_term = row_term[:1] + [swapped(row_term[k], "col", 2 * k) for k in range(1, side)]
    d_weights = d_weights[:1] + [swapped(d_weights[k], "seq", k) for k in range(1, seq_count)]
    col_term = lax.all_to_all(col_term, "row", 0, 0, tiled=True)
    col_term = jnp.sum(col_term.astype(F32), axis=0).astype(BF16)
    col_term = lax.ppermute(
        col_term,
        ("row", "col"),
        [(r * col_count + c, c * col_count + r) for r in range(row_count) for c in range(col_count)],
    )
    row_keep, inner, row_send = call(
        fold_kernel,
        [
            jax.ShapeDtypeStruct((stretch, wide), F32),
            jax.ShapeDtypeStruct((heads, 256), F32),
            jax.ShapeDtypeStruct((stretch, message), BF16),
        ],
        row_term,
        scalars=place,
        moved=2 << 20,
    )
    row_send = swapped(row_send, "col", 1)
    inner = call(inner_kernel, jax.ShapeDtypeStruct((heads, 256), F32), [inner, row_send], moved=1 << 20)
    inners = [inner] + [swapped(inner, "seq", k) for k in range(1, seq_count)]
    score_cotangent = call(
        score_kernel,
        jax.ShapeDtypeStruct((own, rows, columns), F32),
        d_weights + inners + [weights],
        scalars=place,
        moved=2 << 20,
    )
    alignment_cotangent = call(
        join_kernel,
        jax.ShapeDtypeStruct((sequences, stretch, features), F32),
        [row_keep, row_send, col_term],
        moved=2 << 20,
    )
    return (alignment_cotangent, score_cotangent)


def solution(mesh):
    return jax.shard_map(
        body,
        mesh=mesh,
        in_specs=(
            P("seq", "row", None),
            P("seq", "row", None),
            P("seq", "row"),
            P(),
            P(None, "row", "col"),
            P(),
            P(),
            P(),
        ),
        out_specs=(P("seq", ("row", "col"), None), P("seq", "row", "col")),
        check_vma=False,
    )
```

time: 105 us -> 88.5 us (0.84)
  starting transfers between devices: 53.4 us -> 38.4 us
  Pallas kernels: 33.6 us -> 27.9 us
  waiting for transfers between devices: 14.3 us -> 17.2 us
  local copies, waits for them, and re-layouts: 0.78 us -> 3.43 us
  other arithmetic: 1.33 us -> 0.19 us
    ppermute x14 -> x10, starting transfers between devices: 33.2 us -> 19 us  [swapped(): lax.ppermute(a, axis, [(i, i ^ bits) for i in range(lax.axis_size(axis))])]
    pallas_call x7, Pallas kernels: 33.6 us -> 27.9 us  [call(): pl.pallas_call(kernel, out_shape=outs, in_specs=[pl.BlockSpec(memory_spac...]
    unnamed x0 -> x8, local copies, waits for them, and re-layouts: none -> 2.65 us
    ppermute x1, waiting for transfers between devices: 0.01 us -> 2.33 us  [body(): other = lax.ppermute(mine, 'row', [(i, i ^ 1) for i in range(row_count)])]
    ppermute x1, waiting for transfers between devices: 1.81 us -> 0.01 us  [body(): lax.ppermute(col_term, ('row', 'col'), [(r * col_count + c, c * col_count...]
    ppermute x14 -> x10, waiting for transfers between devices: 9.76 us -> 11.6 us  [swapped(): lax.ppermute(a, axis, [(i, i ^ bits) for i in range(lax.axis_size(axis))])]
    reduce_sum x1, other arithmetic: 1.25 us -> 0.11 us  [body(): col_term = jnp.sum(col_term.astype(F32), axis=0).astype(BF16)]
  transfers between devices with their start and end apart: 19 -> 15, of which waited for: 5 -> 8; matrix products, arithmetic and copies ran while one was open for 1% -> 1% of each run, Pallas kernels for 28% -> 15%
where the time goes in v2:
time: 88.5 us; the launch traced here: 87.8 us
  starting transfers between devices  38.4 us (43%)
  Pallas kernels  27.9 us (32%)
  waiting for transfers between devices  17.2 us (19%)
  local copies, waits for them, and re-layouts  3.43 us (4%)
    pallas_call x7, Pallas kernels, call(): pl.pallas_call(kernel, out_shape=outs, in_specs=[pl.BlockSpec(memory_spac...  27.9 us
    ppermute x10, starting transfers between devices, swapped(): lax.ppermute(a, axis, [(i, i ^ bits) for i in range(lax.axis_size(axis))])  19 us
    ppermute x10, waiting for transfers between devices, swapped(): lax.ppermute(a, axis, [(i, i ^ bits) for i in range(lax.axis_size(axis))])  11.6 us
    all_to_all x1, starting transfers between devices, body(): stats = lax.all_to_all(stats, 'col', 0, 0, tiled=True)  7.41 us
    all_to_all x1, starting transfers between devices, body(): col_term = lax.all_to_all(col_term, 'row', 0, 0, tiled=True)  5.41 us
    ppermute x1, starting transfers between devices, body(): lax.ppermute(jnp.swapaxes(layernormed_alignment, 1, 2), ('row', 'col'), r...  4.41 us
    all_to_all x1, waiting for transfers between devices, body(): stats = lax.all_to_all(stats, 'col', 0, 0, tiled=True)  3.35 us
    unnamed x8, local copies, waits for them, and re-layouts  2.65 us
  transfers between devices with their start and end apart: 15, of which 8 were waited for; matrix products, arithmetic and copies ran while one was open for 1% of the time, Pallas kernels for 15%

profile of v2, /device:TPU:2, one launch (start us, length us, event | category | flops | bytes accessed | tf_op | source)
XLA Modules:
  0.0 87.8 jit_solution(16471320946060567616)
XLA Ops:
  0.6 4.4 %collective-permute-start = (bf16[32,64,192]{2,1,0:T(8,128)(2,1)}, bf16[32,64,192]{2,1,0:T(8,128)(2,1)S(1)}, u32[]{:S(2)}, u32[]{:S(2)}) collective-permute-start(bf16[32,64,192]{2,1,0:T(8,128)(2,1)} %bitcast.11), channel_id=1, source_target_pairs={{0,0},{9,9},{2,16},{11,25},{4,32},{13,41},{6,48},{15,57},{16,34},{... | collective-permute-start | bytes 2359304 | tf_op jit(solution)/shard_map/ppermute | solution.py:315
  5.1 0.8 dynamic_slice.3
  5.8 2.9 %shard_map.95 = f32[8,16,192]{2,1,0:T(8,128)} custom-call(f32[8,192,192]{2,1,0:T(8,128)} %scores_ref.3, s32[1,192]{1,0:T(1,128)S(1)} %bitcast.8), custom_call_target="tpu_custom_call" | custom-call | bytes 4194304 | tf_op jit(solution)/shard_map/pallas_call | solution.py:24
  8.7 7.4 %all-to-all-start = ((f32[8,16,192]{2,1,0:T(8,128)}), f32[8,16,192]{2,1,0:T(8,128)S(1)}, u32[]{:S(2)}, u32[]{:S(2)}) async-start(f32[8,16,192]{2,1,0:T(8,128)} %shard_map.95), calls=%async_computation | async-start | bytes 262144 | tf_op jit(solution)/shard_map/all_to_all | solution.py:323
  16.2 7.6 %shard_map.96 = (bf16[32,256,192]{2,1,0:T(8,128)(2,1)}, bf16[32,256,192]{2,1,0:T(8,128)(2,1)}, bf16[8,192,1024]{2,1,0:T(8,128)(2,1)}) custom-call(bf16[32,64,192]{2,1,0:T(8,128)(2,1)} %bitcast.12, bf16[32,64,192]{2,1,0:T(8,128)(2,1)} %bitcast.10, s32[32,192]{1,0:T(8,128)} %mask_ref.1, bf16[64,256]{1,0:T(8,128)(2,1)} %gate_w_ref.3, bf16[64,256]{1,0:T(8,128)(2,1)} %bitcast.13), custom_call_target="tpu_custom_call" | custom-call | flops 1073741824 | bytes 14680064 | tf_op jit(solution)/shard_map/pallas_call | solution.py:24
  23.7 3.3 %all-to-all-done.stats_ref = f32[8,16,192]{2,1,0:T(8,128)S(1)} async-done(((f32[8,16,192]{2,1,0:T(8,128)}), f32[8,16,192]{2,1,0:T(8,128)S(1)}, u32[]{:S(2)}, u32[]{:S(2)}) %all-to-all-start) | async-done | bytes 98336 | tf_op jit(solution)/shard_map/all_to_all | solution.py:323
  27.1 0.0 collective-permute-done.mine_ref
  27.1 0.3 collective-permute-start.1
  27.3 0.1 pad_add_fusion.place_ref
  27.4 2.3 %collective-permute-done.1.other_ref = bf16[32,64,192]{2,1,0:T(8,128)(2,1)S(1)} collective-permute-done((bf16[32,64,192]{2,1,0:T(8,128)(2,1)S(1)}, bf16[32,64,192]{2,1,0:T(8,128)(2,1)S(1)}, u32[]{:S(2)}, u32[]{:S(2)}) %collective-permute-start.1) | collective-permute-done | bytes 786464 | tf_op jit(solution)/shard_map/ppermute | solution.py:348
  29.7 14.2 %shard_map.97 = (f32[2,192,192]{2,1,0:T(8,128)S(1)}, bf16[8,24,2048]{2,1,0:T(8,128)(2,1)}, bf16[2,24,2304]{2,1,0:T(8,128)(2,1)S(1)}, bf16[2,24,2304]{2,1,0:T(8,1...) custom-call(s32[4]{0:T(128)S(1)} %pad_add_fusion.place_ref, ...), custom_call_target="tpu_custom_call" | custom-call | flops 1073741824 | bytes 18874368 | tf_op jit(solution)/shard_map/pallas_call | solution.py:24
  44.0 0.0 copy-start
  44.0 0.7 copy-done
  44.7 0.0 copy-start.1
  44.7 0.7 copy-done.1
  45.3 0.0 copy-start.2
  45.3 0.7 copy-done.2
  46.0 0.0 copy-start.3
  46.0 0.7 copy-done.3
  46.6 5.4 %all-to-all-start.1 = ((bf16[8,24,2048]{2,1,0:T(8,128)(2,1)}), bf16[8,24,2048]{2,1,0:T(8,128)(2,1)S(1)}, u32[]{:S(2)}, u32[]{:S(2)}) async-start(bf16[8,24,2048]{2,1,0:T(8,128)(2,1)} %get-tuple-element.33), calls=%async_computation.1 | async-start | bytes 1572864 | tf_op jit(solution)/shard_map/all_to_all | solution.py:398
  52.0 0.4 collective-permute-start.2
  52.4 2.2 %collective-permute-start.3 = (bf16[2,24,2304]{2,1,0:T(8,128)(2,1)S(1)}, bf16[2,24,2304]{2,1,0:T(8,128)(2,1)S(1)}, u32[]{:S(2)}, u32[]{:S(2)}) collective-permute-start(bf16[2,24,2304]{2,1,0:T(8,128)(2,1)S(1)} %get-tuple-element.29), channel_id=1, source_target_pairs={{0,4},{1,5},{2,6},{3,7},{4,0},{5,1},{6,2},{7,3},{8,12},{9,13},{10,... | collective-permute-start | bytes 663560 | tf_op jit(solution)/shard_map/ppermute | solution.py:394
  54.7 2.1 %collective-permute-start.4 = (bf16[2,24,2304]{2,1,0:T(8,128)(2,1)S(1)}, bf16[2,24,2304]{2,1,0:T(8,128)(2,1)S(1)}, u32[]{:S(2)}, u32[]{:S(2)}) collective-permute-start(bf16[2,24,2304]{2,1,0:T(8,128)(2,1)S(1)} %get-tuple-element.30), channel_id=1, source_target_pairs={{0,6},{1,7},{2,4},{3,5},{4,2},{5,3},{6,0},{7,1},{8,14},{9,15},{10,... | collective-permute-start | bytes 663560 | tf_op jit(solution)/shard_map/ppermute | solution.py:394
  56.7 1.6 %collective-permute-start.7 = (bf16[3,192,128]{2,1,0:T(8,128)(2,1)}, bf16[3,192,128]{2,1,0:T(8,128)(2,1)S(1)}, u32[]{:S(2)}, u32[]{:S(2)}) collective-permute-start(bf16[3,192,128]{2,1,0:T(8,128)(2,1)} %copy-done.3), channel_id=1, source_target_pairs={{0,64},{64,0},{128,192},{192,128},{1,65},{65,1},{129,193},{193,129... | collective-permute-start | bytes 442376 | tf_op jit(solution)/shard_map/ppermute | solution.py:394
  58.4 0.9 collective-permute-start.8
  59.2 1.3 %collective-permute-done.2.part1_ref = bf16[2,24,2304]{2,1,0:T(8,128)(2,1)S(1)} collective-permute-done((bf16[2,24,2304]{2,1,0:T(8,128)(2,1)}, bf16[2,24,2304]{2,1,0:T(8,128)(2,1)S(1)}, u32[]{:S(2)}, u32[]{:S(2)}) %collective-permute-start.2) | collective-permute-done | bytes 221216 | tf_op jit(solution)/shard_map/ppermute | solution.py:394
  60.5 1.9 %collective-permute-start.9 = (bf16[3,192,128]{2,1,0:T(8,128)(2,1)}, bf16[3,192,128]{2,1,0:T(8,128)(2,1)S(1)}, u32[]{:S(2)}, u32[]{:S(2)}) collective-permute-start(bf16[3,192,128]{2,1,0:T(8,128)(2,1)} %copy-done.1), channel_id=1, source_target_pairs={{0,192},{64,128},{128,64},{192,0},{1,193},{65,129},{129,65},{193,1... | collective-permute-start | bytes 442376 | tf_op jit(solution)/shard_map/ppermute | solution.py:394
  62.5 2.7 %collective-permute-done.3.part2_ref = bf16[2,24,2304]{2,1,0:T(8,128)(2,1)S(1)} collective-permute-done((bf16[2,24,2304]{2,1,0:T(8,128)(2,1)S(1)}, bf16[2,24,2304]{2,1,0:T(8,128)(2,1)S(1)}, u32[]{:S(2)}, u32[]{:S(2)}) %collective-permute-start.3) | collective-permute-done | bytes 221216 | tf_op jit(solution)/shard_map/ppermute | solution.py:394
  65.2 2.4 %collective-permute-done.4.part3_ref = bf16[2,24,2304]{2,1,0:T(8,128)(2,1)S(1)} collective-permute-done((bf16[2,24,2304]{2,1,0:T(8,128)(2,1)S(1)}, bf16[2,24,2304]{2,1,0:T(8,128)(2,1)S(1)}, u32[]{:S(2)}, u32[]{:S(2)}) %collective-permute-start.4) | collective-permute-done | bytes 221216 | tf_op jit(solution)/shard_map/ppermute | solution.py:394
  67.5 0.7 shard_map.98
  68.2 5.5 %collective-permute-start.5 = (bf16[24,2304]{1,0:T(8,128)(2,1)S(1)}, bf16[24,2304]{1,0:T(8,128)(2,1)S(1)}, u32[]{:S(2)}, u32[]{:S(2)}) collective-permute-start(bf16[24,2304]{1,0:T(8,128)(2,1)S(1)} %get-tuple-element.32), channel_id=1, source_target_pairs={{0,1},{1,0},{2,3},{3,2},{4,5},{5,4},{6,7},{7,6},{8,9},{9,8},{10,11... | collective-permute-start | bytes 331784 | tf_op jit(solution)/shard_map/ppermute | solution.py:394
  73.7 0.0 all-to-all-done.1
  73.7 0.1 reduce_sum.12
  73.8 1.9 %collective-permute-start.6 = (bf16[24,2048]{1,0:T(8,128)(2,1)S(1)}, bf16[24,2048]{1,0:T(8,128)(2,1)S(1)}, u32[]{:S(2)}, u32[]{:S(2)}) collective-permute-start(bf16[24,2048]{1,0:T(8,128)(2,1)S(1)} %reduce_sum.12), channel_id=1, source_target_pairs={{0,0},{1,8},{2,16},{3,24},{4,32},{5,40},{6,48},{7,56},{8,1},{9,9},... | collective-permute-start | bytes 294920 | tf_op jit(solution)/shard_map/ppermute | solution.py:400
  75.7 3.1 %collective-permute-done.5.rows_ref = bf16[24,2304]{1,0:T(8,128)(2,1)S(1)} collective-permute-done((bf16[24,2304]{1,0:T(8,128)(2,1)S(1)}, bf16[24,2304]{1,0:T(8,128)(2,1)S(1)}, u32[]{:S(2)}, u32[]{:S(2)}) %collective-permute-start.5) | collective-permute-done | bytes 110624 | tf_op jit(solution)/shard_map/ppermute | solution.py:394
  78.8 1.9 %collective-permute-start.12 = (f32[8,256]{1,0:T(8,128)S(1)}, f32[8,256]{1,0:T(8,128)S(1)}, u32[]{:S(2)}, u32[]{:S(2)}) collective-permute-start(f32[8,256]{1,0:T(8,128)S(1)} %shard_map.100.inner0_ref), channel_id=1, source_target_pairs={{0,192},{64,128},{128,64},{192,0},{1,193},{65,129},{129,65},{193,1... | collective-permute-start | bytes 24584 | tf_op jit(solution)/shard_map/ppermute | solution.py:394
  80.7 0.0 collective-permute-done.7.part1_ref
  80.7 0.7 collective-permute-start.11
  81.4 0.0 collective-permute-done.8.part2_ref
  81.4 1.8 %collective-permute-start.10 = (f32[8,256]{1,0:T(8,128)S(1)}, f32[8,256]{1,0:T(8,128)S(1)}, u32[]{:S(2)}, u32[]{:S(2)}) collective-permute-start(f32[8,256]{1,0:T(8,128)S(1)} %shard_map.100.inner0_ref), channel_id=1, source_target_pairs={{0,64},{64,0},{128,192},{192,128},{1,65},{65,1},{129,193},{193,129... | collective-permute-start | bytes 24584 | tf_op jit(solution)/shard_map/ppermute | solution.py:394
  83.2 0.0 collective-permute-done.9.part3_ref
  83.2 1.0 %collective-permute-done.12.inner3_ref = f32[8,256]{1,0:T(8,128)S(1)} collective-permute-done((f32[8,256]{1,0:T(8,128)S(1)}, f32[8,256]{1,0:T(8,128)S(1)}, u32[]{:S(2)}, u32[]{:S(2)}) %collective-permute-start.12) | collective-permute-done | bytes 8224 | tf_op jit(solution)/shard_map/ppermute | solution.py:394
  84.3 1.0 %collective-permute-done.11.inner2_ref = f32[8,256]{1,0:T(8,128)S(1)} collective-permute-done((f32[8,256]{1,0:T(8,128)S(1)}, f32[8,256]{1,0:T(8,128)S(1)}, u32[]{:S(2)}, u32[]{:S(2)}) %collective-permute-start.11) | collective-permute-done | bytes 8224 | tf_op jit(solution)/shard_map/ppermute | solution.py:394
  85.3 0.0 collective-permute-done.10.inner1_ref
  85.3 1.6 %shard_map.101 = f32[2,192,192]{2,1,0:T(8,128)} custom-call(s32[4]{0:T(128)S(1)} %pad_add_fusion.place_ref, bf16[3,192,128]{2,1,0:T(8,128)(2,1)S(1)} %get-tuple-element.34.part0_ref, bf16[3,192,128]{2,1,0:T(8,128)(2,1)S(1)} %collective-permute-done.7.part1_ref, bf16[3,192,128]{2,1,0:T(8,128)(2,1)S(1)} %collective-permute-done.8.part2_ref, ...), custom_call_target="tpu_custom_call" | custom-call | bytes 2097152 | tf_op jit(solution)/shard_map/pallas_call | solution.py:24
  86.9 0.0 collective-permute-done.6.cols_ref
  86.9 0.9 shard_map.99
  (1 shorter events, 0.0 us)
Async XLA Ops:
  0.6 26.5 %collective-permute-start = (bf16[32,64,192]{2,1,0:T(8,128)(2,1)}, bf16[32,64,192]{2,1,0:T(8,128)(2,1)S(1)}, u32[]{:S(2)}, u32[]{:S(2)}) collective-permute-start(bf16[32,64,192]{2,1,0:T(8,128)(2,1)} %bitcast.11), channel_id=1, source_target_pairs={{0,0},{9,9},{2,16},{11,25},{4,32},{13,41},{6,48},{15,57},{16,34},{... | collective-permute-start | bytes 2359304 | tf_op jit(solution)/shard_map/ppermute | solution.py:315
  8.7 18.3 %all-to-all-start = ((f32[8,16,192]{2,1,0:T(8,128)}), f32[8,16,192]{2,1,0:T(8,128)S(1)}, u32[]{:S(2)}, u32[]{:S(2)}) async-start(f32[8,16,192]{2,1,0:T(8,128)} %shard_map.95), calls=%async_computation | async-start | bytes 262144 | tf_op jit(solution)/shard_map/all_to_all | solution.py:323
  27.1 2.7 %collective-permute-start.1 = (bf16[32,64,192]{2,1,0:T(8,128)(2,1)S(1)}, bf16[32,64,192]{2,1,0:T(8,128)(2,1)S(1)}, u32[]{:S(2)}, u32[]{:S(2)}) collective-permute-start(bf16[32,64,192]{2,1,0:T(8,128)(2,1)S(1)} %collective-permute-done.mine_ref), channel_id=1, source_target_pairs={{0,8},{8,0},{16,24},{24,16},{32,40},{40,32},{48,56},{56,48},{1,9},... | collective-permute-start | bytes 2359304 | tf_op jit(solution)/shard_map/ppermute | solution.py:348
  44.0 0.7 copy-start
  44.7 0.7 copy-start.1
  45.3 0.7 copy-start.2
  46.0 0.7 copy-start.3
  46.6 27.0 %all-to-all-start.1 = ((bf16[8,24,2048]{2,1,0:T(8,128)(2,1)}), bf16[8,24,2048]{2,1,0:T(8,128)(2,1)S(1)}, u32[]{:S(2)}, u32[]{:S(2)}) async-start(bf16[8,24,2048]{2,1,0:T(8,128)(2,1)} %get-tuple-element.33), calls=%async_computation.1 | async-start | bytes 1572864 | tf_op jit(solution)/shard_map/all_to_all | solution.py:398
  52.0 8.5 %collective-permute-start.2 = (bf16[2,24,2304]{2,1,0:T(8,128)(2,1)}, bf16[2,24,2304]{2,1,0:T(8,128)(2,1)S(1)}, u32[]{:S(2)}, u32[]{:S(2)}) collective-permute-start(bf16[2,24,2304]{2,1,0:T(8,128)(2,1)} %copy-done), channel_id=1, source_target_pairs={{0,2},{1,3},{2,0},{3,1},{4,6},{5,7},{6,4},{7,5},{8,10},{9,11},{10,... | collective-permute-start | bytes 663560 | tf_op jit(solution)/shard_map/ppermute | solution.py:394
  52.4 12.7 %collective-permute-start.3 = (bf16[2,24,2304]{2,1,0:T(8,128)(2,1)S(1)}, bf16[2,24,2304]{2,1,0:T(8,128)(2,1)S(1)}, u32[]{:S(2)}, u32[]{:S(2)}) collective-permute-start(bf16[2,24,2304]{2,1,0:T(8,128)(2,1)S(1)} %get-tuple-element.29), channel_id=1, source_target_pairs={{0,4},{1,5},{2,6},{3,7},{4,0},{5,1},{6,2},{7,3},{8,12},{9,13},{10,... | collective-permute-start | bytes 663560 | tf_op jit(solution)/shard_map/ppermute | solution.py:394
  54.7 12.9 %collective-permute-start.4 = (bf16[2,24,2304]{2,1,0:T(8,128)(2,1)S(1)}, bf16[2,24,2304]{2,1,0:T(8,128)(2,1)S(1)}, u32[]{:S(2)}, u32[]{:S(2)}) collective-permute-start(bf16[2,24,2304]{2,1,0:T(8,128)(2,1)S(1)} %get-tuple-element.30), channel_id=1, source_target_pairs={{0,6},{1,7},{2,4},{3,5},{4,2},{5,3},{6,0},{7,1},{8,14},{9,15},{10,... | collective-permute-start | bytes 663560 | tf_op jit(solution)/shard_map/ppermute | solution.py:394
  56.7 24.0 %collective-permute-start.7 = (bf16[3,192,128]{2,1,0:T(8,128)(2,1)}, bf16[3,192,128]{2,1,0:T(8,128)(2,1)S(1)}, u32[]{:S(2)}, u32[]{:S(2)}) collective-permute-start(bf16[3,192,128]{2,1,0:T(8,128)(2,1)} %copy-done.3), channel_id=1, source_target_pairs={{0,64},{64,0},{128,192},{192,128},{1,65},{65,1},{129,193},{193,129... | collective-permute-start | bytes 442376 | tf_op jit(solution)/shard_map/ppermute | solution.py:394
  58.4 23.1 %collective-permute-start.8 = (bf16[3,192,128]{2,1,0:T(8,128)(2,1)}, bf16[3,192,128]{2,1,0:T(8,128)(2,1)S(1)}, u32[]{:S(2)}, u32[]{:S(2)}) collective-permute-start(bf16[3,192,128]{2,1,0:T(8,128)(2,1)} %copy-done.2), channel_id=1, source_target_pairs={{0,128},{64,192},{128,0},{192,64},{1,129},{65,193},{129,1},{193,65... | collective-permute-start | bytes 442376 | tf_op jit(solution)/shard_map/ppermute | solution.py:394
  60.5 22.7 %collective-permute-start.9 = (bf16[3,192,128]{2,1,0:T(8,128)(2,1)}, bf16[3,192,128]{2,1,0:T(8,128)(2,1)S(1)}, u32[]{:S(2)}, u32[]{:S(2)}) collective-permute-start(bf16[3,192,128]{2,1,0:T(8,128)(2,1)} %copy-done.1), channel_id=1, source_target_pairs={{0,192},{64,128},{128,64},{192,0},{1,193},{65,129},{129,65},{193,1... | collective-permute-start | bytes 442376 | tf_op jit(solution)/shard_map/ppermute | solution.py:394
  68.2 10.6 %collective-permute-start.5 = (bf16[24,2304]{1,0:T(8,128)(2,1)S(1)}, bf16[24,2304]{1,0:T(8,128)(2,1)S(1)}, u32[]{:S(2)}, u32[]{:S(2)}) collective-permute-start(bf16[24,2304]{1,0:T(8,128)(2,1)S(1)} %get-tuple-element.32), channel_id=1, source_target_pairs={{0,1},{1,0},{2,3},{3,2},{4,5},{5,4},{6,7},{7,6},{8,9},{9,8},{10,11... | collective-permute-start | bytes 331784 | tf_op jit(solution)/shard_map/ppermute | solution.py:394
  73.8 13.1 %collective-permute-start.6 = (bf16[24,2048]{1,0:T(8,128)(2,1)S(1)}, bf16[24,2048]{1,0:T(8,128)(2,1)S(1)}, u32[]{:S(2)}, u32[]{:S(2)}) collective-permute-start(bf16[24,2048]{1,0:T(8,128)(2,1)S(1)} %reduce_sum.12), channel_id=1, source_target_pairs={{0,0},{1,8},{2,16},{3,24},{4,32},{5,40},{6,48},{7,56},{8,1},{9,9},... | collective-permute-start | bytes 294920 | tf_op jit(solution)/shard_map/ppermute | solution.py:400
  78.8 5.4 %collective-permute-start.12 = (f32[8,256]{1,0:T(8,128)S(1)}, f32[8,256]{1,0:T(8,128)S(1)}, u32[]{:S(2)}, u32[]{:S(2)}) collective-permute-start(f32[8,256]{1,0:T(8,128)S(1)} %shard_map.100.inner0_ref), channel_id=1, source_target_pairs={{0,192},{64,128},{128,64},{192,0},{1,193},{65,129},{129,65},{193,1... | collective-permute-start | bytes 24584 | tf_op jit(solution)/shard_map/ppermute | solution.py:394
  80.7 4.6 %collective-permute-start.11 = (f32[8,256]{1,0:T(8,128)S(1)}, f32[8,256]{1,0:T(8,128)S(1)}, u32[]{:S(2)}, u32[]{:S(2)}) collective-permute-start(f32[8,256]{1,0:T(8,128)S(1)} %shard_map.100.inner0_ref), channel_id=1, source_target_pairs={{0,128},{64,192},{128,0},{192,64},{1,129},{65,193},{129,1},{193,65... | collective-permute-start | bytes 24584 | tf_op jit(solution)/shard_map/ppermute | solution.py:394
  81.4 3.9 %collective-permute-start.10 = (f32[8,256]{1,0:T(8,128)S(1)}, f32[8,256]{1,0:T(8,128)S(1)}, u32[]{:S(2)}, u32[]{:S(2)}) collective-permute-start(f32[8,256]{1,0:T(8,128)S(1)} %shard_map.100.inner0_ref), channel_id=1, source_target_pairs={{0,64},{64,0},{128,192},{192,128},{1,65},{65,1},{129,193},{193,129... | collective-permute-start | bytes 24584 | tf_op jit(solution)/shard_map/ppermute | solution.py:394

commit v3 on v2

--- a/solution.py
+++ b/solution.py
@@ -69,42 +69,15 @@
         stats_ref[k] = packed
 
 
-def gate_kernel(x_ref, cot_ref, mask_ref, gate_w_ref, final_w_ref, att_ref, term_ref, att_rows_ref, wt):
-    @pl.when(pl.program_id(0) == 0)
-    def _():
-        wt[0] = turned(gate_w_ref[...])
-        wt[1] = turned(final_w_ref[...])
-
-    sequences, _, rows = x_ref.shape
-    heads = att_rows_ref.shape[0]
-    dim = wt.shape[1] // heads
-    mask = mask_ref[...].astype(F32)
-    for s in range(sequences):
-        gate = 1.0 / (1.0 + jnp.exp(-dot(wt[0], x_ref[s])))
-        cot = dot(wt[1], cot_ref[s]) * mask[s : s + 1]
-        att = cot * gate
-        att_ref[s] = att.astype(BF16)
-        term_ref[s] = (att * (1.0 - gate)).astype(BF16)
-    for h in range(heads):
-        block = att_ref[:, h * dim : (h + 1) * dim, :].reshape(sequences * dim, rows)
-        att_rows_ref[h] = turned(block)
-
-
-def project_rows(weight, hi, lo, out_ref, first):
-    sequences = hi.shape[0]
+def project_rows(weight, pieces, out_ref, first):
+    sequences = pieces.shape[0]
     chunks, stretch, _ = out_ref.shape
     features = weight.shape[0]
     for s in range(0, sequences, 2):
-        pair = [dot(weight, hi[s + k]) + dot(weight, lo[s + k]) for k in (0, 1)]
+        pair = [dot(weight, pieces[s + k]) for k in (0, 1)]
         rows = jnp.concatenate(pair, axis=0).T.reshape(chunks, stretch, 2 * features)
         lanes = pl.ds(pl.multiple_of((first + s) * features, 128), 2 * features)
         out_ref[:, :, lanes] = rows.astype(out_ref.dtype)
-
-
-def split(grad, hi, lo, h, dim):
-    top = grad.astype(BF16)
-    hi[:, h * dim : (h + 1) * dim, :] = top
-    lo[:, h * dim : (h + 1) * dim, :] = (grad - top.astype(F32)).astype(BF16)
 
 
 def thirds(table):
@@ -126,13 +99,14 @@
     scores_ref,
     keep_ref,
     stats_ref,
-    att_ref,
-    term_ref,
-    att_rows_ref,
+    x_ref,
+    cot_ref,
+    mask_ref,
     mine_ref,
     other_ref,
     payload_ref,
     gate_w_ref,
+    final_w_ref,
     weights_ref,
     col_ref,
     row0_ref,
@@ -147,22 +121,25 @@
     weights,
     wb,
     turned_wb,
+    att,
+    term,
     values,
-    hi,
-    lo,
+    pieces,
     row_out,
     pair_sum,
     pair_out,
 ):
     step = pl.program_id(0)
     heads, rows, columns = scores_ref.shape
-    group, width, _ = att_ref.shape
+    group = x_ref.shape[0]
+    width = payload_ref.shape[1]
     dim = width // heads
     wide = col_ref.shape[2]
 
     @pl.when(step == 0)
     def _():
-        wt[...] = turned(payload_ref[...])
+        for k, weight in enumerate((payload_ref, gate_w_ref, final_w_ref)):
+            wt[k] = turned(weight[...])
         pair_sum[...] = jnp.zeros(pair_sum.shape, F32)
         peaks = stats_ref[:, 0:heads]
         peak = jnp.max(peaks, axis=0)
@@ -177,21 +154,29 @@
             turned_wb[h] = exact.T.astype(BF16)
 
     first = pl.multiple_of(step * group, group)
+    mask = mask_ref[...].astype(F32)
+    for k in range(group):
+        gate = 1.0 / (1.0 + jnp.exp(-dot(wt[1], x_ref[k])))
+        cot = dot(wt[2], cot_ref[k]) * mask[k : k + 1]
+        exact = cot * gate
+        att[k] = exact.astype(BF16)
+        term[k] = exact * (1.0 - gate)
     for h in range(heads):
-        block = att_ref[:, h * dim : (h + 1) * dim, :].reshape(group * dim, rows)
-        split(dot(block, wb[h]).reshape(group, dim, columns), hi, lo, h, dim)
-    project_rows(payload_ref[...], hi, lo, col_ref, first)
-
-    own = place_ref[0] == place_ref[1]
+        block = att[:, h * dim : (h + 1) * dim, :].reshape(group * dim, rows)
+        pieces[:, h * dim : (h + 1) * dim, :] = dot(block, wb[h]).astype(BF16).reshape(group, dim, columns)
+    project_rows(payload_ref[...], pieces, col_ref, first)
+
+    own = place_ref[0] != place_ref[1]
     tokens = jnp.where(own, mine_ref[pl.ds(first, group)], other_ref[pl.ds(first, group)])
     for k in range(group):
-        values[k] = dot(wt[...], tokens[k]).astype(BF16)
+        values[k] = dot(wt[0], tokens[k]).astype(BF16)
     for h in range(heads):
         block = values[:, h * dim : (h + 1) * dim, :].reshape(group * dim, columns)
         average = dot(block, turned_wb[h]).reshape(group, dim, rows)
-        split(average * term_ref[:, h * dim : (h + 1) * dim, :].astype(F32), hi, lo, h, dim)
-        pair_sum[h] += dot(att_rows_ref[h], block)
-    project_rows(gate_w_ref[...], hi, lo, row_out, first)
+        pieces[:, h * dim : (h + 1) * dim, :] = (average * term[:, h * dim : (h + 1) * dim, :]).astype(BF16)
+        att_rows = turned(att[:, h * dim : (h + 1) * dim, :].reshape(group * dim, rows))
+        pair_sum[h] += dot(att_rows, block)
+    project_rows(gate_w_ref[...], pieces, row_out, first)
 
     @pl.when(step == pl.num_programs(0) - 1)
     def _():
@@ -307,44 +292,22 @@
 
     at = lambda x, core, y, z: (x * 2 + core) * col_count + y * 2 + z
     routes = [
-        (at(a, z, b, z), at((b + 2 * a) % side, z, a, z))
+        (at(a, z, b, z), at((b + 2 * a) % side, 1 - z, a, z))
         for a in range(side)
         for b in range(side)
         for z in range(2)
     ]
     mine = lax.ppermute(jnp.swapaxes(layernormed_alignment, 1, 2), ("row", "col"), routes)
 
-    stats = call(
+    local_stats = call(
         stats_kernel,
         jax.ShapeDtypeStruct((col_count, 2 * heads, rows), F32),
         [scores, keep],
         moved=4 << 20,
     )
-    stats = lax.all_to_all(stats, "col", 0, 0, tiled=True)
-
-    by_lanes = pl.BlockSpec((heads, rows, group * dim), lambda i: (0, 0, i))
-    d_att, gate_term, att_rows = call(
-        gate_kernel,
-        [
-            pltpu.HBM((sequences, width, rows), BF16),
-            pltpu.HBM((sequences, width, rows), BF16),
-            pltpu.HBM((heads, rows, sequences * dim), BF16),
-        ],
-        [tokens, cotangent, far(sequence_validity), gate_w, final_w],
-        [
-            by_step(group, features, rows),
-            by_step(group, features, rows),
-            by_step(group, rows),
-            whole((features, width)),
-            whole((features, width)),
-        ],
-        [by_step(group, width, rows), by_step(group, width, rows), by_lanes],
-        grid=(STEPS,),
-        scratch=[pltpu.VMEM((2, width, features), BF16)],
-        flops=1 << 30,
-        moved=14 << 20,
-    )
-    mine, stats, d_att = lax.optimization_barrier((mine, stats, d_att))
+    stats = lax.all_to_all(local_stats, "col", 0, 0, tiled=True)
+
+    mine, stats = lax.optimization_barrier((mine, stats))
     other = lax.ppermute(mine, "row", [(i, i ^ 1) for i in range(row_count)])
 
     message = wide + 256
@@ -353,18 +316,20 @@
     weights, col_term, *sent = call(
         main_kernel,
         [jax.ShapeDtypeStruct((own, rows, columns), F32), jax.ShapeDtypeStruct((row_count, stretch, wide), BF16)]
-        + [jax.ShapeDtypeStruct((2, stretch, message), BF16)] * side
+        + [jax.ShapeDtypeStruct((2, stretch, message), BF16)]
+        + [pltpu.HBM((2, stretch, message), BF16)] * (side - 1)
         + [jax.ShapeDtypeStruct((own + 1, rows, 128), BF16)] * seq_count,
-        [scores, keep, stats, far(d_att), far(gate_term), far(att_rows), mine, other, payload_w, gate_w],
+        [scores, keep, stats, tokens, cotangent, far(sequence_validity), mine, other, payload_w, gate_w, final_w],
         [
             whole((heads, rows, columns)),
             whole((1, columns)),
             whole((col_count, 2 * heads, rows)),
-            by_step(group, width, rows),
-            by_step(group, width, rows),
-            by_lanes,
+            by_step(group, features, rows),
+            by_step(group, features, rows),
+            by_step(group, rows),
             whole((sequences, features, rows)),
             whole((sequences, features, rows)),
+            whole((features, width)),
             whole((features, width)),
             whole((features, width)),
         ],
@@ -373,11 +338,12 @@
         + [whole((own + 1, rows, 128)) for _ in range(seq_count)],
         grid=(STEPS,),
         scratch=[
-            pltpu.VMEM((width, features), BF16),
+            pltpu.VMEM((3, width, features), BF16),
             square,
             pltpu.VMEM((heads, rows, columns), BF16),
             pltpu.VMEM((heads, columns, rows), BF16),
             pieces,
+            pltpu.VMEM((group, width, rows), F32),
             pieces,
             pieces,
             pltpu.VMEM((col_count, stretch, wide), BF16),

time: 88.5 us -> 86.1 us (0.973)
  blocking collectives: 0 us -> 19.1 us
  starting transfers between devices: 38.4 us -> 27.9 us
  Pallas kernels: 27.9 us -> 20.3 us
  local copies, waits for them, and re-layouts: 3.43 us -> 0.79 us
    all_to_all x0 -> x1, blocking collectives: none -> 19.1 us  [body(): stats = lax.all_to_all(local_stats, 'col', 0, 0, tiled=True)]
    pallas_call x7 -> x6, Pallas kernels: 27.9 us -> 20.3 us  [call(): pl.pallas_call(kernel, out_shape=outs, in_specs=[pl.BlockSpec(memory_spac...]
    all_to_all x1 -> x0, starting transfers between devices: 7.41 us -> none  [body(): stats = lax.all_to_all(stats, 'col', 0, 0, tiled=True)]
    all_to_all x1 -> x0, waiting for transfers between devices: 3.35 us -> none  [body(): stats = lax.all_to_all(stats, 'col', 0, 0, tiled=True)]
    ppermute x10, waiting for transfers between devices: 11.6 us -> 14.6 us  [swapped(): lax.ppermute(a, axis, [(i, i ^ bits) for i in range(lax.axis_size(axis))])]
    ppermute x10, starting transfers between devices: 19 us -> 16 us  [swapped(): lax.ppermute(a, axis, [(i, i ^ bits) for i in range(lax.axis_size(axis))])]
    unnamed x8 -> x6, local copies, waits for them, and re-layouts: 2.65 us -> 0.01 us
  transfers between devices with their start and end apart: 15 -> 14, of which waited for: 8 -> 8; matrix products, arithmetic and copies ran while one was open for 1% -> 1% of each run, Pallas kernels for 15% -> 5%
where the time goes in v3:
time: 86.1 us; the launch traced here: 85.8 us
  starting transfers between devices  27.9 us (32%)
  Pallas kernels  20.3 us (24%)
  blocking collectives  19.1 us (22%)
  waiting for transfers between devices  16.9 us (20%)
    pallas_call x6, Pallas kernels, call(): pl.pallas_call(kernel, out_shape=outs, in_specs=[pl.BlockSpec(memory_spac...  20.3 us
    all_to_all x1, blocking collectives, body(): stats = lax.all_to_all(local_stats, 'col', 0, 0, tiled=True)  19.1 us
    ppermute x10, starting transfers between devices, swapped(): lax.ppermute(a, axis, [(i, i ^ bits) for i in range(lax.axis_size(axis))])  16 us
    ppermute x10, waiting for transfers between devices, swapped(): lax.ppermute(a, axis, [(i, i ^ bits) for i in range(lax.axis_size(axis))])  14.6 us
    all_to_all x1, starting transfers between devices, body(): col_term = lax.all_to_all(col_term, 'row', 0, 0, tiled=True)  5.67 us
    ppermute x1, starting transfers between devices, body(): lax.ppermute(jnp.swapaxes(layernormed_alignment, 1, 2), ('row', 'col'), r...  3.92 us
    ppermute x1, waiting for transfers between devices, body(): other = lax.ppermute(mine, 'row', [(i, i ^ 1) for i in range(row_count)])  2.23 us
    ppermute x1, starting transfers between devices, body(): lax.ppermute(col_term, ('row', 'col'), [(r * col_count + c, c * col_count...  1.92 us
  transfers between devices with their start and end apart: 14, of which 8 were waited for; matrix products, arithmetic and copies ran while one was open for 1% of the time, Pallas kernels for 5%

profile of v3, /device:TPU:2, one launch (start us, length us, event | category | flops | bytes accessed | tf_op | source)
XLA Modules:
  0.0 85.8 jit_solution(12565335192212868144)
XLA Ops:
  0.6 3.9 %collective-permute-start = (bf16[32,64,192]{2,1,0:T(8,128)(2,1)}, bf16[32,64,192]{2,1,0:T(8,128)(2,1)S(1)}, u32[]{:S(2)}, u32[]{:S(2)}) collective-permute-start(bf16[32,64,192]{2,1,0:T(8,128)(2,1)} %bitcast.10), channel_id=1, source_target_pairs={{0,8},{9,1},{2,24},{11,17},{4,40},{13,33},{6,56},{15,49},{16,42},{... | collective-permute-start | bytes 2359304 | tf_op jit(solution)/shard_map/ppermute | solution.py:300
  4.6 0.8 dynamic_slice.3
  5.3 2.3 %shard_map.95 = f32[8,16,192]{2,1,0:T(8,128)S(1)} custom-call(f32[8,192,192]{2,1,0:T(8,128)} %scores_ref.3, s32[1,192]{1,0:T(1,128)S(1)} %bitcast.8), custom_call_target="tpu_custom_call" | custom-call | bytes 4194304 | tf_op jit(solution)/shard_map/pallas_call | solution.py:24
  7.6 19.1 %all_to_all.10.stats_ref = f32[8,16,192]{2,1,0:T(8,128)S(1)} all-to-all(f32[8,16,192]{2,1,0:T(8,128)S(1)} %shard_map.95), channel_id=1, replica_groups=mesh['seq'=4,'row'=8,'col'=8] {'col'}, dimensions={0} | all-to-all | bytes 196608 | tf_op jit(solution)/shard_map/all_to_all | solution.py:308
  26.7 0.0 collective-permute-done.mine_ref
  26.7 0.4 collective-permute-start.1
  27.1 0.1 pad_add_fusion.place_ref
  27.1 2.2 %collective-permute-done.1.other_ref = bf16[32,64,192]{2,1,0:T(8,128)(2,1)S(1)} collective-permute-done((bf16[32,64,192]{2,1,0:T(8,128)(2,1)S(1)}, bf16[32,64,192]{2,1,0:T(8,128)(2,1)S(1)}, u32[]{:S(2)}, u32[]{:S(2)}) %collective-permute-start.1) | collective-permute-done | bytes 786464 | tf_op jit(solution)/shard_map/ppermute | solution.py:311
  29.4 14.8 %shard_map.96 = (f32[2,192,192]{2,1,0:T(8,128)S(1)}, bf16[8,24,2048]{2,1,0:T(8,128)(2,1)}, bf16[2,24,2304]{2,1,0:T(8,128)(2,1)S(1)}, bf16[2,24,2304]{2,1,0:T(8,1...) custom-call(s32[4]{0:T(128)S(1)} %pad_add_fusion.place_ref, ...), custom_call_target="tpu_custom_call" | custom-call | flops 1073741824 | bytes 18874368 | tf_op jit(solution)/shard_map/pallas_call | solution.py:24
  44.2 0.0 copy-start.2
  44.2 0.0 copy-start.1
  44.2 0.0 copy-start
  44.2 5.7 %all-to-all-start.1 = ((bf16[8,24,2048]{2,1,0:T(8,128)(2,1)}), bf16[8,24,2048]{2,1,0:T(8,128)(2,1)S(1)}, u32[]{:S(2)}, u32[]{:S(2)}) async-start(bf16[8,24,2048]{2,1,0:T(8,128)(2,1)} %get-tuple-element.25), calls=%async_computation.1 | async-start | bytes 1572864 | tf_op jit(solution)/shard_map/all_to_all | solution.py:364
  49.9 0.0 copy-done.2
  49.9 0.4 collective-permute-start.2
  50.3 0.0 copy-done.1
  50.3 2.1 %collective-permute-start.3 = (bf16[2,24,2304]{2,1,0:T(8,128)(2,1)S(1)}, bf16[2,24,2304]{2,1,0:T(8,128)(2,1)S(1)}, u32[]{:S(2)}, u32[]{:S(2)}) collective-permute-start(bf16[2,24,2304]{2,1,0:T(8,128)(2,1)S(1)} %copy-done.1), channel_id=1, source_target_pairs={{0,4},{1,5},{2,6},{3,7},{4,0},{5,1},{6,2},{7,3},{8,12},{9,13},{10,... | collective-permute-start | bytes 663560 | tf_op jit(solution)/shard_map/ppermute | solution.py:360
  52.4 0.0 copy-done
  52.4 2.2 %collective-permute-start.4 = (bf16[2,24,2304]{2,1,0:T(8,128)(2,1)S(1)}, bf16[2,24,2304]{2,1,0:T(8,128)(2,1)S(1)}, u32[]{:S(2)}, u32[]{:S(2)}) collective-permute-start(bf16[2,24,2304]{2,1,0:T(8,128)(2,1)S(1)} %copy-done), channel_id=1, source_target_pairs={{0,6},{1,7},{2,4},{3,5},{4,2},{5,3},{6,0},{7,1},{8,14},{9,15},{10,... | collective-permute-start | bytes 663560 | tf_op jit(solution)/shard_map/ppermute | solution.py:360
  54.6 1.6 %collective-permute-start.7 = (bf16[3,192,128]{2,1,0:T(8,128)(2,1)S(1)}, bf16[3,192,128]{2,1,0:T(8,128)(2,1)S(1)}, u32[]{:S(2)}, u32[]{:S(2)}) collective-permute-start(bf16[3,192,128]{2,1,0:T(8,128)(2,1)S(1)} %get-tuple-element.27), channel_id=1, source_target_pairs={{0,64},{64,0},{128,192},{192,128},{1,65},{65,1},{129,193},{193,129... | collective-permute-start | bytes 442376 | tf_op jit(solution)/shard_map/ppermute | solution.py:360
  56.2 0.9 %collective-permute-start.8 = (bf16[3,192,128]{2,1,0:T(8,128)(2,1)S(1)}, bf16[3,192,128]{2,1,0:T(8,128)(2,1)S(1)}, u32[]{:S(2)}, u32[]{:S(2)}) collective-permute-start(bf16[3,192,128]{2,1,0:T(8,128)(2,1)S(1)} %get-tuple-element.28), channel_id=1, source_target_pairs={{0,128},{64,192},{128,0},{192,64},{1,129},{65,193},{129,1},{193,65... | collective-permute-start | bytes 442376 | tf_op jit(solution)/shard_map/ppermute | solution.py:360
  57.1 1.1 %collective-permute-done.2.part1_ref = bf16[2,24,2304]{2,1,0:T(8,128)(2,1)S(1)} collective-permute-done((bf16[2,24,2304]{2,1,0:T(8,128)(2,1)S(1)}, bf16[2,24,2304]{2,1,0:T(8,128)(2,1)S(1)}, u32[]{:S(2)}, u32[]{:S(2)}) %collective-permute-start.2) | collective-permute-done | bytes 221216 | tf_op jit(solution)/shard_map/ppermute | solution.py:360
  58.2 1.9 %collective-permute-start.9 = (bf16[3,192,128]{2,1,0:T(8,128)(2,1)S(1)}, bf16[3,192,128]{2,1,0:T(8,128)(2,1)S(1)}, u32[]{:S(2)}, u32[]{:S(2)}) collective-permute-start(bf16[3,192,128]{2,1,0:T(8,128)(2,1)S(1)} %get-tuple-element.29), channel_id=1, source_target_pairs={{0,192},{64,128},{128,64},{192,0},{1,193},{65,129},{129,65},{193,1... | collective-permute-start | bytes 442376 | tf_op jit(solution)/shard_map/ppermute | solution.py:360
  60.1 2.6 %collective-permute-done.3.part2_ref = bf16[2,24,2304]{2,1,0:T(8,128)(2,1)S(1)} collective-permute-done((bf16[2,24,2304]{2,1,0:T(8,128)(2,1)S(1)}, bf16[2,24,2304]{2,1,0:T(8,128)(2,1)S(1)}, u32[]{:S(2)}, u32[]{:S(2)}) %collective-permute-start.3) | collective-permute-done | bytes 221216 | tf_op jit(solution)/shard_map/ppermute | solution.py:360
  62.7 2.6 %collective-permute-done.4.part3_ref = bf16[2,24,2304]{2,1,0:T(8,128)(2,1)S(1)} collective-permute-done((bf16[2,24,2304]{2,1,0:T(8,128)(2,1)S(1)}, bf16[2,24,2304]{2,1,0:T(8,128)(2,1)S(1)}, u32[]{:S(2)}, u32[]{:S(2)}) %collective-permute-start.4) | collective-permute-done | bytes 221216 | tf_op jit(solution)/shard_map/ppermute | solution.py:360
  65.2 0.7 shard_map.97
  65.9 2.5 %collective-permute-start.5 = (bf16[24,2304]{1,0:T(8,128)(2,1)S(1)}, bf16[24,2304]{1,0:T(8,128)(2,1)S(1)}, u32[]{:S(2)}, u32[]{:S(2)}) collective-permute-start(bf16[24,2304]{1,0:T(8,128)(2,1)S(1)} %get-tuple-element.24), channel_id=1, source_target_pairs={{0,1},{1,0},{2,3},{3,2},{4,5},{5,4},{6,7},{7,6},{8,9},{9,8},{10,11... | collective-permute-start | bytes 331784 | tf_op jit(solution)/shard_map/ppermute | solution.py:360
  68.4 0.0 all-to-all-done.1
  68.4 0.1 reduce_sum.12
  68.5 1.9 %collective-permute-start.6 = (bf16[24,2048]{1,0:T(8,128)(2,1)S(1)}, bf16[24,2048]{1,0:T(8,128)(2,1)S(1)}, u32[]{:S(2)}, u32[]{:S(2)}) collective-permute-start(bf16[24,2048]{1,0:T(8,128)(2,1)S(1)} %reduce_sum.12), channel_id=1, source_target_pairs={{0,0},{1,8},{2,16},{3,24},{4,32},{5,40},{6,48},{7,56},{8,1},{9,9},... | collective-permute-start | bytes 294920 | tf_op jit(solution)/shard_map/ppermute | solution.py:366
  70.5 5.1 %collective-permute-done.5.rows_ref = bf16[24,2304]{1,0:T(8,128)(2,1)S(1)} collective-permute-done((bf16[24,2304]{1,0:T(8,128)(2,1)S(1)}, bf16[24,2304]{1,0:T(8,128)(2,1)S(1)}, u32[]{:S(2)}, u32[]{:S(2)}) %collective-permute-start.5) | collective-permute-done | bytes 110624 | tf_op jit(solution)/shard_map/ppermute | solution.py:360
  75.6 1.1 %collective-permute-start.12 = (f32[8,256]{1,0:T(8,128)S(1)}, f32[8,256]{1,0:T(8,128)S(1)}, u32[]{:S(2)}, u32[]{:S(2)}) collective-permute-start(f32[8,256]{1,0:T(8,128)S(1)} %shard_map.99.inner0_ref), channel_id=1, source_target_pairs={{0,192},{64,128},{128,64},{192,0},{1,193},{65,129},{129,65},{193,1... | collective-permute-start | bytes 24584 | tf_op jit(solution)/shard_map/ppermute | solution.py:360
  76.7 0.0 collective-permute-done.7.part1_ref
  76.7 2.9 %collective-permute-start.11 = (f32[8,256]{1,0:T(8,128)S(1)}, f32[8,256]{1,0:T(8,128)S(1)}, u32[]{:S(2)}, u32[]{:S(2)}) collective-permute-start(f32[8,256]{1,0:T(8,128)S(1)} %shard_map.99.inner0_ref), channel_id=1, source_target_pairs={{0,128},{64,192},{128,0},{192,64},{1,129},{65,193},{129,1},{193,65... | collective-permute-start | bytes 24584 | tf_op jit(solution)/shard_map/ppermute | solution.py:360
  79.6 0.0 collective-permute-done.8.part2_ref
  79.6 0.3 collective-permute-start.10
  80.0 0.0 collective-permute-done.9.part3_ref
  80.0 1.0 %collective-permute-done.12.inner3_ref = f32[8,256]{1,0:T(8,128)S(1)} collective-permute-done((f32[8,256]{1,0:T(8,128)S(1)}, f32[8,256]{1,0:T(8,128)S(1)}, u32[]{:S(2)}, u32[]{:S(2)}) %collective-permute-start.12) | collective-permute-done | bytes 8224 | tf_op jit(solution)/shard_map/ppermute | solution.py:360
  81.0 0.3 collective-permute-done.11.inner2_ref
  81.3 1.9 %collective-permute-done.10.inner1_ref = f32[8,256]{1,0:T(8,128)S(1)} collective-permute-done((f32[8,256]{1,0:T(8,128)S(1)}, f32[8,256]{1,0:T(8,128)S(1)}, u32[]{:S(2)}, u32[]{:S(2)}) %collective-permute-start.10) | collective-permute-done | bytes 8224 | tf_op jit(solution)/shard_map/ppermute | solution.py:360
  83.3 1.6 %shard_map.100 = f32[2,192,192]{2,1,0:T(8,128)} custom-call(s32[4]{0:T(128)S(1)} %pad_add_fusion.place_ref, bf16[3,192,128]{2,1,0:T(8,128)(2,1)S(1)} %get-tuple-element.26.part0_ref, bf16[3,192,128]{2,1,0:T(8,128)(2,1)S(1)} %collective-permute-done.7.part1_ref, bf16[3,192,128]{2,1,0:T(8,128)(2,1)S(1)} %collective-permute-done.8.part2_ref, ...), custom_call_target="tpu_custom_call" | custom-call | bytes 2097152 | tf_op jit(solution)/shard_map/pallas_call | solution.py:24
  84.9 0.0 collective-permute-done.6.cols_ref
  84.9 0.9 %shard_map.98 = f32[32,24,64]{2,1,0:T(8,128)} custom-call(f32[24,2048]{1,0:T(8,128)S(1)} %get-tuple-element.23.keep_ref, bf16[24,2304]{1,0:T(8,128)(2,1)S(1)} %collective-permute-done.5.rows_ref, bf16[24,2048]{1,0:T(8,128)(2,1)S(1)} %collective-permute-done.6.cols_ref), custom_call_target="tpu_custom_call" | custom-call | bytes 2097152 | tf_op jit(solution)/shard_map/pallas_call | solution.py:24
  (1 shorter events, 0.0 us)
Async XLA Ops:
  0.6 26.1 %collective-permute-start = (bf16[32,64,192]{2,1,0:T(8,128)(2,1)}, bf16[32,64,192]{2,1,0:T(8,128)(2,1)S(1)}, u32[]{:S(2)}, u32[]{:S(2)}) collective-permute-start(bf16[32,64,192]{2,1,0:T(8,128)(2,1)} %bitcast.10), channel_id=1, source_target_pairs={{0,8},{9,1},{2,24},{11,17},{4,40},{13,33},{6,56},{15,49},{16,42},{... | collective-permute-start | bytes 2359304 | tf_op jit(solution)/shard_map/ppermute | solution.py:300
  26.7 2.7 %collective-permute-start.1 = (bf16[32,64,192]{2,1,0:T(8,128)(2,1)S(1)}, bf16[32,64,192]{2,1,0:T(8,128)(2,1)S(1)}, u32[]{:S(2)}, u32[]{:S(2)}) collective-permute-start(bf16[32,64,192]{2,1,0:T(8,128)(2,1)S(1)} %collective-permute-done.mine_ref), channel_id=1, source_target_pairs={{0,8},{8,0},{16,24},{24,16},{32,40},{40,32},{48,56},{56,48},{1,9},... | collective-permute-start | bytes 2359304 | tf_op jit(solution)/shard_map/ppermute | solution.py:311
  44.2 5.7 %copy-start.2 = (bf16[2,24,2304]{2,1,0:T(8,128)(2,1)S(1)}, bf16[2,24,2304]{2,1,0:T(8,128)(2,1)}, u32[]{:S(2)}) copy-start(bf16[2,24,2304]{2,1,0:T(8,128)(2,1)} %get-tuple-element.20) | copy-start | bytes 663556
  44.2 6.1 %copy-start.1 = (bf16[2,24,2304]{2,1,0:T(8,128)(2,1)S(1)}, bf16[2,24,2304]{2,1,0:T(8,128)(2,1)}, u32[]{:S(2)}) copy-start(bf16[2,24,2304]{2,1,0:T(8,128)(2,1)} %get-tuple-element.21) | copy-start | bytes 663556
  44.2 8.1 %copy-start = (bf16[2,24,2304]{2,1,0:T(8,128)(2,1)S(1)}, bf16[2,24,2304]{2,1,0:T(8,128)(2,1)}, u32[]{:S(2)}) copy-start(bf16[2,24,2304]{2,1,0:T(8,128)(2,1)} %get-tuple-element.22) | copy-start | bytes 663556
  44.2 24.2 %all-to-all-start.1 = ((bf16[8,24,2048]{2,1,0:T(8,128)(2,1)}), bf16[8,24,2048]{2,1,0:T(8,128)(2,1)S(1)}, u32[]{:S(2)}, u32[]{:S(2)}) async-start(bf16[8,24,2048]{2,1,0:T(8,128)(2,1)} %get-tuple-element.25), calls=%async_computation.1 | async-start | bytes 1572864 | tf_op jit(solution)/shard_map/all_to_all | solution.py:364
  49.9 8.3 %collective-permute-start.2 = (bf16[2,24,2304]{2,1,0:T(8,128)(2,1)S(1)}, bf16[2,24,2304]{2,1,0:T(8,128)(2,1)S(1)}, u32[]{:S(2)}, u32[]{:S(2)}) collective-permute-start(bf16[2,24,2304]{2,1,0:T(8,128)(2,1)S(1)} %copy-done.2), channel_id=1, source_target_pairs={{0,2},{1,3},{2,0},{3,1},{4,6},{5,7},{6,4},{7,5},{8,10},{9,11},{10,... | collective-permute-start | bytes 663560 | tf_op jit(solution)/shard_map/ppermute | solution.py:360
  50.3 12.4 %collective-permute-start.3 = (bf16[2,24,2304]{2,1,0:T(8,128)(2,1)S(1)}, bf16[2,24,2304]{2,1,0:T(8,128)(2,1)S(1)}, u32[]{:S(2)}, u32[]{:S(2)}) collective-permute-start(bf16[2,24,2304]{2,1,0:T(8,128)(2,1)S(1)} %copy-done.1), channel_id=1, source_target_pairs={{0,4},{1,5},{2,6},{3,7},{4,0},{5,1},{6,2},{7,3},{8,12},{9,13},{10,... | collective-permute-start | bytes 663560 | tf_op jit(solution)/shard_map/ppermute | solution.py:360
  52.4 12.9 %collective-permute-start.4 = (bf16[2,24,2304]{2,1,0:T(8,128)(2,1)S(1)}, bf16[2,24,2304]{2,1,0:T(8,128)(2,1)S(1)}, u32[]{:S(2)}, u32[]{:S(2)}) collective-permute-start(bf16[2,24,2304]{2,1,0:T(8,128)(2,1)S(1)} %copy-done), channel_id=1, source_target_pairs={{0,6},{1,7},{2,4},{3,5},{4,2},{5,3},{6,0},{7,1},{8,14},{9,15},{10,... | collective-permute-start | bytes 663560 | tf_op jit(solution)/shard_map/ppermute | solution.py:360
  54.6 22.1 %collective-permute-start.7 = (bf16[3,192,128]{2,1,0:T(8,128)(2,1)S(1)}, bf16[3,192,128]{2,1,0:T(8,128)(2,1)S(1)}, u32[]{:S(2)}, u32[]{:S(2)}) collective-permute-start(bf16[3,192,128]{2,1,0:T(8,128)(2,1)S(1)} %get-tuple-element.27), channel_id=1, source_target_pairs={{0,64},{64,0},{128,192},{192,128},{1,65},{65,1},{129,193},{193,129... | collective-permute-start | bytes 442376 | tf_op jit(solution)/shard_map/ppermute | solution.py:360
  56.2 23.4 %collective-permute-start.8 = (bf16[3,192,128]{2,1,0:T(8,128)(2,1)S(1)}, bf16[3,192,128]{2,1,0:T(8,128)(2,1)S(1)}, u32[]{:S(2)}, u32[]{:S(2)}) collective-permute-start(bf16[3,192,128]{2,1,0:T(8,128)(2,1)S(1)} %get-tuple-element.28), channel_id=1, source_target_pairs={{0,128},{64,192},{128,0},{192,64},{1,129},{65,193},{129,1},{193,65... | collective-permute-start | bytes 442376 | tf_op jit(solution)/shard_map/ppermute | solution.py:360
  58.2 21.8 %collective-permute-start.9 = (bf16[3,192,128]{2,1,0:T(8,128)(2,1)S(1)}, bf16[3,192,128]{2,1,0:T(8,128)(2,1)S(1)}, u32[]{:S(2)}, u32[]{:S(2)}) collective-permute-start(bf16[3,192,128]{2,1,0:T(8,128)(2,1)S(1)} %get-tuple-element.29), channel_id=1, source_target_pairs={{0,192},{64,128},{128,64},{192,0},{1,193},{65,129},{129,65},{193,1... | collective-permute-start | bytes 442376 | tf_op jit(solution)/shard_map/ppermute | solution.py:360
  65.9 9.7 %collective-permute-start.5 = (bf16[24,2304]{1,0:T(8,128)(2,1)S(1)}, bf16[24,2304]{1,0:T(8,128)(2,1)S(1)}, u32[]{:S(2)}, u32[]{:S(2)}) collective-permute-start(bf16[24,2304]{1,0:T(8,128)(2,1)S(1)} %get-tuple-element.24), channel_id=1, source_target_pairs={{0,1},{1,0},{2,3},{3,2},{4,5},{5,4},{6,7},{7,6},{8,9},{9,8},{10,11... | collective-permute-start | bytes 331784 | tf_op jit(solution)/shard_map/ppermute | solution.py:360
  68.5 16.4 %collective-permute-start.6 = (bf16[24,2048]{1,0:T(8,128)(2,1)S(1)}, bf16[24,2048]{1,0:T(8,128)(2,1)S(1)}, u32[]{:S(2)}, u32[]{:S(2)}) collective-permute-start(bf16[24,2048]{1,0:T(8,128)(2,1)S(1)} %reduce_sum.12), channel_id=1, source_target_pairs={{0,0},{1,8},{2,16},{3,24},{4,32},{5,40},{6,48},{7,56},{8,1},{9,9},... | collective-permute-start | bytes 294920 | tf_op jit(solution)/shard_map/ppermute | solution.py:366
  75.6 5.4 %collective-permute-start.12 = (f32[8,256]{1,0:T(8,128)S(1)}, f32[8,256]{1,0:T(8,128)S(1)}, u32[]{:S(2)}, u32[]{:S(2)}) collective-permute-start(f32[8,256]{1,0:T(8,128)S(1)} %shard_map.99.inner0_ref), channel_id=1, source_target_pairs={{0,192},{64,128},{128,64},{192,0},{1,193},{65,129},{129,65},{193,1... | collective-permute-start | bytes 24584 | tf_op jit(solution)/shard_map/ppermute | solution.py:360
  76.7 4.6 %collective-permute-start.11 = (f32[8,256]{1,0:T(8,128)S(1)}, f32[8,256]{1,0:T(8,128)S(1)}, u32[]{:S(2)}, u32[]{:S(2)}) collective-permute-start(f32[8,256]{1,0:T(8,128)S(1)} %shard_map.99.inner0_ref), channel_id=1, source_target_pairs={{0,128},{64,192},{128,0},{192,64},{1,129},{65,193},{129,1},{193,65... | collective-permute-start | bytes 24584 | tf_op jit(solution)/shard_map/ppermute | solution.py:360
  79.6 3.7 %collective-permute-start.10 = (f32[8,256]{1,0:T(8,128)S(1)}, f32[8,256]{1,0:T(8,128)S(1)}, u32[]{:S(2)}, u32[]{:S(2)}) collective-permute-start(f32[8,256]{1,0:T(8,128)S(1)} %shard_map.99.inner0_ref), channel_id=1, source_target_pairs={{0,64},{64,0},{128,192},{192,128},{1,65},{65,1},{129,193},{193,129... | collective-permute-start | bytes 24584 | tf_op jit(solution)/shard_map/ppermute | solution.py:360

commit v4 on v3

--- a/solution.py
+++ b/solution.py
@@ -9,7 +9,7 @@
 BF16 = jnp.bfloat16
 MASKED = -1000000000.0
 VMEM_BYTES = 24 * 1024 * 1024
-STEPS = 4
+STEPS = 2
 
 
 def call(kernel, outs, inputs, in_specs=None, out_specs=None, grid=None, scratch=(), scalars=None, flops=0, moved=0):

time: 86.1 us -> 84.8 us (0.985)
  Pallas kernels: 20.3 us -> 19 us
    pallas_call x6, Pallas kernels: 20.3 us -> 19 us  [call(): pl.pallas_call(kernel, out_shape=outs, in_specs=[pl.BlockSpec(memory_spac...]
where the time goes in v4:
time: 84.8 us; the launch traced here: 84.5 us
  starting transfers between devices  27.8 us (33%)
  blocking collectives  19.1 us (23%)
  Pallas kernels  19 us (22%)
  waiting for transfers between devices  16.8 us (20%)
    all_to_all x1, blocking collectives, body(): stats = lax.all_to_all(local_stats, 'col', 0, 0, tiled=True)  19.1 us
    pallas_call x6, Pallas kernels, call(): pl.pallas_call(kernel, out_shape=outs, in_specs=[pl.BlockSpec(memory_spac...  19 us
    ppermute x10, starting transfers between devices, swapped(): lax.ppermute(a, axis, [(i, i ^ bits) for i in range(lax.axis_size(axis))])  16 us
    ppermute x10, waiting for transfers between devices, swapped(): lax.ppermute(a, axis, [(i, i ^ bits) for i in range(lax.axis_size(axis))])  14.6 us
    all_to_all x1, starting transfers between devices, body(): col_term = lax.all_to_all(col_term, 'row', 0, 0, tiled=True)  5.66 us
    ppermute x1, starting transfers between devices, body(): lax.ppermute(jnp.swapaxes(layernormed_alignment, 1, 2), ('row', 'col'), r...  3.92 us
    ppermute x1, waiting for transfers between devices, body(): other = lax.ppermute(mine, 'row', [(i, i ^ 1) for i in range(row_count)])  2.23 us
    ppermute x1, starting transfers between devices, body(): lax.ppermute(col_term, ('row', 'col'), [(r * col_count + c, c * col_count...  1.92 us
  transfers between devices with their start and end apart: 14, of which 8 were waited for; matrix products, arithmetic and copies ran while one was open for 1% of the time, Pallas kernels for 5%

profile of v4, /device:TPU:2, one launch (start us, length us, event | category | flops | bytes accessed | tf_op | source)
XLA Modules:
  0.0 84.5 jit_solution(6899629466508456305)
XLA Ops:
  0.6 3.9 %collective-permute-start = (bf16[32,64,192]{2,1,0:T(8,128)(2,1)}, bf16[32,64,192]{2,1,0:T(8,128)(2,1)S(1)}, u32[]{:S(2)}, u32[]{:S(2)}) collective-permute-start(bf16[32,64,192]{2,1,0:T(8,128)(2,1)} %bitcast.10), channel_id=1, source_target_pairs={{0,8},{9,1},{2,24},{11,17},{4,40},{13,33},{6,56},{15,49},{16,42},{... | collective-permute-start | bytes 2359304 | tf_op jit(solution)/shard_map/ppermute | solution.py:300
  4.6 0.8 dynamic_slice.3
  5.3 2.3 %shard_map.95 = f32[8,16,192]{2,1,0:T(8,128)S(1)} custom-call(f32[8,192,192]{2,1,0:T(8,128)} %scores_ref.3, s32[1,192]{1,0:T(1,128)S(1)} %bitcast.8), custom_call_target="tpu_custom_call" | custom-call | bytes 4194304 | tf_op jit(solution)/shard_map/pallas_call | solution.py:24
  7.6 19.1 %all_to_all.10.stats_ref = f32[8,16,192]{2,1,0:T(8,128)S(1)} all-to-all(f32[8,16,192]{2,1,0:T(8,128)S(1)} %shard_map.95), channel_id=1, replica_groups=mesh['seq'=4,'row'=8,'col'=8] {'col'}, dimensions={0} | all-to-all | bytes 196608 | tf_op jit(solution)/shard_map/all_to_all | solution.py:308
  26.7 0.0 collective-permute-done.mine_ref
  26.7 0.4 collective-permute-start.1
  27.1 0.1 pad_add_fusion.place_ref
  27.1 2.2 %collective-permute-done.1.other_ref = bf16[32,64,192]{2,1,0:T(8,128)(2,1)S(1)} collective-permute-done((bf16[32,64,192]{2,1,0:T(8,128)(2,1)S(1)}, bf16[32,64,192]{2,1,0:T(8,128)(2,1)S(1)}, u32[]{:S(2)}, u32[]{:S(2)}) %collective-permute-start.1) | collective-permute-done | bytes 786464 | tf_op jit(solution)/shard_map/ppermute | solution.py:311
  29.4 13.6 %shard_map.96 = (f32[2,192,192]{2,1,0:T(8,128)S(1)}, bf16[8,24,2048]{2,1,0:T(8,128)(2,1)}, bf16[2,24,2304]{2,1,0:T(8,128)(2,1)S(1)}, bf16[2,24,2304]{2,1,0:T(8,1...) custom-call(s32[4]{0:T(128)S(1)} %pad_add_fusion.place_ref, ...), custom_call_target="tpu_custom_call" | custom-call | flops 1073741824 | bytes 18874368 | tf_op jit(solution)/shard_map/pallas_call | solution.py:24
  42.9 0.0 copy-start.2
  42.9 0.0 copy-start.1
  42.9 0.0 copy-start
  43.0 5.7 %all-to-all-start.1 = ((bf16[8,24,2048]{2,1,0:T(8,128)(2,1)}), bf16[8,24,2048]{2,1,0:T(8,128)(2,1)S(1)}, u32[]{:S(2)}, u32[]{:S(2)}) async-start(bf16[8,24,2048]{2,1,0:T(8,128)(2,1)} %get-tuple-element.25), calls=%async_computation.1 | async-start | bytes 1572864 | tf_op jit(solution)/shard_map/all_to_all | solution.py:364
  48.6 0.0 copy-done.2
  48.6 0.4 collective-permute-start.2
  49.0 0.0 copy-done.1
  49.0 2.1 %collective-permute-start.3 = (bf16[2,24,2304]{2,1,0:T(8,128)(2,1)S(1)}, bf16[2,24,2304]{2,1,0:T(8,128)(2,1)S(1)}, u32[]{:S(2)}, u32[]{:S(2)}) collective-permute-start(bf16[2,24,2304]{2,1,0:T(8,128)(2,1)S(1)} %copy-done.1), channel_id=1, source_target_pairs={{0,4},{1,5},{2,6},{3,7},{4,0},{5,1},{6,2},{7,3},{8,12},{9,13},{10,... | collective-permute-start | bytes 663560 | tf_op jit(solution)/shard_map/ppermute | solution.py:360
  51.1 0.0 copy-done
  51.1 2.2 %collective-permute-start.4 = (bf16[2,24,2304]{2,1,0:T(8,128)(2,1)S(1)}, bf16[2,24,2304]{2,1,0:T(8,128)(2,1)S(1)}, u32[]{:S(2)}, u32[]{:S(2)}) collective-permute-start(bf16[2,24,2304]{2,1,0:T(8,128)(2,1)S(1)} %copy-done), channel_id=1, source_target_pairs={{0,6},{1,7},{2,4},{3,5},{4,2},{5,3},{6,0},{7,1},{8,14},{9,15},{10,... | collective-permute-start | bytes 663560 | tf_op jit(solution)/shard_map/ppermute | solution.py:360
  53.3 1.6 %collective-permute-start.7 = (bf16[3,192,128]{2,1,0:T(8,128)(2,1)S(1)}, bf16[3,192,128]{2,1,0:T(8,128)(2,1)S(1)}, u32[]{:S(2)}, u32[]{:S(2)}) collective-permute-start(bf16[3,192,128]{2,1,0:T(8,128)(2,1)S(1)} %get-tuple-element.27), channel_id=1, source_target_pairs={{0,64},{64,0},{128,192},{192,128},{1,65},{65,1},{129,193},{193,129... | collective-permute-start | bytes 442376 | tf_op jit(solution)/shard_map/ppermute | solution.py:360
  55.0 0.9 %collective-permute-start.8 = (bf16[3,192,128]{2,1,0:T(8,128)(2,1)S(1)}, bf16[3,192,128]{2,1,0:T(8,128)(2,1)S(1)}, u32[]{:S(2)}, u32[]{:S(2)}) collective-permute-start(bf16[3,192,128]{2,1,0:T(8,128)(2,1)S(1)} %get-tuple-element.28), channel_id=1, source_target_pairs={{0,128},{64,192},{128,0},{192,64},{1,129},{65,193},{129,1},{193,65... | collective-permute-start | bytes 442376 | tf_op jit(solution)/shard_map/ppermute | solution.py:360
  55.8 1.1 %collective-permute-done.2.part1_ref = bf16[2,24,2304]{2,1,0:T(8,128)(2,1)S(1)} collective-permute-done((bf16[2,24,2304]{2,1,0:T(8,128)(2,1)S(1)}, bf16[2,24,2304]{2,1,0:T(8,128)(2,1)S(1)}, u32[]{:S(2)}, u32[]{:S(2)}) %collective-permute-start.2) | collective-permute-done | bytes 221216 | tf_op jit(solution)/shard_map/ppermute | solution.py:360
  56.9 1.9 %collective-permute-start.9 = (bf16[3,192,128]{2,1,0:T(8,128)(2,1)S(1)}, bf16[3,192,128]{2,1,0:T(8,128)(2,1)S(1)}, u32[]{:S(2)}, u32[]{:S(2)}) collective-permute-start(bf16[3,192,128]{2,1,0:T(8,128)(2,1)S(1)} %get-tuple-element.29), channel_id=1, source_target_pairs={{0,192},{64,128},{128,64},{192,0},{1,193},{65,129},{129,65},{193,1... | collective-permute-start | bytes 442376 | tf_op jit(solution)/shard_map/ppermute | solution.py:360
  58.8 2.6 %collective-permute-done.3.part2_ref = bf16[2,24,2304]{2,1,0:T(8,128)(2,1)S(1)} collective-permute-done((bf16[2,24,2304]{2,1,0:T(8,128)(2,1)S(1)}, bf16[2,24,2304]{2,1,0:T(8,128)(2,1)S(1)}, u32[]{:S(2)}, u32[]{:S(2)}) %collective-permute-start.3) | collective-permute-done | bytes 221216 | tf_op jit(solution)/shard_map/ppermute | solution.py:360
  61.4 2.6 %collective-permute-done.4.part3_ref = bf16[2,24,2304]{2,1,0:T(8,128)(2,1)S(1)} collective-permute-done((bf16[2,24,2304]{2,1,0:T(8,128)(2,1)S(1)}, bf16[2,24,2304]{2,1,0:T(8,128)(2,1)S(1)}, u32[]{:S(2)}, u32[]{:S(2)}) %collective-permute-start.4) | collective-permute-done | bytes 221216 | tf_op jit(solution)/shard_map/ppermute | solution.py:360
  63.9 0.7 shard_map.97
  64.6 2.5 %collective-permute-start.5 = (bf16[24,2304]{1,0:T(8,128)(2,1)S(1)}, bf16[24,2304]{1,0:T(8,128)(2,1)S(1)}, u32[]{:S(2)}, u32[]{:S(2)}) collective-permute-start(bf16[24,2304]{1,0:T(8,128)(2,1)S(1)} %get-tuple-element.24), channel_id=1, source_target_pairs={{0,1},{1,0},{2,3},{3,2},{4,5},{5,4},{6,7},{7,6},{8,9},{9,8},{10,11... | collective-permute-start | bytes 331784 | tf_op jit(solution)/shard_map/ppermute | solution.py:360
  67.1 0.0 all-to-all-done.1
  67.1 0.1 reduce_sum.12
  67.2 1.9 %collective-permute-start.6 = (bf16[24,2048]{1,0:T(8,128)(2,1)S(1)}, bf16[24,2048]{1,0:T(8,128)(2,1)S(1)}, u32[]{:S(2)}, u32[]{:S(2)}) collective-permute-start(bf16[24,2048]{1,0:T(8,128)(2,1)S(1)} %reduce_sum.12), channel_id=1, source_target_pairs={{0,0},{1,8},{2,16},{3,24},{4,32},{5,40},{6,48},{7,56},{8,1},{9,9},... | collective-permute-start | bytes 294920 | tf_op jit(solution)/shard_map/ppermute | solution.py:366
  69.2 5.2 %collective-permute-done.5.rows_ref = bf16[24,2304]{1,0:T(8,128)(2,1)S(1)} collective-permute-done((bf16[24,2304]{1,0:T(8,128)(2,1)S(1)}, bf16[24,2304]{1,0:T(8,128)(2,1)S(1)}, u32[]{:S(2)}, u32[]{:S(2)}) %collective-permute-start.5) | collective-permute-done | bytes 110624 | tf_op jit(solution)/shard_map/ppermute | solution.py:360
  74.4 1.9 %collective-permute-start.12 = (f32[8,256]{1,0:T(8,128)S(1)}, f32[8,256]{1,0:T(8,128)S(1)}, u32[]{:S(2)}, u32[]{:S(2)}) collective-permute-start(f32[8,256]{1,0:T(8,128)S(1)} %shard_map.99.inner0_ref), channel_id=1, source_target_pairs={{0,192},{64,128},{128,64},{192,0},{1,193},{65,129},{129,65},{193,1... | collective-permute-start | bytes 24584 | tf_op jit(solution)/shard_map/ppermute | solution.py:360
  76.3 0.0 collective-permute-done.7.part1_ref
  76.3 1.9 %collective-permute-start.11 = (f32[8,256]{1,0:T(8,128)S(1)}, f32[8,256]{1,0:T(8,128)S(1)}, u32[]{:S(2)}, u32[]{:S(2)}) collective-permute-start(f32[8,256]{1,0:T(8,128)S(1)} %shard_map.99.inner0_ref), channel_id=1, source_target_pairs={{0,128},{64,192},{128,0},{192,64},{1,129},{65,193},{129,1},{193,65... | collective-permute-start | bytes 24584 | tf_op jit(solution)/shard_map/ppermute | solution.py:360
  78.3 0.0 collective-permute-done.8.part2_ref
  78.3 0.5 collective-permute-start.10
  78.8 0.0 collective-permute-done.9.part3_ref
  78.8 1.0 %collective-permute-done.12.inner3_ref = f32[8,256]{1,0:T(8,128)S(1)} collective-permute-done((f32[8,256]{1,0:T(8,128)S(1)}, f32[8,256]{1,0:T(8,128)S(1)}, u32[]{:S(2)}, u32[]{:S(2)}) %collective-permute-start.12) | collective-permute-done | bytes 8224 | tf_op jit(solution)/shard_map/ppermute | solution.py:360
  79.9 1.0 %collective-permute-done.11.inner2_ref = f32[8,256]{1,0:T(8,128)S(1)} collective-permute-done((f32[8,256]{1,0:T(8,128)S(1)}, f32[8,256]{1,0:T(8,128)S(1)}, u32[]{:S(2)}, u32[]{:S(2)}) %collective-permute-start.11) | collective-permute-done | bytes 8224 | tf_op jit(solution)/shard_map/ppermute | solution.py:360
  80.9 1.0 %collective-permute-done.10.inner1_ref = f32[8,256]{1,0:T(8,128)S(1)} collective-permute-done((f32[8,256]{1,0:T(8,128)S(1)}, f32[8,256]{1,0:T(8,128)S(1)}, u32[]{:S(2)}, u32[]{:S(2)}) %collective-permute-start.10) | collective-permute-done | bytes 8224 | tf_op jit(solution)/shard_map/ppermute | solution.py:360
  81.9 1.6 %shard_map.100 = f32[2,192,192]{2,1,0:T(8,128)} custom-call(s32[4]{0:T(128)S(1)} %pad_add_fusion.place_ref, bf16[3,192,128]{2,1,0:T(8,128)(2,1)S(1)} %get-tuple-element.26.part0_ref, bf16[3,192,128]{2,1,0:T(8,128)(2,1)S(1)} %collective-permute-done.7.part1_ref, bf16[3,192,128]{2,1,0:T(8,128)(2,1)S(1)} %collective-permute-done.8.part2_ref, ...), custom_call_target="tpu_custom_call" | custom-call | bytes 2097152 | tf_op jit(solution)/shard_map/pallas_call | solution.py:24
  83.6 0.0 collective-permute-done.6.cols_ref
  83.6 0.9 %shard_map.98 = f32[32,24,64]{2,1,0:T(8,128)} custom-call(f32[24,2048]{1,0:T(8,128)S(1)} %get-tuple-element.23.keep_ref, bf16[24,2304]{1,0:T(8,128)(2,1)S(1)} %collective-permute-done.5.rows_ref, bf16[24,2048]{1,0:T(8,128)(2,1)S(1)} %collective-permute-done.6.cols_ref), custom_call_target="tpu_custom_call" | custom-call | bytes 2097152 | tf_op jit(solution)/shard_map/pallas_call | solution.py:24
  (1 shorter events, 0.0 us)
Async XLA Ops:
  0.6 26.1 %collective-permute-start = (bf16[32,64,192]{2,1,0:T(8,128)(2,1)}, bf16[32,64,192]{2,1,0:T(8,128)(2,1)S(1)}, u32[]{:S(2)}, u32[]{:S(2)}) collective-permute-start(bf16[32,64,192]{2,1,0:T(8,128)(2,1)} %bitcast.10), channel_id=1, source_target_pairs={{0,8},{9,1},{2,24},{11,17},{4,40},{13,33},{6,56},{15,49},{16,42},{... | collective-permute-start | bytes 2359304 | tf_op jit(solution)/shard_map/ppermute | solution.py:300
  26.7 2.7 %collective-permute-start.1 = (bf16[32,64,192]{2,1,0:T(8,128)(2,1)S(1)}, bf16[32,64,192]{2,1,0:T(8,128)(2,1)S(1)}, u32[]{:S(2)}, u32[]{:S(2)}) collective-permute-start(bf16[32,64,192]{2,1,0:T(8,128)(2,1)S(1)} %collective-permute-done.mine_ref), channel_id=1, source_target_pairs={{0,8},{8,0},{16,24},{24,16},{32,40},{40,32},{48,56},{56,48},{1,9},... | collective-permute-start | bytes 2359304 | tf_op jit(solution)/shard_map/ppermute | solution.py:311
  42.9 5.7 %copy-start.2 = (bf16[2,24,2304]{2,1,0:T(8,128)(2,1)S(1)}, bf16[2,24,2304]{2,1,0:T(8,128)(2,1)}, u32[]{:S(2)}) copy-start(bf16[2,24,2304]{2,1,0:T(8,128)(2,1)} %get-tuple-element.20) | copy-start | bytes 663556
  42.9 6.1 %copy-start.1 = (bf16[2,24,2304]{2,1,0:T(8,128)(2,1)S(1)}, bf16[2,24,2304]{2,1,0:T(8,128)(2,1)}, u32[]{:S(2)}) copy-start(bf16[2,24,2304]{2,1,0:T(8,128)(2,1)} %get-tuple-element.21) | copy-start | bytes 663556
  42.9 8.1 %copy-start = (bf16[2,24,2304]{2,1,0:T(8,128)(2,1)S(1)}, bf16[2,24,2304]{2,1,0:T(8,128)(2,1)}, u32[]{:S(2)}) copy-start(bf16[2,24,2304]{2,1,0:T(8,128)(2,1)} %get-tuple-element.22) | copy-start | bytes 663556
  43.0 24.2 %all-to-all-start.1 = ((bf16[8,24,2048]{2,1,0:T(8,128)(2,1)}), bf16[8,24,2048]{2,1,0:T(8,128)(2,1)S(1)}, u32[]{:S(2)}, u32[]{:S(2)}) async-start(bf16[8,24,2048]{2,1,0:T(8,128)(2,1)} %get-tuple-element.25), calls=%async_computation.1 | async-start | bytes 1572864 | tf_op jit(solution)/shard_map/all_to_all | solution.py:364
  48.6 8.3 %collective-permute-start.2 = (bf16[2,24,2304]{2,1,0:T(8,128)(2,1)S(1)}, bf16[2,24,2304]{2,1,0:T(8,128)(2,1)S(1)}, u32[]{:S(2)}, u32[]{:S(2)}) collective-permute-start(bf16[2,24,2304]{2,1,0:T(8,128)(2,1)S(1)} %copy-done.2), channel_id=1, source_target_pairs={{0,2},{1,3},{2,0},{3,1},{4,6},{5,7},{6,4},{7,5},{8,10},{9,11},{10,... | collective-permute-start | bytes 663560 | tf_op jit(solution)/shard_map/ppermute | solution.py:360
  49.0 12.4 %collective-permute-start.3 = (bf16[2,24,2304]{2,1,0:T(8,128)(2,1)S(1)}, bf16[2,24,2304]{2,1,0:T(8,128)(2,1)S(1)}, u32[]{:S(2)}, u32[]{:S(2)}) collective-permute-start(bf16[2,24,2304]{2,1,0:T(8,128)(2,1)S(1)} %copy-done.1), channel_id=1, source_target_pairs={{0,4},{1,5},{2,6},{3,7},{4,0},{5,1},{6,2},{7,3},{8,12},{9,13},{10,... | collective-permute-start | bytes 663560 | tf_op jit(solution)/shard_map/ppermute | solution.py:360
  51.1 12.9 %collective-permute-start.4 = (bf16[2,24,2304]{2,1,0:T(8,128)(2,1)S(1)}, bf16[2,24,2304]{2,1,0:T(8,128)(2,1)S(1)}, u32[]{:S(2)}, u32[]{:S(2)}) collective-permute-start(bf16[2,24,2304]{2,1,0:T(8,128)(2,1)S(1)} %copy-done), channel_id=1, source_target_pairs={{0,6},{1,7},{2,4},{3,5},{4,2},{5,3},{6,0},{7,1},{8,14},{9,15},{10,... | collective-permute-start | bytes 663560 | tf_op jit(solution)/shard_map/ppermute | solution.py:360
  53.3 23.0 %collective-permute-start.7 = (bf16[3,192,128]{2,1,0:T(8,128)(2,1)S(1)}, bf16[3,192,128]{2,1,0:T(8,128)(2,1)S(1)}, u32[]{:S(2)}, u32[]{:S(2)}) collective-permute-start(bf16[3,192,128]{2,1,0:T(8,128)(2,1)S(1)} %get-tuple-element.27), channel_id=1, source_target_pairs={{0,64},{64,0},{128,192},{192,128},{1,65},{65,1},{129,193},{193,129... | collective-permute-start | bytes 442376 | tf_op jit(solution)/shard_map/ppermute | solution.py:360
  55.0 23.3 %collective-permute-start.8 = (bf16[3,192,128]{2,1,0:T(8,128)(2,1)S(1)}, bf16[3,192,128]{2,1,0:T(8,128)(2,1)S(1)}, u32[]{:S(2)}, u32[]{:S(2)}) collective-permute-start(bf16[3,192,128]{2,1,0:T(8,128)(2,1)S(1)} %get-tuple-element.28), channel_id=1, source_target_pairs={{0,128},{64,192},{128,0},{192,64},{1,129},{65,193},{129,1},{193,65... | collective-permute-start | bytes 442376 | tf_op jit(solution)/shard_map/ppermute | solution.py:360
  56.9 21.9 %collective-permute-start.9 = (bf16[3,192,128]{2,1,0:T(8,128)(2,1)S(1)}, bf16[3,192,128]{2,1,0:T(8,128)(2,1)S(1)}, u32[]{:S(2)}, u32[]{:S(2)}) collective-permute-start(bf16[3,192,128]{2,1,0:T(8,128)(2,1)S(1)} %get-tuple-element.29), channel_id=1, source_target_pairs={{0,192},{64,128},{128,64},{192,0},{1,193},{65,129},{129,65},{193,1... | collective-permute-start | bytes 442376 | tf_op jit(solution)/shard_map/ppermute | solution.py:360
  64.6 9.8 %collective-permute-start.5 = (bf16[24,2304]{1,0:T(8,128)(2,1)S(1)}, bf16[24,2304]{1,0:T(8,128)(2,1)S(1)}, u32[]{:S(2)}, u32[]{:S(2)}) collective-permute-start(bf16[24,2304]{1,0:T(8,128)(2,1)S(1)} %get-tuple-element.24), channel_id=1, source_target_pairs={{0,1},{1,0},{2,3},{3,2},{4,5},{5,4},{6,7},{7,6},{8,9},{9,8},{10,11... | collective-permute-start | bytes 331784 | tf_op jit(solution)/shard_map/ppermute | solution.py:360
  67.2 16.3 %collective-permute-start.6 = (bf16[24,2048]{1,0:T(8,128)(2,1)S(1)}, bf16[24,2048]{1,0:T(8,128)(2,1)S(1)}, u32[]{:S(2)}, u32[]{:S(2)}) collective-permute-start(bf16[24,2048]{1,0:T(8,128)(2,1)S(1)} %reduce_sum.12), channel_id=1, source_target_pairs={{0,0},{1,8},{2,16},{3,24},{4,32},{5,40},{6,48},{7,56},{8,1},{9,9},... | collective-permute-start | bytes 294920 | tf_op jit(solution)/shard_map/ppermute | solution.py:366
  74.4 5.4 %collective-permute-start.12 = (f32[8,256]{1,0:T(8,128)S(1)}, f32[8,256]{1,0:T(8,128)S(1)}, u32[]{:S(2)}, u32[]{:S(2)}) collective-permute-start(f32[8,256]{1,0:T(8,128)S(1)} %shard_map.99.inner0_ref), channel_id=1, source_target_pairs={{0,192},{64,128},{128,64},{192,0},{1,193},{65,129},{129,65},{193,1... | collective-permute-start | bytes 24584 | tf_op jit(solution)/shard_map/ppermute | solution.py:360
  76.3 4.6 %collective-permute-start.11 = (f32[8,256]{1,0:T(8,128)S(1)}, f32[8,256]{1,0:T(8,128)S(1)}, u32[]{:S(2)}, u32[]{:S(2)}) collective-permute-start(f32[8,256]{1,0:T(8,128)S(1)} %shard_map.99.inner0_ref), channel_id=1, source_target_pairs={{0,128},{64,192},{128,0},{192,64},{1,129},{65,193},{129,1},{193,65... | collective-permute-start | bytes 24584 | tf_op jit(solution)/shard_map/ppermute | solution.py:360
  78.3 3.7 %collective-permute-start.10 = (f32[8,256]{1,0:T(8,128)S(1)}, f32[8,256]{1,0:T(8,128)S(1)}, u32[]{:S(2)}, u32[]{:S(2)}) collective-permute-start(f32[8,256]{1,0:T(8,128)S(1)} %shard_map.99.inner0_ref), channel_id=1, source_target_pairs={{0,64},{64,0},{128,192},{192,128},{1,65},{65,1},{129,193},{193,129... | collective-permute-start | bytes 24584 | tf_op jit(solution)/shard_map/ppermute | solution.py:360

commit v5 on v4

--- a/solution.py
+++ b/solution.py
@@ -8,7 +8,7 @@
 F32 = jnp.float32
 BF16 = jnp.bfloat16
 MASKED = -1000000000.0
-VMEM_BYTES = 24 * 1024 * 1024
+VMEM_BYTES = 32 * 1024 * 1024
 STEPS = 2
 
 
@@ -47,6 +47,10 @@
 
 def dot(a, b):
     return jnp.dot(a, b, preferred_element_type=F32)
+
+
+def dot_last(a, b):
+    return lax.dot_general(a, b, (((1,), (1,)), ((), ())), preferred_element_type=F32)
 
 
 def turned(a):
@@ -120,7 +124,6 @@
     wt,
     weights,
     wb,
-    turned_wb,
     att,
     term,
     values,
@@ -151,7 +154,6 @@
             exact = jnp.exp(masked - table[:, h : h + 1]) * table[:, heads + h : heads + h + 1]
             weights[h] = exact
             wb[h] = exact.astype(BF16)
-            turned_wb[h] = exact.T.astype(BF16)
 
     first = pl.multiple_of(step * group, group)
     mask = mask_ref[...].astype(F32)
@@ -172,7 +174,7 @@
         values[k] = dot(wt[0], tokens[k]).astype(BF16)
     for h in range(heads):
         block = values[:, h * dim : (h + 1) * dim, :].reshape(group * dim, columns)
-        average = dot(block, turned_wb[h]).reshape(group, dim, rows)
+        average = dot_last(block, wb[h]).reshape(group, dim, rows)
         pieces[:, h * dim : (h + 1) * dim, :] = (average * term[:, h * dim : (h + 1) * dim, :]).astype(BF16)
         att_rows = turned(att[:, h * dim : (h + 1) * dim, :].reshape(group * dim, rows))
         pair_sum[h] += dot(att_rows, block)
@@ -198,7 +200,7 @@
         for k, out_ref in enumerate((row0_ref, row1_ref, row2_ref, row3_ref)):
             out_ref[:, :, 0:wide] = row_out[pl.ds(2 * (place_ref[2] ^ k), 2)]
             for z in range(2):
-                out_ref[z, :, wide:] = inner
+                out_ref[z, :, wide:] = inner[:, 128 * z : 128 * z + 128]
         for k, out_ref in enumerate((pair0_ref, pair1_ref, pair2_ref, pair3_ref)):
             out_ref[...] = pair_out[place_ref[3] ^ k]
         weights_ref[...] = weights[pl.ds(place_ref[3] * own_heads, own_heads)]
@@ -231,6 +233,10 @@
         out_ref[h] = weights_ref[h] * (grad - own)
 
 
+def total_kernel(parts_ref, out_ref):
+    out_ref[...] = jnp.sum(parts_ref[...].astype(F32), axis=0).astype(BF16)
+
+
 def fold_kernel(place_ref, part0_ref, part1_ref, part2_ref, part3_ref, keep_ref, inner_ref, send_ref):
     wide = keep_ref.shape[1]
     parts = (part0_ref, part1_ref, part2_ref, part3_ref)
@@ -238,7 +244,7 @@
     high = place_ref[1] == 1
     keep_ref[...] = jnp.where(high, total[1], total[0])
     send_ref[:, 0:wide] = jnp.where(high, total[0], total[1]).astype(BF16)
-    inner = sum(joined(part[0, :, wide:]) for part in parts)
+    inner = sum(joined(jnp.concatenate([part[0, :, wide:], part[1, :, wide:]], axis=-1)) for part in parts)
     inner_ref[...] = inner
     send_ref[:, wide:] = thirds(inner)
 
@@ -311,13 +317,14 @@
     other = lax.ppermute(mine, "row", [(i, i ^ 1) for i in range(row_count)])
 
     message = wide + 256
+    half_message = wide + 128
     pieces = pltpu.VMEM((group, width, rows), BF16)
     square = pltpu.VMEM((heads, rows, columns), F32)
     weights, col_term, *sent = call(
         main_kernel,
         [jax.ShapeDtypeStruct((own, rows, columns), F32), jax.ShapeDtypeStruct((row_count, stretch, wide), BF16)]
-        + [jax.ShapeDtypeStruct((2, stretch, message), BF16)]
-        + [pltpu.HBM((2, stretch, message), BF16)] * (side - 1)
+        + [jax.ShapeDtypeStruct((2, stretch, half_message), BF16)]
+        + [pltpu.HBM((2, stretch, half_message), BF16)] * (side - 1)
         + [jax.ShapeDtypeStruct((own + 1, rows, 128), BF16)] * seq_count,
         [scores, keep, stats, tokens, cotangent, far(sequence_validity), mine, other, payload_w, gate_w, final_w],
         [
@@ -334,14 +341,13 @@
             whole((features, width)),
         ],
         [whole((own, rows, columns)), whole((row_count, stretch, wide))]
-        + [whole((2, stretch, message)) for _ in range(side)]
+        + [whole((2, stretch, half_message)) for _ in range(side)]
         + [whole((own + 1, rows, 128)) for _ in range(seq_count)],
         grid=(STEPS,),
         scratch=[
             pltpu.VMEM((3, width, features), BF16),
             square,
             pltpu.VMEM((heads, rows, columns), BF16),
-            pltpu.VMEM((heads, columns, rows), BF16),
             pieces,
             pltpu.VMEM((group, width, rows), F32),
             pieces,
@@ -362,7 +368,8 @@
     row_term = row_term[:1] + [swapped(row_term[k], "col", 2 * k) for k in range(1, side)]
     d_weights = d_weights[:1] + [swapped(d_weights[k], "seq", k) for k in range(1, seq_count)]
     col_term = lax.all_to_all(col_term, "row", 0, 0, tiled=True)
-    col_term = jnp.sum(col_term.astype(F32), axis=0).astype(BF16)
+    col_term = call(total_kernel, jax.ShapeDtypeStruct((stretch, wide), BF16), [col_term], moved=1 << 20)
+    col_term, row_term[3] = lax.optimization_barrier((col_term, row_term[3]))
     col_term = lax.ppermute(
         col_term,
         ("row", "col"),

time: 84.8 us -> 84.1 us (level); the launches traced: 84.5 us -> 82.8 us
  waiting for transfers between devices: 16.8 us -> 15.3 us
    ppermute x10, waiting for transfers between devices: 14.6 us -> 11.9 us  [swapped(): lax.ppermute(a, axis, [(i, i ^ bits) for i in range(lax.axis_size(axis))])]
    all_to_all x1, waiting for transfers between devices: 0.01 us -> 1.16 us  [body(): col_term = lax.all_to_all(col_term, 'row', 0, 0, tiled=True)]
    pallas_call x6 -> x7, Pallas kernels: 19 us -> 18.6 us  [call(): pl.pallas_call(kernel, out_shape=outs, in_specs=[pl.BlockSpec(memory_spac...]
  transfers between devices with their start and end apart: 14 -> 14, of which waited for: 8 -> 7; matrix products, arithmetic and copies ran while one was open for 1% -> 1% of each run, Pallas kernels for 5% -> 5%
where the time goes in v5:
time: 84.1 us; the launch traced here: 82.8 us
  starting transfers between devices  28.2 us (34%)
  blocking collectives  19.1 us (23%)
  Pallas kernels  18.6 us (22%)
  waiting for transfers between devices  15.3 us (18%)
    all_to_all x1, blocking collectives, body(): stats = lax.all_to_all(local_stats, 'col', 0, 0, tiled=True)  19.1 us
    pallas_call x7, Pallas kernels, call(): pl.pallas_call(kernel, out_shape=outs, in_specs=[pl.BlockSpec(memory_spac...  18.6 us
    ppermute x10, starting transfers between devices, swapped(): lax.ppermute(a, axis, [(i, i ^ bits) for i in range(lax.axis_size(axis))])  16.4 us
    ppermute x10, waiting for transfers between devices, swapped(): lax.ppermute(a, axis, [(i, i ^ bits) for i in range(lax.axis_size(axis))])  11.9 us
    all_to_all x1, starting transfers between devices, body(): col_term = lax.all_to_all(col_term, 'row', 0, 0, tiled=True)  5.66 us
    ppermute x1, starting transfers between devices, body(): lax.ppermute(jnp.swapaxes(layernormed_alignment, 1, 2), ('row', 'col'), r...  3.92 us
    ppermute x1, waiting for transfers between devices, body(): other = lax.ppermute(mine, 'row', [(i, i ^ 1) for i in range(row_count)])  2.23 us
    ppermute x1, starting transfers between devices, body(): lax.ppermute(col_term, ('row', 'col'), [(r * col_count + c, c * col_count...  1.91 us
  transfers between devices with their start and end apart: 14, of which 7 were waited for; matrix products, arithmetic and copies ran while one was open for 1% of the time, Pallas kernels for 5%

profile of v5, /device:TPU:2, one launch (start us, length us, event | category | flops | bytes accessed | tf_op | source)
XLA Modules:
  0.0 82.8 jit_solution(4777683231390764586)
XLA Ops:
  0.6 3.9 %collective-permute-start = (bf16[32,64,192]{2,1,0:T(8,128)(2,1)}, bf16[32,64,192]{2,1,0:T(8,128)(2,1)S(1)}, u32[]{:S(2)}, u32[]{:S(2)}) collective-permute-start(bf16[32,64,192]{2,1,0:T(8,128)(2,1)} %bitcast.10), channel_id=1, source_target_pairs={{0,8},{9,1},{2,24},{11,17},{4,40},{13,33},{6,56},{15,49},{16,42},{... | collective-permute-start | bytes 2359304 | tf_op jit(solution)/shard_map/ppermute | solution.py:306
  4.6 0.8 dynamic_slice.3
  5.3 2.3 %shard_map.95 = f32[8,16,192]{2,1,0:T(8,128)S(1)} custom-call(f32[8,192,192]{2,1,0:T(8,128)} %scores_ref.3, s32[1,192]{1,0:T(1,128)S(1)} %bitcast.8), custom_call_target="tpu_custom_call" | custom-call | bytes 4194304 | tf_op jit(solution)/shard_map/pallas_call | solution.py:24
  7.6 19.1 %all_to_all.10.stats_ref = f32[8,16,192]{2,1,0:T(8,128)S(1)} all-to-all(f32[8,16,192]{2,1,0:T(8,128)S(1)} %shard_map.95), channel_id=1, replica_groups=mesh['seq'=4,'row'=8,'col'=8] {'col'}, dimensions={0} | all-to-all | bytes 196608 | tf_op jit(solution)/shard_map/all_to_all | solution.py:314
  26.7 0.0 collective-permute-done.mine_ref
  26.7 0.4 collective-permute-start.1
  27.1 0.1 pad_add_fusion.place_ref
  27.1 2.2 %collective-permute-done.1.other_ref = bf16[32,64,192]{2,1,0:T(8,128)(2,1)S(1)} collective-permute-done((bf16[32,64,192]{2,1,0:T(8,128)(2,1)S(1)}, bf16[32,64,192]{2,1,0:T(8,128)(2,1)S(1)}, u32[]{:S(2)}, u32[]{:S(2)}) %collective-permute-start.1) | collective-permute-done | bytes 786464 | tf_op jit(solution)/shard_map/ppermute | solution.py:317
  29.4 13.1 %shard_map.96 = (f32[2,192,192]{2,1,0:T(8,128)S(1)}, bf16[8,24,2048]{2,1,0:T(8,128)(2,1)}, bf16[2,24,2176]{2,1,0:T(8,128)(2,1)S(1)}, bf16[2,24,2176]{2,1,0:T(8,1...) custom-call(s32[4]{0:T(128)S(1)} %pad_add_fusion.place_ref, ...), custom_call_target="tpu_custom_call" | custom-call | flops 1073741824 | bytes 18874368 | tf_op jit(solution)/shard_map/pallas_call | solution.py:24
  42.4 0.0 copy-start
  42.5 5.7 %all-to-all-start.1 = ((bf16[8,24,2048]{2,1,0:T(8,128)(2,1)}), bf16[8,24,2048]{2,1,0:T(8,128)(2,1)S(1)}, u32[]{:S(2)}, u32[]{:S(2)}) async-start(bf16[8,24,2048]{2,1,0:T(8,128)(2,1)} %get-tuple-element.24), calls=%async_computation.1 | async-start | bytes 1572864 | tf_op jit(solution)/shard_map/all_to_all | solution.py:370
  48.1 1.0 %collective-permute-start.4 = (bf16[2,24,2176]{2,1,0:T(8,128)(2,1)}, bf16[2,24,2176]{2,1,0:T(8,128)(2,1)S(1)}, u32[]{:S(2)}, u32[]{:S(2)}) collective-permute-start(bf16[2,24,2176]{2,1,0:T(8,128)(2,1)} %get-tuple-element.25), channel_id=1, source_target_pairs={{0,6},{1,7},{2,4},{3,5},{4,2},{5,3},{6,0},{7,1},{8,14},{9,15},{10,... | collective-permute-start | bytes 626696 | tf_op jit(solution)/shard_map/ppermute | solution.py:366
  49.1 0.1 collective-permute-start.2
  49.2 0.0 copy-done
  49.2 3.6 %collective-permute-start.3 = (bf16[2,24,2176]{2,1,0:T(8,128)(2,1)S(1)}, bf16[2,24,2176]{2,1,0:T(8,128)(2,1)S(1)}, u32[]{:S(2)}, u32[]{:S(2)}) collective-permute-start(bf16[2,24,2176]{2,1,0:T(8,128)(2,1)S(1)} %copy-done), channel_id=1, source_target_pairs={{0,4},{1,5},{2,6},{3,7},{4,0},{5,1},{6,2},{7,3},{8,12},{9,13},{10,... | collective-permute-start | bytes 626696 | tf_op jit(solution)/shard_map/ppermute | solution.py:366
  52.8 1.6 %collective-permute-start.7 = (bf16[3,192,128]{2,1,0:T(8,128)(2,1)S(1)}, bf16[3,192,128]{2,1,0:T(8,128)(2,1)S(1)}, u32[]{:S(2)}, u32[]{:S(2)}) collective-permute-start(bf16[3,192,128]{2,1,0:T(8,128)(2,1)S(1)} %get-tuple-element.31), channel_id=1, source_target_pairs={{0,64},{64,0},{128,192},{192,128},{1,65},{65,1},{129,193},{193,129... | collective-permute-start | bytes 442376 | tf_op jit(solution)/shard_map/ppermute | solution.py:366
  54.4 0.9 %collective-permute-start.8 = (bf16[3,192,128]{2,1,0:T(8,128)(2,1)S(1)}, bf16[3,192,128]{2,1,0:T(8,128)(2,1)S(1)}, u32[]{:S(2)}, u32[]{:S(2)}) collective-permute-start(bf16[3,192,128]{2,1,0:T(8,128)(2,1)S(1)} %get-tuple-element.32), channel_id=1, source_target_pairs={{0,128},{64,192},{128,0},{192,64},{1,129},{65,193},{129,1},{193,65... | collective-permute-start | bytes 442376 | tf_op jit(solution)/shard_map/ppermute | solution.py:366
  55.3 1.4 %collective-permute-done.4.part3_ref = bf16[2,24,2176]{2,1,0:T(8,128)(2,1)S(1)} collective-permute-done((bf16[2,24,2176]{2,1,0:T(8,128)(2,1)}, bf16[2,24,2176]{2,1,0:T(8,128)(2,1)S(1)}, u32[]{:S(2)}, u32[]{:S(2)}) %collective-permute-start.4) | collective-permute-done | bytes 208928 | tf_op jit(solution)/shard_map/ppermute | solution.py:366
  56.7 1.9 %collective-permute-start.9 = (bf16[3,192,128]{2,1,0:T(8,128)(2,1)S(1)}, bf16[3,192,128]{2,1,0:T(8,128)(2,1)S(1)}, u32[]{:S(2)}, u32[]{:S(2)}) collective-permute-start(bf16[3,192,128]{2,1,0:T(8,128)(2,1)S(1)} %get-tuple-element.33), channel_id=1, source_target_pairs={{0,192},{64,128},{128,64},{192,0},{1,193},{65,129},{129,65},{193,1... | collective-permute-start | bytes 442376 | tf_op jit(solution)/shard_map/ppermute | solution.py:366
  58.7 1.2 %all-to-all-done.1.parts_ref = bf16[8,24,2048]{2,1,0:T(8,128)(2,1)S(1)} async-done(((bf16[8,24,2048]{2,1,0:T(8,128)(2,1)}), bf16[8,24,2048]{2,1,0:T(8,128)(2,1)S(1)}, u32[]{:S(2)}, u32[]{:S(2)}) %all-to-all-start.1) | async-done | bytes 786464 | tf_op jit(solution)/shard_map/all_to_all | solution.py:370
  59.8 0.1 shard_map.97
  59.9 0.0 collective-permute-done.2.part1_ref
  60.0 2.5 %collective-permute-done.3.part2_ref = bf16[2,24,2176]{2,1,0:T(8,128)(2,1)S(1)} collective-permute-done((bf16[2,24,2176]{2,1,0:T(8,128)(2,1)S(1)}, bf16[2,24,2176]{2,1,0:T(8,128)(2,1)S(1)}, u32[]{:S(2)}, u32[]{:S(2)}) %collective-permute-start.3) | collective-permute-done | bytes 208928 | tf_op jit(solution)/shard_map/ppermute | solution.py:366
  62.4 0.7 shard_map.98
  63.1 2.1 %collective-permute-start.5 = (bf16[24,2304]{1,0:T(8,128)(2,1)S(1)}, bf16[24,2304]{1,0:T(8,128)(2,1)S(1)}, u32[]{:S(2)}, u32[]{:S(2)}) collective-permute-start(bf16[24,2304]{1,0:T(8,128)(2,1)S(1)} %get-tuple-element.28), channel_id=1, source_target_pairs={{0,1},{1,0},{2,3},{3,2},{4,5},{5,4},{6,7},{7,6},{8,9},{9,8},{10,11... | collective-permute-start | bytes 331784 | tf_op jit(solution)/shard_map/ppermute | solution.py:366
  65.1 1.9 %collective-permute-start.6 = (bf16[24,2048]{1,0:T(8,128)(2,1)S(1)}, bf16[24,2048]{1,0:T(8,128)(2,1)S(1)}, u32[]{:S(2)}, u32[]{:S(2)}) collective-permute-start(bf16[24,2048]{1,0:T(8,128)(2,1)S(1)} %shard_map.97), channel_id=1, source_target_pairs={{0,0},{1,8},{2,16},{3,24},{4,32},{5,40},{6,48},{7,56},{8,1},{9,9},... | collective-permute-start | bytes 294920 | tf_op jit(solution)/shard_map/ppermute | solution.py:373
  67.1 5.2 %collective-permute-done.5.rows_ref = bf16[24,2304]{1,0:T(8,128)(2,1)S(1)} collective-permute-done((bf16[24,2304]{1,0:T(8,128)(2,1)S(1)}, bf16[24,2304]{1,0:T(8,128)(2,1)S(1)}, u32[]{:S(2)}, u32[]{:S(2)}) %collective-permute-start.5) | collective-permute-done | bytes 110624 | tf_op jit(solution)/shard_map/ppermute | solution.py:366
  72.3 1.9 %collective-permute-start.12 = (f32[8,256]{1,0:T(8,128)S(1)}, f32[8,256]{1,0:T(8,128)S(1)}, u32[]{:S(2)}, u32[]{:S(2)}) collective-permute-start(f32[8,256]{1,0:T(8,128)S(1)} %shard_map.100.inner0_ref), channel_id=1, source_target_pairs={{0,192},{64,128},{128,64},{192,0},{1,193},{65,129},{129,65},{193,1... | collective-permute-start | bytes 24584 | tf_op jit(solution)/shard_map/ppermute | solution.py:366
  74.2 0.0 collective-permute-done.7.part1_ref
  74.2 3.3 %collective-permute-start.11 = (f32[8,256]{1,0:T(8,128)S(1)}, f32[8,256]{1,0:T(8,128)S(1)}, u32[]{:S(2)}, u32[]{:S(2)}) collective-permute-start(f32[8,256]{1,0:T(8,128)S(1)} %shard_map.100.inner0_ref), channel_id=1, source_target_pairs={{0,128},{64,192},{128,0},{192,64},{1,129},{65,193},{129,1},{193,65... | collective-permute-start | bytes 24584 | tf_op jit(solution)/shard_map/ppermute | solution.py:366
  77.5 0.0 collective-permute-done.6.cols_ref
  77.5 0.0 collective-permute-start.10
  77.5 0.9 %shard_map.99 = f32[32,24,64]{2,1,0:T(8,128)} custom-call(f32[24,2048]{1,0:T(8,128)S(1)} %get-tuple-element.27.keep_ref, bf16[24,2304]{1,0:T(8,128)(2,1)S(1)} %collective-permute-done.5.rows_ref, bf16[24,2048]{1,0:T(8,128)(2,1)S(1)} %collective-permute-done.6.cols_ref), custom_call_target="tpu_custom_call" | custom-call | bytes 2097152 | tf_op jit(solution)/shard_map/pallas_call | solution.py:24
  78.4 0.0 collective-permute-done.8.part2_ref
  78.4 0.0 collective-permute-done.9.part3_ref
  78.4 0.0 collective-permute-done.12.inner3_ref
  78.4 0.8 collective-permute-done.11.inner2_ref
  79.2 1.9 %collective-permute-done.10.inner1_ref = f32[8,256]{1,0:T(8,128)S(1)} collective-permute-done((f32[8,256]{1,0:T(8,128)S(1)}, f32[8,256]{1,0:T(8,128)S(1)}, u32[]{:S(2)}, u32[]{:S(2)}) %collective-permute-start.10) | collective-permute-done | bytes 8224 | tf_op jit(solution)/shard_map/ppermute | solution.py:366
  81.1 1.6 %shard_map.101 = f32[2,192,192]{2,1,0:T(8,128)} custom-call(s32[4]{0:T(128)S(1)} %pad_add_fusion.place_ref, bf16[3,192,128]{2,1,0:T(8,128)(2,1)S(1)} %get-tuple-element.30.part0_ref, bf16[3,192,128]{2,1,0:T(8,128)(2,1)S(1)} %collective-permute-done.7.part1_ref, bf16[3,192,128]{2,1,0:T(8,128)(2,1)S(1)} %collective-permute-done.8.part2_ref, ...), custom_call_target="tpu_custom_call" | custom-call | bytes 2097152 | tf_op jit(solution)/shard_map/pallas_call | solution.py:24
  (1 shorter events, 0.0 us)
Async XLA Ops:
  0.6 26.1 %collective-permute-start = (bf16[32,64,192]{2,1,0:T(8,128)(2,1)}, bf16[32,64,192]{2,1,0:T(8,128)(2,1)S(1)}, u32[]{:S(2)}, u32[]{:S(2)}) collective-permute-start(bf16[32,64,192]{2,1,0:T(8,128)(2,1)} %bitcast.10), channel_id=1, source_target_pairs={{0,8},{9,1},{2,24},{11,17},{4,40},{13,33},{6,56},{15,49},{16,42},{... | collective-permute-start | bytes 2359304 | tf_op jit(solution)/shard_map/ppermute | solution.py:306
  26.7 2.7 %collective-permute-start.1 = (bf16[32,64,192]{2,1,0:T(8,128)(2,1)S(1)}, bf16[32,64,192]{2,1,0:T(8,128)(2,1)S(1)}, u32[]{:S(2)}, u32[]{:S(2)}) collective-permute-start(bf16[32,64,192]{2,1,0:T(8,128)(2,1)S(1)} %collective-permute-done.mine_ref), channel_id=1, source_target_pairs={{0,8},{8,0},{16,24},{24,16},{32,40},{40,32},{48,56},{56,48},{1,9},... | collective-permute-start | bytes 2359304 | tf_op jit(solution)/shard_map/ppermute | solution.py:317
  42.4 6.8 %copy-start = (bf16[2,24,2176]{2,1,0:T(8,128)(2,1)S(1)}, bf16[2,24,2176]{2,1,0:T(8,128)(2,1)}, u32[]{:S(2)}) copy-start(bf16[2,24,2176]{2,1,0:T(8,128)(2,1)} %get-tuple-element.23) | copy-start | bytes 626692
  42.5 17.4 %all-to-all-start.1 = ((bf16[8,24,2048]{2,1,0:T(8,128)(2,1)}), bf16[8,24,2048]{2,1,0:T(8,128)(2,1)S(1)}, u32[]{:S(2)}, u32[]{:S(2)}) async-start(bf16[8,24,2048]{2,1,0:T(8,128)(2,1)} %get-tuple-element.24), calls=%async_computation.1 | async-start | bytes 1572864 | tf_op jit(solution)/shard_map/all_to_all | solution.py:370
  48.1 8.6 %collective-permute-start.4 = (bf16[2,24,2176]{2,1,0:T(8,128)(2,1)}, bf16[2,24,2176]{2,1,0:T(8,128)(2,1)S(1)}, u32[]{:S(2)}, u32[]{:S(2)}) collective-permute-start(bf16[2,24,2176]{2,1,0:T(8,128)(2,1)} %get-tuple-element.25), channel_id=1, source_target_pairs={{0,6},{1,7},{2,4},{3,5},{4,2},{5,3},{6,0},{7,1},{8,14},{9,15},{10,... | collective-permute-start | bytes 626696 | tf_op jit(solution)/shard_map/ppermute | solution.py:366
  49.1 10.8 %collective-permute-start.2 = (bf16[2,24,2176]{2,1,0:T(8,128)(2,1)}, bf16[2,24,2176]{2,1,0:T(8,128)(2,1)S(1)}, u32[]{:S(2)}, u32[]{:S(2)}) collective-permute-start(bf16[2,24,2176]{2,1,0:T(8,128)(2,1)} %get-tuple-element.22), channel_id=1, source_target_pairs={{0,2},{1,3},{2,0},{3,1},{4,6},{5,7},{6,4},{7,5},{8,10},{9,11},{10,... | collective-permute-start | bytes 626696 | tf_op jit(solution)/shard_map/ppermute | solution.py:366
  49.2 13.2 %collective-permute-start.3 = (bf16[2,24,2176]{2,1,0:T(8,128)(2,1)S(1)}, bf16[2,24,2176]{2,1,0:T(8,128)(2,1)S(1)}, u32[]{:S(2)}, u32[]{:S(2)}) collective-permute-start(bf16[2,24,2176]{2,1,0:T(8,128)(2,1)S(1)} %copy-done), channel_id=1, source_target_pairs={{0,4},{1,5},{2,6},{3,7},{4,0},{5,1},{6,2},{7,3},{8,12},{9,13},{10,... | collective-permute-start | bytes 626696 | tf_op jit(solution)/shard_map/ppermute | solution.py:366
  52.8 21.4 %collective-permute-start.7 = (bf16[3,192,128]{2,1,0:T(8,128)(2,1)S(1)}, bf16[3,192,128]{2,1,0:T(8,128)(2,1)S(1)}, u32[]{:S(2)}, u32[]{:S(2)}) collective-permute-start(bf16[3,192,128]{2,1,0:T(8,128)(2,1)S(1)} %get-tuple-element.31), channel_id=1, source_target_pairs={{0,64},{64,0},{128,192},{192,128},{1,65},{65,1},{129,193},{193,129... | collective-permute-start | bytes 442376 | tf_op jit(solution)/shard_map/ppermute | solution.py:366
  54.4 23.9 %collective-permute-start.8 = (bf16[3,192,128]{2,1,0:T(8,128)(2,1)S(1)}, bf16[3,192,128]{2,1,0:T(8,128)(2,1)S(1)}, u32[]{:S(2)}, u32[]{:S(2)}) collective-permute-start(bf16[3,192,128]{2,1,0:T(8,128)(2,1)S(1)} %get-tuple-element.32), channel_id=1, source_target_pairs={{0,128},{64,192},{128,0},{192,64},{1,129},{65,193},{129,1},{193,65... | collective-permute-start | bytes 442376 | tf_op jit(solution)/shard_map/ppermute | solution.py:366
  56.7 21.6 %collective-permute-start.9 = (bf16[3,192,128]{2,1,0:T(8,128)(2,1)S(1)}, bf16[3,192,128]{2,1,0:T(8,128)(2,1)S(1)}, u32[]{:S(2)}, u32[]{:S(2)}) collective-permute-start(bf16[3,192,128]{2,1,0:T(8,128)(2,1)S(1)} %get-tuple-element.33), channel_id=1, source_target_pairs={{0,192},{64,128},{128,64},{192,0},{1,193},{65,129},{129,65},{193,1... | collective-permute-start | bytes 442376 | tf_op jit(solution)/shard_map/ppermute | solution.py:366
  63.1 9.2 %collective-permute-start.5 = (bf16[24,2304]{1,0:T(8,128)(2,1)S(1)}, bf16[24,2304]{1,0:T(8,128)(2,1)S(1)}, u32[]{:S(2)}, u32[]{:S(2)}) collective-permute-start(bf16[24,2304]{1,0:T(8,128)(2,1)S(1)} %get-tuple-element.28), channel_id=1, source_target_pairs={{0,1},{1,0},{2,3},{3,2},{4,5},{5,4},{6,7},{7,6},{8,9},{9,8},{10,11... | collective-permute-start | bytes 331784 | tf_op jit(solution)/shard_map/ppermute | solution.py:366
  65.1 12.3 %collective-permute-start.6 = (bf16[24,2048]{1,0:T(8,128)(2,1)S(1)}, bf16[24,2048]{1,0:T(8,128)(2,1)S(1)}, u32[]{:S(2)}, u32[]{:S(2)}) collective-permute-start(bf16[24,2048]{1,0:T(8,128)(2,1)S(1)} %shard_map.97), channel_id=1, source_target_pairs={{0,0},{1,8},{2,16},{3,24},{4,32},{5,40},{6,48},{7,56},{8,1},{9,9},... | collective-permute-start | bytes 294920 | tf_op jit(solution)/shard_map/ppermute | solution.py:373
  72.3 6.1 %collective-permute-start.12 = (f32[8,256]{1,0:T(8,128)S(1)}, f32[8,256]{1,0:T(8,128)S(1)}, u32[]{:S(2)}, u32[]{:S(2)}) collective-permute-start(f32[8,256]{1,0:T(8,128)S(1)} %shard_map.100.inner0_ref), channel_id=1, source_target_pairs={{0,192},{64,128},{128,64},{192,0},{1,193},{65,129},{129,65},{193,1... | collective-permute-start | bytes 24584 | tf_op jit(solution)/shard_map/ppermute | solution.py:366
  74.2 5.0 %collective-permute-start.11 = (f32[8,256]{1,0:T(8,128)S(1)}, f32[8,256]{1,0:T(8,128)S(1)}, u32[]{:S(2)}, u32[]{:S(2)}) collective-permute-start(f32[8,256]{1,0:T(8,128)S(1)} %shard_map.100.inner0_ref), channel_id=1, source_target_pairs={{0,128},{64,192},{128,0},{192,64},{1,129},{65,193},{129,1},{193,65... | collective-permute-start | bytes 24584 | tf_op jit(solution)/shard_map/ppermute | solution.py:366
  77.5 3.7 %collective-permute-start.10 = (f32[8,256]{1,0:T(8,128)S(1)}, f32[8,256]{1,0:T(8,128)S(1)}, u32[]{:S(2)}, u32[]{:S(2)}) collective-permute-start(f32[8,256]{1,0:T(8,128)S(1)} %shard_map.100.inner0_ref), channel_id=1, source_target_pairs={{0,64},{64,0},{128,192},{192,128},{1,65},{65,1},{129,193},{193,129... | collective-permute-start | bytes 24584 | tf_op jit(solution)/shard_map/ppermute | solution.py:366

commit v6 on v5

--- a/solution.py
+++ b/solution.py
@@ -206,31 +206,25 @@
         weights_ref[...] = weights[pl.ds(place_ref[3] * own_heads, own_heads)]
 
 
-def score_kernel(
-    place_ref,
-    part0_ref,
-    part1_ref,
-    part2_ref,
-    part3_ref,
-    inner0_ref,
-    inner1_ref,
-    inner2_ref,
-    inner3_ref,
-    weights_ref,
-    out_ref,
-):
-    heads, rows, _ = out_ref.shape
+def gradient_kernel(part0_ref, part1_ref, part2_ref, part3_ref, out_ref):
+    heads = out_ref.shape[0]
     total = part0_ref[...].astype(F32)
     for part in (part1_ref, part2_ref, part3_ref):
         total = total + part[...].astype(F32)
+    for h in range(heads):
+        grad = jnp.concatenate([total[h], total[heads][:, 64 * h : 64 * h + 64]], axis=-1)
+        out_ref[h] = grad
+
+
+def score_kernel(place_ref, inner0_ref, inner1_ref, inner2_ref, inner3_ref, grad_ref, weights_ref, out_ref):
+    heads, rows, _ = out_ref.shape
     inner = ((inner0_ref[...] + inner1_ref[...]) + (inner2_ref[...] + inner3_ref[...]))[:, 0:rows]
     table = jnp.concatenate([inner, jnp.zeros((128 - inner.shape[0], rows), F32)], axis=0).T
     lane = lax.broadcasted_iota(jnp.int32, table.shape, 1)
     for h in range(heads):
         mine = place_ref[3] * heads + h
-        grad = jnp.concatenate([total[h], total[heads][:, 64 * h : 64 * h + 64]], axis=-1)
         own = jnp.sum(jnp.where(lane == mine, table, 0.0), axis=1, keepdims=True)
-        out_ref[h] = weights_ref[h] * (grad - own)
+        out_ref[h] = weights_ref[h] * (grad_ref[h] - own)
 
 
 def total_kernel(parts_ref, out_ref):
@@ -387,12 +381,16 @@
         moved=2 << 20,
     )
     row_send = swapped(row_send, "col", 1)
+    gradient = call(
+        gradient_kernel, jax.ShapeDtypeStruct((own, rows, columns), F32), d_weights, moved=1 << 20
+    )
+    row_send, gradient = lax.optimization_barrier((row_send, gradient))
     inner = call(inner_kernel, jax.ShapeDtypeStruct((heads, 256), F32), [inner, row_send], moved=1 << 20)
     inners = [inner] + [swapped(inner, "seq", k) for k in range(1, seq_count)]
     score_cotangent = call(
         score_kernel,
         jax.ShapeDtypeStruct((own, rows, columns), F32),
-        d_weights + inners + [weights],
+        inners + [gradient, weights],
         scalars=place,
         moved=2 << 20,
     )

time: 84.1 us -> 84.3 us (level)
    pallas_call x7 -> x8, Pallas kernels: 18.6 us -> 18.7 us  [call(): pl.pallas_call(kernel, out_shape=outs, in_specs=[pl.BlockSpec(memory_spac...]
  transfers between devices with their start and end apart: 14 -> 14, of which waited for: 7 -> 8; matrix products, arithmetic and copies ran while one was open for 1% -> 1% of each run, Pallas kernels for 5% -> 5%
where the time goes in v6:
time: 84.3 us; the launch traced here: 83.3 us
  starting transfers between devices  28.8 us (34%)
  blocking collectives  19.1 us (23%)
  Pallas kernels  18.7 us (22%)
  waiting for transfers between devices  15.1 us (18%)
    all_to_all x1, blocking collectives, body(): stats = lax.all_to_all(local_stats, 'col', 0, 0, tiled=True)  19.1 us
    pallas_call x8, Pallas kernels, call(): pl.pallas_call(kernel, out_shape=outs, in_specs=[pl.BlockSpec(memory_spac...  18.7 us
    ppermute x10, starting transfers between devices, swapped(): lax.ppermute(a, axis, [(i, i ^ bits) for i in range(lax.axis_size(axis))])  17 us
    ppermute x10, waiting for transfers between devices, swapped(): lax.ppermute(a, axis, [(i, i ^ bits) for i in range(lax.axis_size(axis))])  11.5 us
    all_to_all x1, starting transfers between devices, body(): col_term = lax.all_to_all(col_term, 'row', 0, 0, tiled=True)  5.66 us
    ppermute x1, starting transfers between devices, body(): lax.ppermute(jnp.swapaxes(layernormed_alignment, 1, 2), ('row', 'col'), r...  3.92 us
    ppermute x1, waiting for transfers between devices, body(): other = lax.ppermute(mine, 'row', [(i, i ^ 1) for i in range(row_count)])  2.23 us
    ppermute x1, starting transfers between devices, body(): lax.ppermute(col_term, ('row', 'col'), [(r * col_count + c, c * col_count...  1.91 us
  transfers between devices with their start and end apart: 14, of which 8 were waited for; matrix products, arithmetic and copies ran while one was open for 1% of the time, Pallas kernels for 5%

profile of v6, /device:TPU:2, one launch (start us, length us, event | category | flops | bytes accessed | tf_op | source)
XLA Modules:
  0.0 83.3 jit_solution(2820124625953047695)
XLA Ops:
  0.6 3.9 %collective-permute-start = (bf16[32,64,192]{2,1,0:T(8,128)(2,1)}, bf16[32,64,192]{2,1,0:T(8,128)(2,1)S(1)}, u32[]{:S(2)}, u32[]{:S(2)}) collective-permute-start(bf16[32,64,192]{2,1,0:T(8,128)(2,1)} %bitcast.10), channel_id=1, source_target_pairs={{0,8},{9,1},{2,24},{11,17},{4,40},{13,33},{6,56},{15,49},{16,42},{... | collective-permute-start | bytes 2359304 | tf_op jit(solution)/shard_map/ppermute | solution.py:300
  4.6 0.8 dynamic_slice.3
  5.3 2.3 %shard_map.95 = f32[8,16,192]{2,1,0:T(8,128)S(1)} custom-call(f32[8,192,192]{2,1,0:T(8,128)} %scores_ref.3, s32[1,192]{1,0:T(1,128)S(1)} %bitcast.8), custom_call_target="tpu_custom_call" | custom-call | bytes 4194304 | tf_op jit(solution)/shard_map/pallas_call | solution.py:24
  7.6 19.1 %all_to_all.10.stats_ref = f32[8,16,192]{2,1,0:T(8,128)S(1)} all-to-all(f32[8,16,192]{2,1,0:T(8,128)S(1)} %shard_map.95), channel_id=1, replica_groups=mesh['seq'=4,'row'=8,'col'=8] {'col'}, dimensions={0} | all-to-all | bytes 196608 | tf_op jit(solution)/shard_map/all_to_all | solution.py:308
  26.7 0.0 collective-permute-done.mine_ref
  26.7 0.4 collective-permute-start.1
  27.1 0.1 pad_add_fusion.place_ref
  27.1 2.2 %collective-permute-done.1.other_ref = bf16[32,64,192]{2,1,0:T(8,128)(2,1)S(1)} collective-permute-done((bf16[32,64,192]{2,1,0:T(8,128)(2,1)S(1)}, bf16[32,64,192]{2,1,0:T(8,128)(2,1)S(1)}, u32[]{:S(2)}, u32[]{:S(2)}) %collective-permute-start.1) | collective-permute-done | bytes 786464 | tf_op jit(solution)/shard_map/ppermute | solution.py:311
  29.4 13.1 %shard_map.96 = (f32[2,192,192]{2,1,0:T(8,128)S(1)}, bf16[8,24,2048]{2,1,0:T(8,128)(2,1)}, bf16[2,24,2176]{2,1,0:T(8,128)(2,1)S(1)}, bf16[2,24,2176]{2,1,0:T(8,1...) custom-call(s32[4]{0:T(128)S(1)} %pad_add_fusion.place_ref, ...), custom_call_target="tpu_custom_call" | custom-call | flops 1073741824 | bytes 18874368 | tf_op jit(solution)/shard_map/pallas_call | solution.py:24
  42.4 0.0 copy-start
  42.5 5.7 %all-to-all-start.1 = ((bf16[8,24,2048]{2,1,0:T(8,128)(2,1)}), bf16[8,24,2048]{2,1,0:T(8,128)(2,1)S(1)}, u32[]{:S(2)}, u32[]{:S(2)}) async-start(bf16[8,24,2048]{2,1,0:T(8,128)(2,1)} %get-tuple-element.26), calls=%async_computation.1 | async-start | bytes 1572864 | tf_op jit(solution)/shard_map/all_to_all | solution.py:364
  48.1 0.0 copy-done
  48.1 1.0 %collective-permute-start.4 = (bf16[2,24,2176]{2,1,0:T(8,128)(2,1)S(1)}, bf16[2,24,2176]{2,1,0:T(8,128)(2,1)S(1)}, u32[]{:S(2)}, u32[]{:S(2)}) collective-permute-start(bf16[2,24,2176]{2,1,0:T(8,128)(2,1)S(1)} %copy-done), channel_id=1, source_target_pairs={{0,6},{1,7},{2,4},{3,5},{4,2},{5,3},{6,0},{7,1},{8,14},{9,15},{10,... | collective-permute-start | bytes 626696 | tf_op jit(solution)/shard_map/ppermute | solution.py:360
  49.1 0.1 collective-permute-start.2
  49.2 3.6 %collective-permute-start.3 = (bf16[2,24,2176]{2,1,0:T(8,128)(2,1)}, bf16[2,24,2176]{2,1,0:T(8,128)(2,1)S(1)}, u32[]{:S(2)}, u32[]{:S(2)}) collective-permute-start(bf16[2,24,2176]{2,1,0:T(8,128)(2,1)} %get-tuple-element.25), channel_id=1, source_target_pairs={{0,4},{1,5},{2,6},{3,7},{4,0},{5,1},{6,2},{7,3},{8,12},{9,13},{10,... | collective-permute-start | bytes 626696 | tf_op jit(solution)/shard_map/ppermute | solution.py:360
  52.8 1.6 %collective-permute-start.6 = (bf16[3,192,128]{2,1,0:T(8,128)(2,1)S(1)}, bf16[3,192,128]{2,1,0:T(8,128)(2,1)S(1)}, u32[]{:S(2)}, u32[]{:S(2)}) collective-permute-start(bf16[3,192,128]{2,1,0:T(8,128)(2,1)S(1)} %get-tuple-element.32), channel_id=1, source_target_pairs={{0,64},{64,0},{128,192},{192,128},{1,65},{65,1},{129,193},{193,129... | collective-permute-start | bytes 442376 | tf_op jit(solution)/shard_map/ppermute | solution.py:360
  54.4 0.9 %collective-permute-start.7 = (bf16[3,192,128]{2,1,0:T(8,128)(2,1)S(1)}, bf16[3,192,128]{2,1,0:T(8,128)(2,1)S(1)}, u32[]{:S(2)}, u32[]{:S(2)}) collective-permute-start(bf16[3,192,128]{2,1,0:T(8,128)(2,1)S(1)} %get-tuple-element.33), channel_id=1, source_target_pairs={{0,128},{64,192},{128,0},{192,64},{1,129},{65,193},{129,1},{193,65... | collective-permute-start | bytes 442376 | tf_op jit(solution)/shard_map/ppermute | solution.py:360
  55.3 1.2 %collective-permute-done.4.part3_ref = bf16[2,24,2176]{2,1,0:T(8,128)(2,1)S(1)} collective-permute-done((bf16[2,24,2176]{2,1,0:T(8,128)(2,1)S(1)}, bf16[2,24,2176]{2,1,0:T(8,128)(2,1)S(1)}, u32[]{:S(2)}, u32[]{:S(2)}) %collective-permute-start.4) | collective-permute-done | bytes 208928 | tf_op jit(solution)/shard_map/ppermute | solution.py:360
  56.5 1.9 %collective-permute-start.8 = (bf16[3,192,128]{2,1,0:T(8,128)(2,1)S(1)}, bf16[3,192,128]{2,1,0:T(8,128)(2,1)S(1)}, u32[]{:S(2)}, u32[]{:S(2)}) collective-permute-start(bf16[3,192,128]{2,1,0:T(8,128)(2,1)S(1)} %get-tuple-element.34), channel_id=1, source_target_pairs={{0,192},{64,128},{128,64},{192,0},{1,193},{65,129},{129,65},{193,1... | collective-permute-start | bytes 442376 | tf_op jit(solution)/shard_map/ppermute | solution.py:360
  58.5 1.4 %all-to-all-done.1.parts_ref = bf16[8,24,2048]{2,1,0:T(8,128)(2,1)S(1)} async-done(((bf16[8,24,2048]{2,1,0:T(8,128)(2,1)}), bf16[8,24,2048]{2,1,0:T(8,128)(2,1)S(1)}, u32[]{:S(2)}, u32[]{:S(2)}) %all-to-all-start.1) | async-done | bytes 786464 | tf_op jit(solution)/shard_map/all_to_all | solution.py:364
  59.8 0.1 shard_map.97
  59.9 0.0 collective-permute-done.2.part1_ref
  60.0 2.5 %collective-permute-done.3.part2_ref = bf16[2,24,2176]{2,1,0:T(8,128)(2,1)S(1)} collective-permute-done((bf16[2,24,2176]{2,1,0:T(8,128)(2,1)}, bf16[2,24,2176]{2,1,0:T(8,128)(2,1)S(1)}, u32[]{:S(2)}, u32[]{:S(2)}) %collective-permute-start.3) | collective-permute-done | bytes 208928 | tf_op jit(solution)/shard_map/ppermute | solution.py:360
  62.4 0.7 shard_map.98
  63.1 2.1 %collective-permute-start.5 = (bf16[24,2304]{1,0:T(8,128)(2,1)S(1)}, bf16[24,2304]{1,0:T(8,128)(2,1)S(1)}, u32[]{:S(2)}, u32[]{:S(2)}) collective-permute-start(bf16[24,2304]{1,0:T(8,128)(2,1)S(1)} %get-tuple-element.30), channel_id=1, source_target_pairs={{0,1},{1,0},{2,3},{3,2},{4,5},{5,4},{6,7},{7,6},{8,9},{9,8},{10,11... | collective-permute-start | bytes 331784 | tf_op jit(solution)/shard_map/ppermute | solution.py:360
  65.2 1.9 %collective-permute-start.9 = (bf16[24,2048]{1,0:T(8,128)(2,1)S(1)}, bf16[24,2048]{1,0:T(8,128)(2,1)S(1)}, u32[]{:S(2)}, u32[]{:S(2)}) collective-permute-start(bf16[24,2048]{1,0:T(8,128)(2,1)S(1)} %shard_map.97), channel_id=1, source_target_pairs={{0,0},{1,8},{2,16},{3,24},{4,32},{5,40},{6,48},{7,56},{8,1},{9,9},... | collective-permute-start | bytes 294920 | tf_op jit(solution)/shard_map/ppermute | solution.py:367
  67.1 0.0 collective-permute-done.6.part1_ref
  67.1 3.5 %collective-permute-done.7.part2_ref = bf16[3,192,128]{2,1,0:T(8,128)(2,1)S(1)} collective-permute-done((bf16[3,192,128]{2,1,0:T(8,128)(2,1)S(1)}, bf16[3,192,128]{2,1,0:T(8,128)(2,1)S(1)}, u32[]{:S(2)}, u32[]{:S(2)}) %collective-permute-start.7) | collective-permute-done | bytes 147488 | tf_op jit(solution)/shard_map/ppermute | solution.py:360
  70.6 0.0 collective-permute-done.8.part3_ref
  70.6 0.2 shard_map.99.grad_ref
  70.8 1.5 %collective-permute-done.5.rows_ref = bf16[24,2304]{1,0:T(8,128)(2,1)S(1)} collective-permute-done((bf16[24,2304]{1,0:T(8,128)(2,1)S(1)}, bf16[24,2304]{1,0:T(8,128)(2,1)S(1)}, u32[]{:S(2)}, u32[]{:S(2)}) %collective-permute-start.5) | collective-permute-done | bytes 110624 | tf_op jit(solution)/shard_map/ppermute | solution.py:360
  72.3 1.9 %collective-permute-start.12 = (f32[8,256]{1,0:T(8,128)S(1)}, f32[8,256]{1,0:T(8,128)S(1)}, u32[]{:S(2)}, u32[]{:S(2)}) collective-permute-start(f32[8,256]{1,0:T(8,128)S(1)} %shard_map.101.inner0_ref), channel_id=1, source_target_pairs={{0,192},{64,128},{128,64},{192,0},{1,193},{65,129},{129,65},{193,1... | collective-permute-start | bytes 24584 | tf_op jit(solution)/shard_map/ppermute | solution.py:360
  74.2 3.8 %collective-permute-start.11 = (f32[8,256]{1,0:T(8,128)S(1)}, f32[8,256]{1,0:T(8,128)S(1)}, u32[]{:S(2)}, u32[]{:S(2)}) collective-permute-start(f32[8,256]{1,0:T(8,128)S(1)} %shard_map.101.inner0_ref), channel_id=1, source_target_pairs={{0,128},{64,192},{128,0},{192,64},{1,129},{65,193},{129,1},{193,65... | collective-permute-start | bytes 24584 | tf_op jit(solution)/shard_map/ppermute | solution.py:360
  78.1 0.0 collective-permute-start.10
  78.1 0.0 collective-permute-done.9.cols_ref
  78.1 0.9 %shard_map.100 = f32[32,24,64]{2,1,0:T(8,128)} custom-call(f32[24,2048]{1,0:T(8,128)S(1)} %get-tuple-element.29.keep_ref, bf16[24,2304]{1,0:T(8,128)(2,1)S(1)} %collective-permute-done.5.rows_ref, bf16[24,2048]{1,0:T(8,128)(2,1)S(1)} %collective-permute-done.9.cols_ref), custom_call_target="tpu_custom_call" | custom-call | bytes 2097152 | tf_op jit(solution)/shard_map/pallas_call | solution.py:24
  78.9 0.0 collective-permute-done.12.inner3_ref
  78.9 0.8 collective-permute-done.11.inner2_ref
  79.8 1.9 %collective-permute-done.10.inner1_ref = f32[8,256]{1,0:T(8,128)S(1)} collective-permute-done((f32[8,256]{1,0:T(8,128)S(1)}, f32[8,256]{1,0:T(8,128)S(1)}, u32[]{:S(2)}, u32[]{:S(2)}) %collective-permute-start.10) | collective-permute-done | bytes 8224 | tf_op jit(solution)/shard_map/ppermute | solution.py:360
  81.7 1.6 %shard_map.102 = f32[2,192,192]{2,1,0:T(8,128)} custom-call(s32[4]{0:T(128)S(1)} %pad_add_fusion.place_ref, f32[8,256]{1,0:T(8,128)S(1)} %shard_map.101.inner0_ref, f32[8,256]{1,0:T(8,128)S(1)} %collective-permute-done.10.inner1_ref, f32[8,256]{1,0:T(8,128)S(1)} %collective-permute-done.11.inner2_ref, f32[8,256]{1,0:T(8,128)S(1)} %collective-permute-done.12.inner3_ref, ...), custom_call_target="tpu_custom_call" | custom-call | bytes 2097152 | tf_op jit(solution)/shard_map/pallas_call | solution.py:24
  (1 shorter events, 0.0 us)
Async XLA Ops:
  0.6 26.1 %collective-permute-start = (bf16[32,64,192]{2,1,0:T(8,128)(2,1)}, bf16[32,64,192]{2,1,0:T(8,128)(2,1)S(1)}, u32[]{:S(2)}, u32[]{:S(2)}) collective-permute-start(bf16[32,64,192]{2,1,0:T(8,128)(2,1)} %bitcast.10), channel_id=1, source_target_pairs={{0,8},{9,1},{2,24},{11,17},{4,40},{13,33},{6,56},{15,49},{16,42},{... | collective-permute-start | bytes 2359304 | tf_op jit(solution)/shard_map/ppermute | solution.py:300
  26.7 2.7 %collective-permute-start.1 = (bf16[32,64,192]{2,1,0:T(8,128)(2,1)S(1)}, bf16[32,64,192]{2,1,0:T(8,128)(2,1)S(1)}, u32[]{:S(2)}, u32[]{:S(2)}) collective-permute-start(bf16[32,64,192]{2,1,0:T(8,128)(2,1)S(1)} %collective-permute-done.mine_ref), channel_id=1, source_target_pairs={{0,8},{8,0},{16,24},{24,16},{32,40},{40,32},{48,56},{56,48},{1,9},... | collective-permute-start | bytes 2359304 | tf_op jit(solution)/shard_map/ppermute | solution.py:311
  42.4 5.7 %copy-start = (bf16[2,24,2176]{2,1,0:T(8,128)(2,1)S(1)}, bf16[2,24,2176]{2,1,0:T(8,128)(2,1)}, u32[]{:S(2)}) copy-start(bf16[2,24,2176]{2,1,0:T(8,128)(2,1)} %get-tuple-element.27) | copy-start | bytes 626692
  42.5 17.4 %all-to-all-start.1 = ((bf16[8,24,2048]{2,1,0:T(8,128)(2,1)}), bf16[8,24,2048]{2,1,0:T(8,128)(2,1)S(1)}, u32[]{:S(2)}, u32[]{:S(2)}) async-start(bf16[8,24,2048]{2,1,0:T(8,128)(2,1)} %get-tuple-element.26), calls=%async_computation.1 | async-start | bytes 1572864 | tf_op jit(solution)/shard_map/all_to_all | solution.py:364
  48.1 8.4 %collective-permute-start.4 = (bf16[2,24,2176]{2,1,0:T(8,128)(2,1)S(1)}, bf16[2,24,2176]{2,1,0:T(8,128)(2,1)S(1)}, u32[]{:S(2)}, u32[]{:S(2)}) collective-permute-start(bf16[2,24,2176]{2,1,0:T(8,128)(2,1)S(1)} %copy-done), channel_id=1, source_target_pairs={{0,6},{1,7},{2,4},{3,5},{4,2},{5,3},{6,0},{7,1},{8,14},{9,15},{10,... | collective-permute-start | bytes 626696 | tf_op jit(solution)/shard_map/ppermute | solution.py:360
  49.1 10.8 %collective-permute-start.2 = (bf16[2,24,2176]{2,1,0:T(8,128)(2,1)}, bf16[2,24,2176]{2,1,0:T(8,128)(2,1)S(1)}, u32[]{:S(2)}, u32[]{:S(2)}) collective-permute-start(bf16[2,24,2176]{2,1,0:T(8,128)(2,1)} %get-tuple-element.24), channel_id=1, source_target_pairs={{0,2},{1,3},{2,0},{3,1},{4,6},{5,7},{6,4},{7,5},{8,10},{9,11},{10,... | collective-permute-start | bytes 626696 | tf_op jit(solution)/shard_map/ppermute | solution.py:360
  49.2 13.2 %collective-permute-start.3 = (bf16[2,24,2176]{2,1,0:T(8,128)(2,1)}, bf16[2,24,2176]{2,1,0:T(8,128)(2,1)S(1)}, u32[]{:S(2)}, u32[]{:S(2)}) collective-permute-start(bf16[2,24,2176]{2,1,0:T(8,128)(2,1)} %get-tuple-element.25), channel_id=1, source_target_pairs={{0,4},{1,5},{2,6},{3,7},{4,0},{5,1},{6,2},{7,3},{8,12},{9,13},{10,... | collective-permute-start | bytes 626696 | tf_op jit(solution)/shard_map/ppermute | solution.py:360
  52.8 14.3 %collective-permute-start.6 = (bf16[3,192,128]{2,1,0:T(8,128)(2,1)S(1)}, bf16[3,192,128]{2,1,0:T(8,128)(2,1)S(1)}, u32[]{:S(2)}, u32[]{:S(2)}) collective-permute-start(bf16[3,192,128]{2,1,0:T(8,128)(2,1)S(1)} %get-tuple-element.32), channel_id=1, source_target_pairs={{0,64},{64,0},{128,192},{192,128},{1,65},{65,1},{129,193},{193,129... | collective-permute-start | bytes 442376 | tf_op jit(solution)/shard_map/ppermute | solution.py:360
  54.4 16.2 %collective-permute-start.7 = (bf16[3,192,128]{2,1,0:T(8,128)(2,1)S(1)}, bf16[3,192,128]{2,1,0:T(8,128)(2,1)S(1)}, u32[]{:S(2)}, u32[]{:S(2)}) collective-permute-start(bf16[3,192,128]{2,1,0:T(8,128)(2,1)S(1)} %get-tuple-element.33), channel_id=1, source_target_pairs={{0,128},{64,192},{128,0},{192,64},{1,129},{65,193},{129,1},{193,65... | collective-permute-start | bytes 442376 | tf_op jit(solution)/shard_map/ppermute | solution.py:360
  56.5 14.1 %collective-permute-start.8 = (bf16[3,192,128]{2,1,0:T(8,128)(2,1)S(1)}, bf16[3,192,128]{2,1,0:T(8,128)(2,1)S(1)}, u32[]{:S(2)}, u32[]{:S(2)}) collective-permute-start(bf16[3,192,128]{2,1,0:T(8,128)(2,1)S(1)} %get-tuple-element.34), channel_id=1, source_target_pairs={{0,192},{64,128},{128,64},{192,0},{1,193},{65,129},{129,65},{193,1... | collective-permute-start | bytes 442376 | tf_op jit(solution)/shard_map/ppermute | solution.py:360
  63.1 9.2 %collective-permute-start.5 = (bf16[24,2304]{1,0:T(8,128)(2,1)S(1)}, bf16[24,2304]{1,0:T(8,128)(2,1)S(1)}, u32[]{:S(2)}, u32[]{:S(2)}) collective-permute-start(bf16[24,2304]{1,0:T(8,128)(2,1)S(1)} %get-tuple-element.30), channel_id=1, source_target_pairs={{0,1},{1,0},{2,3},{3,2},{4,5},{5,4},{6,7},{7,6},{8,9},{9,8},{10,11... | collective-permute-start | bytes 331784 | tf_op jit(solution)/shard_map/ppermute | solution.py:360
  65.2 12.9 %collective-permute-start.9 = (bf16[24,2048]{1,0:T(8,128)(2,1)S(1)}, bf16[24,2048]{1,0:T(8,128)(2,1)S(1)}, u32[]{:S(2)}, u32[]{:S(2)}) collective-permute-start(bf16[24,2048]{1,0:T(8,128)(2,1)S(1)} %shard_map.97), channel_id=1, source_target_pairs={{0,0},{1,8},{2,16},{3,24},{4,32},{5,40},{6,48},{7,56},{8,1},{9,9},... | collective-permute-start | bytes 294920 | tf_op jit(solution)/shard_map/ppermute | solution.py:367
  72.3 6.7 %collective-permute-start.12 = (f32[8,256]{1,0:T(8,128)S(1)}, f32[8,256]{1,0:T(8,128)S(1)}, u32[]{:S(2)}, u32[]{:S(2)}) collective-permute-start(f32[8,256]{1,0:T(8,128)S(1)} %shard_map.101.inner0_ref), channel_id=1, source_target_pairs={{0,192},{64,128},{128,64},{192,0},{1,193},{65,129},{129,65},{193,1... | collective-permute-start | bytes 24584 | tf_op jit(solution)/shard_map/ppermute | solution.py:360
  74.2 5.6 %collective-permute-start.11 = (f32[8,256]{1,0:T(8,128)S(1)}, f32[8,256]{1,0:T(8,128)S(1)}, u32[]{:S(2)}, u32[]{:S(2)}) collective-permute-start(f32[8,256]{1,0:T(8,128)S(1)} %shard_map.101.inner0_ref), channel_id=1, source_target_pairs={{0,128},{64,192},{128,0},{192,64},{1,129},{65,193},{129,1},{193,65... | collective-permute-start | bytes 24584 | tf_op jit(solution)/shard_map/ppermute | solution.py:360
  78.1 3.7 %collective-permute-start.10 = (f32[8,256]{1,0:T(8,128)S(1)}, f32[8,256]{1,0:T(8,128)S(1)}, u32[]{:S(2)}, u32[]{:S(2)}) collective-permute-start(f32[8,256]{1,0:T(8,128)S(1)} %shard_map.101.inner0_ref), channel_id=1, source_target_pairs={{0,64},{64,0},{128,192},{192,128},{1,65},{65,1},{129,193},{193,129... | collective-permute-start | bytes 24584 | tf_op jit(solution)/shard_map/ppermute | solution.py:360

commit v7 on v5

--- a/solution.py
+++ b/solution.py
@@ -8,8 +8,8 @@
 F32 = jnp.float32
 BF16 = jnp.bfloat16
 MASKED = -1000000000.0
-VMEM_BYTES = 32 * 1024 * 1024
-STEPS = 2
+VMEM_BYTES = 48 * 1024 * 1024
+STEPS = 1
 
 
 def call(kernel, outs, inputs, in_specs=None, out_specs=None, grid=None, scratch=(), scalars=None, flops=0, moved=0):

time: 84.1 us -> 83 us (0.987)
  Pallas kernels: 18.6 us -> 17.5 us
    pallas_call x7, Pallas kernels: 18.6 us -> 17.5 us  [call(): pl.pallas_call(kernel, out_shape=outs, in_specs=[pl.BlockSpec(memory_spac...]
where the time goes in v7:
time: 83 us; the launch traced here: 81.7 us
  starting transfers between devices  28.2 us (34%)
  blocking collectives  19.1 us (23%)
  Pallas kernels  17.5 us (21%)
  waiting for transfers between devices  15.2 us (18%)
    all_to_all x1, blocking collectives, body(): stats = lax.all_to_all(local_stats, 'col', 0, 0, tiled=True)  19.1 us
    pallas_call x7, Pallas kernels, call(): pl.pallas_call(kernel, out_shape=outs, in_specs=[pl.BlockSpec(memory_spac...  17.5 us
    ppermute x10, starting transfers between devices, swapped(): lax.ppermute(a, axis, [(i, i ^ bits) for i in range(lax.axis_size(axis))])  16.4 us
    ppermute x10, waiting for transfers between devices, swapped(): lax.ppermute(a, axis, [(i, i ^ bits) for i in range(lax.axis_size(axis))])  11.9 us
    all_to_all x1, starting transfers between devices, body(): col_term = lax.all_to_all(col_term, 'row', 0, 0, tiled=True)  5.65 us
    ppermute x1, starting transfers between devices, body(): lax.ppermute(jnp.swapaxes(layernormed_alignment, 1, 2), ('row', 'col'), r...  3.92 us
    ppermute x1, waiting for transfers between devices, body(): other = lax.ppermute(mine, 'row', [(i, i ^ 1) for i in range(row_count)])  2.23 us
    ppermute x1, starting transfers between devices, body(): lax.ppermute(col_term, ('row', 'col'), [(r * col_count + c, c * col_count...  1.91 us
  transfers between devices with their start and end apart: 14, of which 7 were waited for; matrix products, arithmetic and copies ran while one was open for 1% of the time, Pallas kernels for 5%

profile of v7, /device:TPU:2, one launch (start us, length us, event | category | flops | bytes accessed | tf_op | source)
XLA Modules:
  0.0 81.7 jit_solution(13005472728304998864)
XLA Ops:
  0.6 3.9 %collective-permute-start = (bf16[32,64,192]{2,1,0:T(8,128)(2,1)}, bf16[32,64,192]{2,1,0:T(8,128)(2,1)S(1)}, u32[]{:S(2)}, u32[]{:S(2)}) collective-permute-start(bf16[32,64,192]{2,1,0:T(8,128)(2,1)} %bitcast.10), channel_id=1, source_target_pairs={{0,8},{9,1},{2,24},{11,17},{4,40},{13,33},{6,56},{15,49},{16,42},{... | collective-permute-start | bytes 2359304 | tf_op jit(solution)/shard_map/ppermute | solution.py:306
  4.6 0.8 dynamic_slice.3
  5.3 2.3 %shard_map.95 = f32[8,16,192]{2,1,0:T(8,128)S(1)} custom-call(f32[8,192,192]{2,1,0:T(8,128)} %scores_ref.3, s32[1,192]{1,0:T(1,128)S(1)} %bitcast.8), custom_call_target="tpu_custom_call" | custom-call | bytes 4194304 | tf_op jit(solution)/shard_map/pallas_call | solution.py:24
  7.6 19.1 %all_to_all.10.stats_ref = f32[8,16,192]{2,1,0:T(8,128)S(1)} all-to-all(f32[8,16,192]{2,1,0:T(8,128)S(1)} %shard_map.95), channel_id=1, replica_groups=mesh['seq'=4,'row'=8,'col'=8] {'col'}, dimensions={0} | all-to-all | bytes 196608 | tf_op jit(solution)/shard_map/all_to_all | solution.py:314
  26.7 0.0 collective-permute-done.mine_ref
  26.7 0.4 collective-permute-start.1
  27.1 0.1 pad_add_fusion.place_ref
  27.1 2.2 %collective-permute-done.1.other_ref = bf16[32,64,192]{2,1,0:T(8,128)(2,1)S(1)} collective-permute-done((bf16[32,64,192]{2,1,0:T(8,128)(2,1)S(1)}, bf16[32,64,192]{2,1,0:T(8,128)(2,1)S(1)}, u32[]{:S(2)}, u32[]{:S(2)}) %collective-permute-start.1) | collective-permute-done | bytes 786464 | tf_op jit(solution)/shard_map/ppermute | solution.py:317
  29.4 12.0 %shard_map.96 = (f32[2,192,192]{2,1,0:T(8,128)S(1)}, bf16[8,24,2048]{2,1,0:T(8,128)(2,1)}, bf16[2,24,2176]{2,1,0:T(8,128)(2,1)S(1)}, bf16[2,24,2176]{2,1,0:T(8,1...) custom-call(s32[4]{0:T(128)S(1)} %pad_add_fusion.place_ref, ...), custom_call_target="tpu_custom_call" | custom-call | flops 1073741824 | bytes 18874368 | tf_op jit(solution)/shard_map/pallas_call | solution.py:24
  41.4 0.0 copy-start
  41.4 5.6 %all-to-all-start.1 = ((bf16[8,24,2048]{2,1,0:T(8,128)(2,1)}), bf16[8,24,2048]{2,1,0:T(8,128)(2,1)S(1)}, u32[]{:S(2)}, u32[]{:S(2)}) async-start(bf16[8,24,2048]{2,1,0:T(8,128)(2,1)} %get-tuple-element.24), calls=%async_computation.1 | async-start | bytes 1572864 | tf_op jit(solution)/shard_map/all_to_all | solution.py:370
  47.0 1.0 %collective-permute-start.4 = (bf16[2,24,2176]{2,1,0:T(8,128)(2,1)}, bf16[2,24,2176]{2,1,0:T(8,128)(2,1)S(1)}, u32[]{:S(2)}, u32[]{:S(2)}) collective-permute-start(bf16[2,24,2176]{2,1,0:T(8,128)(2,1)} %get-tuple-element.25), channel_id=1, source_target_pairs={{0,6},{1,7},{2,4},{3,5},{4,2},{5,3},{6,0},{7,1},{8,14},{9,15},{10,... | collective-permute-start | bytes 626696 | tf_op jit(solution)/shard_map/ppermute | solution.py:366
  48.0 0.1 collective-permute-start.2
  48.2 0.0 copy-done
  48.2 3.6 %collective-permute-start.3 = (bf16[2,24,2176]{2,1,0:T(8,128)(2,1)S(1)}, bf16[2,24,2176]{2,1,0:T(8,128)(2,1)S(1)}, u32[]{:S(2)}, u32[]{:S(2)}) collective-permute-start(bf16[2,24,2176]{2,1,0:T(8,128)(2,1)S(1)} %copy-done), channel_id=1, source_target_pairs={{0,4},{1,5},{2,6},{3,7},{4,0},{5,1},{6,2},{7,3},{8,12},{9,13},{10,... | collective-permute-start | bytes 626696 | tf_op jit(solution)/shard_map/ppermute | solution.py:366
  51.7 1.6 %collective-permute-start.7 = (bf16[3,192,128]{2,1,0:T(8,128)(2,1)S(1)}, bf16[3,192,128]{2,1,0:T(8,128)(2,1)S(1)}, u32[]{:S(2)}, u32[]{:S(2)}) collective-permute-start(bf16[3,192,128]{2,1,0:T(8,128)(2,1)S(1)} %get-tuple-element.31), channel_id=1, source_target_pairs={{0,64},{64,0},{128,192},{192,128},{1,65},{65,1},{129,193},{193,129... | collective-permute-start | bytes 442376 | tf_op jit(solution)/shard_map/ppermute | solution.py:366
  53.4 0.9 %collective-permute-start.8 = (bf16[3,192,128]{2,1,0:T(8,128)(2,1)S(1)}, bf16[3,192,128]{2,1,0:T(8,128)(2,1)S(1)}, u32[]{:S(2)}, u32[]{:S(2)}) collective-permute-start(bf16[3,192,128]{2,1,0:T(8,128)(2,1)S(1)} %get-tuple-element.32), channel_id=1, source_target_pairs={{0,128},{64,192},{128,0},{192,64},{1,129},{65,193},{129,1},{193,65... | collective-permute-start | bytes 442376 | tf_op jit(solution)/shard_map/ppermute | solution.py:366
  54.2 1.4 %collective-permute-done.4.part3_ref = bf16[2,24,2176]{2,1,0:T(8,128)(2,1)S(1)} collective-permute-done((bf16[2,24,2176]{2,1,0:T(8,128)(2,1)}, bf16[2,24,2176]{2,1,0:T(8,128)(2,1)S(1)}, u32[]{:S(2)}, u32[]{:S(2)}) %collective-permute-start.4) | collective-permute-done | bytes 208928 | tf_op jit(solution)/shard_map/ppermute | solution.py:366
  55.7 1.9 %collective-permute-start.9 = (bf16[3,192,128]{2,1,0:T(8,128)(2,1)S(1)}, bf16[3,192,128]{2,1,0:T(8,128)(2,1)S(1)}, u32[]{:S(2)}, u32[]{:S(2)}) collective-permute-start(bf16[3,192,128]{2,1,0:T(8,128)(2,1)S(1)} %get-tuple-element.33), channel_id=1, source_target_pairs={{0,192},{64,128},{128,64},{192,0},{1,193},{65,129},{129,65},{193,1... | collective-permute-start | bytes 442376 | tf_op jit(solution)/shard_map/ppermute | solution.py:366
  57.6 1.1 %all-to-all-done.1.parts_ref = bf16[8,24,2048]{2,1,0:T(8,128)(2,1)S(1)} async-done(((bf16[8,24,2048]{2,1,0:T(8,128)(2,1)}), bf16[8,24,2048]{2,1,0:T(8,128)(2,1)S(1)}, u32[]{:S(2)}, u32[]{:S(2)}) %all-to-all-start.1) | async-done | bytes 786464 | tf_op jit(solution)/shard_map/all_to_all | solution.py:370
  58.8 0.1 shard_map.97
  58.9 0.0 collective-permute-done.2.part1_ref
  58.9 2.5 %collective-permute-done.3.part2_ref = bf16[2,24,2176]{2,1,0:T(8,128)(2,1)S(1)} collective-permute-done((bf16[2,24,2176]{2,1,0:T(8,128)(2,1)S(1)}, bf16[2,24,2176]{2,1,0:T(8,128)(2,1)S(1)}, u32[]{:S(2)}, u32[]{:S(2)}) %collective-permute-start.3) | collective-permute-done | bytes 208928 | tf_op jit(solution)/shard_map/ppermute | solution.py:366
  61.3 0.7 shard_map.98
  62.0 2.1 %collective-permute-start.5 = (bf16[24,2304]{1,0:T(8,128)(2,1)S(1)}, bf16[24,2304]{1,0:T(8,128)(2,1)S(1)}, u32[]{:S(2)}, u32[]{:S(2)}) collective-permute-start(bf16[24,2304]{1,0:T(8,128)(2,1)S(1)} %get-tuple-element.28), channel_id=1, source_target_pairs={{0,1},{1,0},{2,3},{3,2},{4,5},{5,4},{6,7},{7,6},{8,9},{9,8},{10,11... | collective-permute-start | bytes 331784 | tf_op jit(solution)/shard_map/ppermute | solution.py:366
  64.1 1.9 %collective-permute-start.6 = (bf16[24,2048]{1,0:T(8,128)(2,1)S(1)}, bf16[24,2048]{1,0:T(8,128)(2,1)S(1)}, u32[]{:S(2)}, u32[]{:S(2)}) collective-permute-start(bf16[24,2048]{1,0:T(8,128)(2,1)S(1)} %shard_map.97), channel_id=1, source_target_pairs={{0,0},{1,8},{2,16},{3,24},{4,32},{5,40},{6,48},{7,56},{8,1},{9,9},... | collective-permute-start | bytes 294920 | tf_op jit(solution)/shard_map/ppermute | solution.py:373
  66.0 5.2 %collective-permute-done.5.rows_ref = bf16[24,2304]{1,0:T(8,128)(2,1)S(1)} collective-permute-done((bf16[24,2304]{1,0:T(8,128)(2,1)S(1)}, bf16[24,2304]{1,0:T(8,128)(2,1)S(1)}, u32[]{:S(2)}, u32[]{:S(2)}) %collective-permute-start.5) | collective-permute-done | bytes 110624 | tf_op jit(solution)/shard_map/ppermute | solution.py:366
  71.2 1.9 %collective-permute-start.12 = (f32[8,256]{1,0:T(8,128)S(1)}, f32[8,256]{1,0:T(8,128)S(1)}, u32[]{:S(2)}, u32[]{:S(2)}) collective-permute-start(f32[8,256]{1,0:T(8,128)S(1)} %shard_map.100.inner0_ref), channel_id=1, source_target_pairs={{0,192},{64,128},{128,64},{192,0},{1,193},{65,129},{129,65},{193,1... | collective-permute-start | bytes 24584 | tf_op jit(solution)/shard_map/ppermute | solution.py:366
  73.2 0.0 collective-permute-done.7.part1_ref
  73.2 3.2 %collective-permute-start.11 = (f32[8,256]{1,0:T(8,128)S(1)}, f32[8,256]{1,0:T(8,128)S(1)}, u32[]{:S(2)}, u32[]{:S(2)}) collective-permute-start(f32[8,256]{1,0:T(8,128)S(1)} %shard_map.100.inner0_ref), channel_id=1, source_target_pairs={{0,128},{64,192},{128,0},{192,64},{1,129},{65,193},{129,1},{193,65... | collective-permute-start | bytes 24584 | tf_op jit(solution)/shard_map/ppermute | solution.py:366
  76.4 0.0 collective-permute-done.6.cols_ref
  76.4 0.0 collective-permute-start.10
  76.4 0.9 %shard_map.99 = f32[32,24,64]{2,1,0:T(8,128)} custom-call(f32[24,2048]{1,0:T(8,128)S(1)} %get-tuple-element.27.keep_ref, bf16[24,2304]{1,0:T(8,128)(2,1)S(1)} %collective-permute-done.5.rows_ref, bf16[24,2048]{1,0:T(8,128)(2,1)S(1)} %collective-permute-done.6.cols_ref), custom_call_target="tpu_custom_call" | custom-call | bytes 2097152 | tf_op jit(solution)/shard_map/pallas_call | solution.py:24
  77.3 0.0 collective-permute-done.8.part2_ref
  77.3 0.0 collective-permute-done.9.part3_ref
  77.3 0.0 collective-permute-done.12.inner3_ref
  77.3 0.8 collective-permute-done.11.inner2_ref
  78.1 1.9 %collective-permute-done.10.inner1_ref = f32[8,256]{1,0:T(8,128)S(1)} collective-permute-done((f32[8,256]{1,0:T(8,128)S(1)}, f32[8,256]{1,0:T(8,128)S(1)}, u32[]{:S(2)}, u32[]{:S(2)}) %collective-permute-start.10) | collective-permute-done | bytes 8224 | tf_op jit(solution)/shard_map/ppermute | solution.py:366
  80.1 1.6 %shard_map.101 = f32[2,192,192]{2,1,0:T(8,128)} custom-call(s32[4]{0:T(128)S(1)} %pad_add_fusion.place_ref, bf16[3,192,128]{2,1,0:T(8,128)(2,1)S(1)} %get-tuple-element.30.part0_ref, bf16[3,192,128]{2,1,0:T(8,128)(2,1)S(1)} %collective-permute-done.7.part1_ref, bf16[3,192,128]{2,1,0:T(8,128)(2,1)S(1)} %collective-permute-done.8.part2_ref, ...), custom_call_target="tpu_custom_call" | custom-call | bytes 2097152 | tf_op jit(solution)/shard_map/pallas_call | solution.py:24
  (1 shorter events, 0.0 us)
Async XLA Ops:
  0.6 26.1 %collective-permute-start = (bf16[32,64,192]{2,1,0:T(8,128)(2,1)}, bf16[32,64,192]{2,1,0:T(8,128)(2,1)S(1)}, u32[]{:S(2)}, u32[]{:S(2)}) collective-permute-start(bf16[32,64,192]{2,1,0:T(8,128)(2,1)} %bitcast.10), channel_id=1, source_target_pairs={{0,8},{9,1},{2,24},{11,17},{4,40},{13,33},{6,56},{15,49},{16,42},{... | collective-permute-start | bytes 2359304 | tf_op jit(solution)/shard_map/ppermute | solution.py:306
  26.7 2.7 %collective-permute-start.1 = (bf16[32,64,192]{2,1,0:T(8,128)(2,1)S(1)}, bf16[32,64,192]{2,1,0:T(8,128)(2,1)S(1)}, u32[]{:S(2)}, u32[]{:S(2)}) collective-permute-start(bf16[32,64,192]{2,1,0:T(8,128)(2,1)S(1)} %collective-permute-done.mine_ref), channel_id=1, source_target_pairs={{0,8},{8,0},{16,24},{24,16},{32,40},{40,32},{48,56},{56,48},{1,9},... | collective-permute-start | bytes 2359304 | tf_op jit(solution)/shard_map/ppermute | solution.py:317
  41.4 6.8 %copy-start = (bf16[2,24,2176]{2,1,0:T(8,128)(2,1)S(1)}, bf16[2,24,2176]{2,1,0:T(8,128)(2,1)}, u32[]{:S(2)}) copy-start(bf16[2,24,2176]{2,1,0:T(8,128)(2,1)} %get-tuple-element.23) | copy-start | bytes 626692
  41.4 17.4 %all-to-all-start.1 = ((bf16[8,24,2048]{2,1,0:T(8,128)(2,1)}), bf16[8,24,2048]{2,1,0:T(8,128)(2,1)S(1)}, u32[]{:S(2)}, u32[]{:S(2)}) async-start(bf16[8,24,2048]{2,1,0:T(8,128)(2,1)} %get-tuple-element.24), calls=%async_computation.1 | async-start | bytes 1572864 | tf_op jit(solution)/shard_map/all_to_all | solution.py:370
  47.0 8.6 %collective-permute-start.4 = (bf16[2,24,2176]{2,1,0:T(8,128)(2,1)}, bf16[2,24,2176]{2,1,0:T(8,128)(2,1)S(1)}, u32[]{:S(2)}, u32[]{:S(2)}) collective-permute-start(bf16[2,24,2176]{2,1,0:T(8,128)(2,1)} %get-tuple-element.25), channel_id=1, source_target_pairs={{0,6},{1,7},{2,4},{3,5},{4,2},{5,3},{6,0},{7,1},{8,14},{9,15},{10,... | collective-permute-start | bytes 626696 | tf_op jit(solution)/shard_map/ppermute | solution.py:366
  48.0 10.8 %collective-permute-start.2 = (bf16[2,24,2176]{2,1,0:T(8,128)(2,1)}, bf16[2,24,2176]{2,1,0:T(8,128)(2,1)S(1)}, u32[]{:S(2)}, u32[]{:S(2)}) collective-permute-start(bf16[2,24,2176]{2,1,0:T(8,128)(2,1)} %get-tuple-element.22), channel_id=1, source_target_pairs={{0,2},{1,3},{2,0},{3,1},{4,6},{5,7},{6,4},{7,5},{8,10},{9,11},{10,... | collective-permute-start | bytes 626696 | tf_op jit(solution)/shard_map/ppermute | solution.py:366
  48.2 13.2 %collective-permute-start.3 = (bf16[2,24,2176]{2,1,0:T(8,128)(2,1)S(1)}, bf16[2,24,2176]{2,1,0:T(8,128)(2,1)S(1)}, u32[]{:S(2)}, u32[]{:S(2)}) collective-permute-start(bf16[2,24,2176]{2,1,0:T(8,128)(2,1)S(1)} %copy-done), channel_id=1, source_target_pairs={{0,4},{1,5},{2,6},{3,7},{4,0},{5,1},{6,2},{7,3},{8,12},{9,13},{10,... | collective-permute-start | bytes 626696 | tf_op jit(solution)/shard_map/ppermute | solution.py:366
  51.7 21.4 %collective-permute-start.7 = (bf16[3,192,128]{2,1,0:T(8,128)(2,1)S(1)}, bf16[3,192,128]{2,1,0:T(8,128)(2,1)S(1)}, u32[]{:S(2)}, u32[]{:S(2)}) collective-permute-start(bf16[3,192,128]{2,1,0:T(8,128)(2,1)S(1)} %get-tuple-element.31), channel_id=1, source_target_pairs={{0,64},{64,0},{128,192},{192,128},{1,65},{65,1},{129,193},{193,129... | collective-permute-start | bytes 442376 | tf_op jit(solution)/shard_map/ppermute | solution.py:366
  53.4 23.9 %collective-permute-start.8 = (bf16[3,192,128]{2,1,0:T(8,128)(2,1)S(1)}, bf16[3,192,128]{2,1,0:T(8,128)(2,1)S(1)}, u32[]{:S(2)}, u32[]{:S(2)}) collective-permute-start(bf16[3,192,128]{2,1,0:T(8,128)(2,1)S(1)} %get-tuple-element.32), channel_id=1, source_target_pairs={{0,128},{64,192},{128,0},{192,64},{1,129},{65,193},{129,1},{193,65... | collective-permute-start | bytes 442376 | tf_op jit(solution)/shard_map/ppermute | solution.py:366
  55.7 21.6 %collective-permute-start.9 = (bf16[3,192,128]{2,1,0:T(8,128)(2,1)S(1)}, bf16[3,192,128]{2,1,0:T(8,128)(2,1)S(1)}, u32[]{:S(2)}, u32[]{:S(2)}) collective-permute-start(bf16[3,192,128]{2,1,0:T(8,128)(2,1)S(1)} %get-tuple-element.33), channel_id=1, source_target_pairs={{0,192},{64,128},{128,64},{192,0},{1,193},{65,129},{129,65},{193,1... | collective-permute-start | bytes 442376 | tf_op jit(solution)/shard_map/ppermute | solution.py:366
  62.0 9.2 %collective-permute-start.5 = (bf16[24,2304]{1,0:T(8,128)(2,1)S(1)}, bf16[24,2304]{1,0:T(8,128)(2,1)S(1)}, u32[]{:S(2)}, u32[]{:S(2)}) collective-permute-start(bf16[24,2304]{1,0:T(8,128)(2,1)S(1)} %get-tuple-element.28), channel_id=1, source_target_pairs={{0,1},{1,0},{2,3},{3,2},{4,5},{5,4},{6,7},{7,6},{8,9},{9,8},{10,11... | collective-permute-start | bytes 331784 | tf_op jit(solution)/shard_map/ppermute | solution.py:366
  64.1 12.3 %collective-permute-start.6 = (bf16[24,2048]{1,0:T(8,128)(2,1)S(1)}, bf16[24,2048]{1,0:T(8,128)(2,1)S(1)}, u32[]{:S(2)}, u32[]{:S(2)}) collective-permute-start(bf16[24,2048]{1,0:T(8,128)(2,1)S(1)} %shard_map.97), channel_id=1, source_target_pairs={{0,0},{1,8},{2,16},{3,24},{4,32},{5,40},{6,48},{7,56},{8,1},{9,9},... | collective-permute-start | bytes 294920 | tf_op jit(solution)/shard_map/ppermute | solution.py:373
  71.2 6.1 %collective-permute-start.12 = (f32[8,256]{1,0:T(8,128)S(1)}, f32[8,256]{1,0:T(8,128)S(1)}, u32[]{:S(2)}, u32[]{:S(2)}) collective-permute-start(f32[8,256]{1,0:T(8,128)S(1)} %shard_map.100.inner0_ref), channel_id=1, source_target_pairs={{0,192},{64,128},{128,64},{192,0},{1,193},{65,129},{129,65},{193,1... | collective-permute-start | bytes 24584 | tf_op jit(solution)/shard_map/ppermute | solution.py:366
  73.2 5.0 %collective-permute-start.11 = (f32[8,256]{1,0:T(8,128)S(1)}, f32[8,256]{1,0:T(8,128)S(1)}, u32[]{:S(2)}, u32[]{:S(2)}) collective-permute-start(f32[8,256]{1,0:T(8,128)S(1)} %shard_map.100.inner0_ref), channel_id=1, source_target_pairs={{0,128},{64,192},{128,0},{192,64},{1,129},{65,193},{129,1},{193,65... | collective-permute-start | bytes 24584 | tf_op jit(solution)/shard_map/ppermute | solution.py:366
  76.4 3.7 %collective-permute-start.10 = (f32[8,256]{1,0:T(8,128)S(1)}, f32[8,256]{1,0:T(8,128)S(1)}, u32[]{:S(2)}, u32[]{:S(2)}) collective-permute-start(f32[8,256]{1,0:T(8,128)S(1)} %shard_map.100.inner0_ref), channel_id=1, source_target_pairs={{0,64},{64,0},{128,192},{192,128},{1,65},{65,1},{129,193},{193,129... | collective-permute-start | bytes 24584 | tf_op jit(solution)/shard_map/ppermute | solution.py:366
